TPU v7x, 32 devices: a whole 2x2x4 slice. The times are simulated.
32 devices in a mesh: dp: 4 (over x, core), tensor: 8 (over z, y).
Axes of the slice: x: 2, y: 2, z: 4, core: 2. Of those that a mesh axis runs over, the one named last changes fastest.
Arguments:
- words: bfloat16 [12, 768, 4096], P('dp', 'tensor'), may hold values from -6 to 6
- w_in: bfloat16 [3072, 768], P('tensor'), may hold values from -0.21875 to 0.21875
- b_in: float32 [3072], P('tensor'), may hold values from -3 to 3
- w_out: bfloat16 [3072, 768], P('tensor'), may hold values from -0.109375 to 0.109375
- b_out: float32 [768], P('tensor'), may hold values from -3 to 3
- gain_one: float32 [768], P('tensor'), may hold values from 0.5 to 1.5
- shift_one: float32 [768], P('tensor'), may hold values from -2 to 2
- gain_two: float32 [768], P('tensor'), may hold values from 0.5 to 1.5
- shift_two: float32 [768], P('tensor'), may hold values from -2 to 2
- cotangent: bfloat16 [12, 768, 4096], P('dp', 'tensor'), may hold values from -6 to 6
- valid: int32 [12], P('dp'), may hold values 0 or 1
Outputs:
- activations: bfloat16 [12, 768, 4096], P('dp', 'tensor')
- grad_words: float32 [12, 768, 4096], P('dp', 'tensor')
- grad_w_in: float32 [3072, 768], P('tensor')
- grad_b_in: float32 [3072], P('tensor')
- grad_w_out: float32 [3072, 768], P('tensor')
- grad_b_out: float32 [768], P('tensor')
- grad_gain_one: float32 [768], P('tensor')
- grad_shift_one: float32 [768], P('tensor')
- grad_gain_two: float32 [768], P('tensor')
- grad_shift_two: float32 [768], P('tensor')
Inputs may be any that keep to these rules, and one draw needn't show every extreme that they name: `valid`: 1 marks a real sequence, 0 a padding sequence whose output gradient is ignored.
All inputs are finite; a program needn't handle non-finite values. No bound on the sum of `valid` on one device may be relied on, other than what follows from the above.
Results may differ from a plain program's by a relative error of at most 0.018.
Values may be sent and summed in bfloat16 or wider, within the bound.
A program may use at most 128 MiB of HBM per device.

v0:
```python
import math

import jax
import jax.numpy as jnp
from jax import lax
from jax.sharding import PartitionSpec as P

ROOT = 64


EPSILON = 1e-12


def angles(left_ids, right_ids, period):
    product_index = left_ids[:, None] * right_ids[None, :] % period
    return product_index.astype(jnp.float32) * (2.0 * math.pi / period)


def gelu_tanh(values):
    return jax.nn.gelu(values, approximate=True)


def contract(left_arr, right_arr, left_dim, right_dim):
    return lax.dot_general(
        left_arr,
        right_arr,
        (((left_dim,), (right_dim,)), ((), ())),
        preferred_element_type=jnp.float32,
    )


def pair_sums(first, second):
    return (
        lax.psum(first.astype(jnp.bfloat16), "tensor").astype(jnp.float32),
        lax.psum(second.astype(jnp.bfloat16), "tensor").astype(jnp.float32),
    )


def whole_rows(values):
    return lax.all_gather(values, "tensor", axis=0, tiled=True)


def unit_total(values):
    return lax.psum_scatter(
        values.astype(jnp.bfloat16), "tensor", scatter_dimension=0, tiled=True
    ).astype(jnp.float32)


def shared_norm(values, model_width):
    totals, squares = pair_sums(jnp.sum(values, axis=0), jnp.sum(values * values, axis=0))
    center = totals / model_width
    spread = squares / model_width - center * center
    inverse = lax.rsqrt(spread + EPSILON)
    return ((values - center[None, :]) * inverse[None, :], inverse)


def shared_norm_back(grad_hat, scaled, inverse, model_width):
    grad_mean, cross_mean = pair_sums(jnp.sum(grad_hat, axis=0), jnp.sum(grad_hat * scaled, axis=0))
    return inverse[None, :] * (
        grad_hat - grad_mean[None, :] / model_width - scaled * (cross_mean[None, :] / model_width)
    )


def on_device(
    words, w_in, b_in, w_out, b_out, gain_one, shift_one, gain_two, shift_two, cotangent, valid
):
    columns = words.shape[1]
    length = words.shape[2]
    model_width = w_in.shape[1]
    tensor_size = lax.axis_size("tensor")
    member = lax.axis_index("tensor")
    mix_scale = 1.0 / math.sqrt(length * model_width)
    all_ids = jnp.arange(model_width, dtype=jnp.int32)
    root_ids = jnp.arange(ROOT, dtype=jnp.int32)
    root_angle = angles(root_ids, root_ids, ROOT)
    cosine = jnp.cos(root_angle).astype(jnp.bfloat16)
    sine_table = jnp.sin(root_angle).astype(jnp.bfloat16)
    table_a = jnp.stack(
        [jnp.stack([cosine, sine_table], axis=-1), jnp.stack([-sine_table, cosine], axis=-1)],
        axis=1,
    )
    table_b = jnp.stack([cosine, sine_table], axis=-1)
    turn_angle = angles(root_ids, root_ids, length)
    turn_cos = jnp.cos(turn_angle)
    turn_sin = jnp.sin(turn_angle)

    def section_forward(spectrum):
        width_now = spectrum.shape[1]
        parts = spectrum.reshape(2, width_now, ROOT, ROOT)
        section_one = jnp.einsum(
            "kpnq,qcnm->pckm", table_a, parts, preferred_element_type=jnp.float32
        )
        real_turn = section_one[0] * turn_cos + section_one[1] * turn_sin
        imag_turn = section_one[1] * turn_cos - section_one[0] * turn_sin
        turned = jnp.stack([real_turn, imag_turn], axis=0).astype(jnp.bfloat16)
        mixed = jnp.einsum("anq,qckn->cak", table_b, turned, preferred_element_type=jnp.float32)
        return mixed.reshape(width_now, length)

    def section_backward(grad_mixed):
        width_now = grad_mixed.shape[0]
        grad_cube = grad_mixed.reshape(width_now, ROOT, ROOT)
        grad_turned = jnp.einsum(
            "anq,cak->qckn", table_b, grad_cube, preferred_element_type=jnp.float32
        )
        grad_real = grad_turned[0] * turn_cos - grad_turned[1] * turn_sin
        grad_imag = grad_turned[0] * turn_sin + grad_turned[1] * turn_cos
        grad_section = jnp.stack([grad_real, grad_imag], axis=0).astype(jnp.bfloat16)
        grad_spectrum = jnp.einsum(
            "kpnq,pckm->qcnm", table_a, grad_section, preferred_element_type=jnp.float32
        )
        return grad_spectrum.reshape(2 * width_now, length).astype(jnp.bfloat16)

    def hidden_step(totals, inputs_now):
        tokens, grad_out, keep_flag = inputs_now
        partial_terms = contract(hidden_table, tokens, 0, 0).reshape(
            tensor_size, 2 * columns, length
        )
        spectrum = lax.psum_scatter(
            partial_terms, "tensor", scatter_dimension=0, tiled=True
        ).reshape(2 * columns, length)
        spectrum = spectrum.astype(jnp.bfloat16).reshape(2, columns, length)
        mixed_rows = section_forward(spectrum)
        first_sum = tokens.astype(jnp.float32) + mixed_rows * mix_scale
        scaled_one, inverse_one = shared_norm(first_sum, model_width)
        normed = scaled_one * gain_one[:, None] + shift_one[:, None]
        gathered = whole_rows(normed.astype(jnp.bfloat16))
        inner_sum = contract(w_in, gathered, 1, 0) + b_in[:, None]
        active, gelu_back = jax.vjp(gelu_tanh, inner_sum)
        active_low = active.astype(jnp.bfloat16)
        outer_sum = unit_total(contract(w_out, active_low, 0, 0)) + b_out[:, None]
        scaled_two, inverse_two = shared_norm(normed + outer_sum, model_width)
        result = (scaled_two * gain_two[:, None] + shift_two[:, None]).astype(jnp.bfloat16)
        grad_result = grad_out.astype(jnp.float32) * keep_flag.astype(jnp.float32)
        grad_second = shared_norm_back(
            grad_result * gain_two[:, None], scaled_two, inverse_two, model_width
        )
        gathered_grad = whole_rows(grad_second.astype(jnp.bfloat16))
        grad_w_out = contract(active_low, gathered_grad, 1, 1)
        grad_active = contract(w_out, gathered_grad, 1, 0)
        (grad_inner,) = gelu_back(grad_active)
        inner_low = grad_inner.astype(jnp.bfloat16)
        grad_w_in = contract(inner_low, gathered, 1, 1)
        grad_normed = grad_second + unit_total(contract(w_in, inner_low, 0, 0))
        grad_first = shared_norm_back(
            grad_normed * gain_one[:, None], scaled_one, inverse_one, model_width
        )
        grad_mixed = (grad_first * mix_scale).astype(jnp.bfloat16)
        grad_spectrum = section_backward(grad_mixed)
        gathered_spec = whole_rows(grad_spectrum)
        grad_mix_words = contract(hidden_table, gathered_spec, 1, 0)
        grad_tokens = grad_first + grad_mix_words
        updates = (
            grad_w_in,
            jnp.sum(grad_inner, axis=1),
            grad_w_out,
            jnp.sum(grad_second, axis=1),
            jnp.sum(grad_normed * scaled_one, axis=1),
            jnp.sum(grad_normed, axis=1),
            jnp.sum(grad_result * scaled_two, axis=1),
            jnp.sum(grad_result, axis=1),
        )
        totals = tuple((total + update for total, update in zip(totals, updates)))
        return (totals, (result, grad_tokens))

    own_ids = member * columns + jnp.arange(columns, dtype=jnp.int32)
    own_angle = angles(own_ids, all_ids, model_width)
    cos_part = jnp.cos(own_angle).reshape(columns, tensor_size, 1, columns)
    sin_part = (-jnp.sin(own_angle)).reshape(columns, tensor_size, 1, columns)
    hidden_table = (
        jnp.concatenate([cos_part, sin_part], axis=2)
        .reshape(columns, tensor_size * 2 * columns)
        .astype(jnp.bfloat16)
    )
    empty_sums = (
        jnp.zeros(w_in.shape, jnp.float32),
        jnp.zeros(b_in.shape, jnp.float32),
        jnp.zeros(w_out.shape, jnp.float32),
        jnp.zeros(b_out.shape, jnp.float32),
        jnp.zeros(gain_one.shape, jnp.float32),
        jnp.zeros(shift_one.shape, jnp.float32),
        jnp.zeros(gain_two.shape, jnp.float32),
        jnp.zeros(shift_two.shape, jnp.float32),
    )
    totals, (activations, grad_words) = lax.scan(hidden_step, empty_sums, (words, cotangent, valid))
    summed = (
        lax.psum(totals[0].astype(jnp.bfloat16), "dp").astype(jnp.float32),
        lax.psum(totals[1].astype(jnp.bfloat16), "dp").astype(jnp.float32),
        lax.psum(totals[2].astype(jnp.bfloat16), "dp").astype(jnp.float32),
        lax.psum(totals[3].astype(jnp.bfloat16), "dp").astype(jnp.float32),
        lax.psum(totals[4].astype(jnp.bfloat16), "dp").astype(jnp.float32),
        lax.psum(totals[5].astype(jnp.bfloat16), "dp").astype(jnp.float32),
        lax.psum(totals[6].astype(jnp.bfloat16), "dp").astype(jnp.float32),
        lax.psum(totals[7].astype(jnp.bfloat16), "dp").astype(jnp.float32),
    )
    return (
        activations,
        grad_words,
        summed[0],
        summed[1],
        summed[2],
        summed[3],
        summed[4],
        summed[5],
        summed[6],
        summed[7],
    )


def solution(mesh):
    placed = (
        P("dp", "tensor", None),
        P("tensor", None),
        P("tensor"),
        P("tensor", None),
        P("tensor"),
        P("tensor"),
        P("tensor"),
        P("tensor"),
        P("tensor"),
        P("dp", "tensor", None),
        P("dp"),
    )
    return jax.shard_map(
        on_device,
        mesh=mesh,
        in_specs=placed,
        out_specs=(
            P("dp", "tensor", None),
            P("dp", "tensor", None),
            P("tensor", None),
            P("tensor"),
            P("tensor", None),
            P("tensor"),
            P("tensor"),
            P("tensor"),
            P("tensor"),
            P("tensor"),
        ),
        check_vma=False,
    )
```

profile of v0, /device:TPU:0, one launch (start us, length us, event | category | flops | bytes accessed | tf_op | source)
XLA Modules:
  0.0 4394.9 jit_solution(7836175531782485485)
XLA Ops:
  11.9 4331.6 %while.32 = (s32[]{:T(128)}, f32[384,768]{1,0:T(8,128)}, f32[384]{0:T(512)}, f32[384,768]{1,0:T(8,128)}, f32[96]{0:T(128)}, /*index=5*/f32[96]{0:T(128)}, f32[96...) while((s32[]{:T(128)}, f32[384,768]{1,0:T(8,128)}, ...), condition=%wide.region_26.27_spmd.clone.clone, body=%wide.region_0.26_spmd.clone.clone.sunk | while | flops 17632010240 | bytes 598244800 | solution.py:184
  52.4 545.7 %reduce-scatter.12.cloned.1.call-done = f32[1,192,4096]{1,2,0:T(8,128)} async-done(((f32[8,192,4096]{1,2,0:T(8,128)}), f32[1,192,4096]{1,2,0:T(8,128)}) %reduce-scatter.12.cloned.1.call-update) | async-done | bytes 3145744 | tf_op jit(solution)/shard_map/while/body/eval_jaxpr/reduce_scatter | solution.py:118
  615.5 35.4 all-reduce.10
  653.1 96.1 %all-gather.4.cloned.1.call-done = bf16[768,4096]{1,0:T(8,128)(2,1)} async-done(((bf16[96,4096]{1,0:T(8,128)(2,1)}), bf16[768,4096]{1,0:T(8,128)(2,1)}) %all-gather.4.cloned.1.call-update) | async-done | bytes 6291472 | tf_op jit(solution)/shard_map/while/body/eval_jaxpr/all_gather | solution.py:40
  775.5 114.3 %reduce-scatter.14.cloned.1.call-done = bf16[96,4096]{1,0:T(8,128)(2,1)} async-done(((bf16[768,4096]{1,0:T(8,128)(2,1)}), bf16[96,4096]{1,0:T(8,128)(2,1)}) %reduce-scatter.14.cloned.1.call-update) | async-done | bytes 786448 | tf_op jit(solution)/shard_map/while/body/eval_jaxpr/reduce_scatter | solution.py:44
  967.1 96.0 %all-gather.6.cloned.1.call-done = bf16[768,4096]{1,0:T(8,128)(2,1)} async-done(((bf16[96,4096]{1,0:T(8,128)(2,1)}), bf16[768,4096]{1,0:T(8,128)(2,1)}) %all-gather.6.cloned.1.call-update) | async-done | bytes 6291472 | tf_op jit(solution)/shard_map/while/body/eval_jaxpr/all_gather | solution.py:40
  1090.7 116.3 %reduce-scatter.16.cloned.1.call-done = bf16[96,4096]{1,0:T(8,128)(2,1)} async-done(((bf16[768,4096]{1,0:T(8,128)(2,1)}), bf16[96,4096]{1,0:T(8,128)(2,1)}) %reduce-scatter.16.cloned.1.call-update) | async-done | bytes 786448 | tf_op jit(solution)/shard_map/while/body/eval_jaxpr/reduce_scatter | solution.py:44
  1211.6 36.5 all-reduce.13
  1294.5 155.6 %all-gather.8.cloned.1.call-done = bf16[1536,4096]{1,0:T(8,128)(2,1)} async-done(((bf16[192,4096]{1,0:T(8,128)(2,1)}), bf16[1536,4096]{1,0:T(8,128)(2,1)}) %all-gather.8.cloned.1.call-update) | async-done | bytes 12582928 | tf_op jit(solution)/shard_map/while/body/eval_jaxpr/all_gather | solution.py:40
  1498.9 541.4 %reduce-scatter.12.cloned.1.call-done = f32[1,192,4096]{1,2,0:T(8,128)} async-done(((f32[8,192,4096]{1,2,0:T(8,128)}), f32[1,192,4096]{1,2,0:T(8,128)}) %reduce-scatter.12.cloned.1.call-update) | async-done | bytes 3145744 | tf_op jit(solution)/shard_map/while/body/eval_jaxpr/reduce_scatter | solution.py:118
  2095.2 96.1 %all-gather.4.cloned.1.call-done = bf16[768,4096]{1,0:T(8,128)(2,1)} async-done(((bf16[96,4096]{1,0:T(8,128)(2,1)}), bf16[768,4096]{1,0:T(8,128)(2,1)}) %all-gather.4.cloned.1.call-update) | async-done | bytes 6291472 | tf_op jit(solution)/shard_map/while/body/eval_jaxpr/all_gather | solution.py:40
  2217.6 114.4 %reduce-scatter.14.cloned.1.call-done = bf16[96,4096]{1,0:T(8,128)(2,1)} async-done(((bf16[768,4096]{1,0:T(8,128)(2,1)}), bf16[96,4096]{1,0:T(8,128)(2,1)}) %reduce-scatter.14.cloned.1.call-update) | async-done | bytes 786448 | tf_op jit(solution)/shard_map/while/body/eval_jaxpr/reduce_scatter | solution.py:44
  2409.4 95.8 %all-gather.6.cloned.1.call-done = bf16[768,4096]{1,0:T(8,128)(2,1)} async-done(((bf16[96,4096]{1,0:T(8,128)(2,1)}), bf16[768,4096]{1,0:T(8,128)(2,1)}) %all-gather.6.cloned.1.call-update) | async-done | bytes 6291472 | tf_op jit(solution)/shard_map/while/body/eval_jaxpr/all_gather | solution.py:40
  2532.8 116.2 %reduce-scatter.16.cloned.1.call-done = bf16[96,4096]{1,0:T(8,128)(2,1)} async-done(((bf16[768,4096]{1,0:T(8,128)(2,1)}), bf16[96,4096]{1,0:T(8,128)(2,1)}) %reduce-scatter.16.cloned.1.call-update) | async-done | bytes 786448 | tf_op jit(solution)/shard_map/while/body/eval_jaxpr/reduce_scatter | solution.py:44
  2653.7 36.2 all-reduce.13
  2737.6 154.3 %all-gather.8.cloned.1.call-done = bf16[1536,4096]{1,0:T(8,128)(2,1)} async-done(((bf16[192,4096]{1,0:T(8,128)(2,1)}), bf16[1536,4096]{1,0:T(8,128)(2,1)}) %all-gather.8.cloned.1.call-update) | async-done | bytes 12582928 | tf_op jit(solution)/shard_map/while/body/eval_jaxpr/all_gather | solution.py:40
  2940.7 541.1 %reduce-scatter.12.cloned.1.call-done = f32[1,192,4096]{1,2,0:T(8,128)} async-done(((f32[8,192,4096]{1,2,0:T(8,128)}), f32[1,192,4096]{1,2,0:T(8,128)}) %reduce-scatter.12.cloned.1.call-update) | async-done | bytes 3145744 | tf_op jit(solution)/shard_map/while/body/eval_jaxpr/reduce_scatter | solution.py:118
  3499.3 35.3 all-reduce.10
  3537.0 95.9 %all-gather.4.cloned.1.call-done = bf16[768,4096]{1,0:T(8,128)(2,1)} async-done(((bf16[96,4096]{1,0:T(8,128)(2,1)}), bf16[768,4096]{1,0:T(8,128)(2,1)}) %all-gather.4.cloned.1.call-update) | async-done | bytes 6291472 | tf_op jit(solution)/shard_map/while/body/eval_jaxpr/all_gather | solution.py:40
  3659.2 114.3 %reduce-scatter.14.cloned.1.call-done = bf16[96,4096]{1,0:T(8,128)(2,1)} async-done(((bf16[768,4096]{1,0:T(8,128)(2,1)}), bf16[96,4096]{1,0:T(8,128)(2,1)}) %reduce-scatter.14.cloned.1.call-update) | async-done | bytes 786448 | tf_op jit(solution)/shard_map/while/body/eval_jaxpr/reduce_scatter | solution.py:44
  3850.7 96.2 %all-gather.6.cloned.1.call-done = bf16[768,4096]{1,0:T(8,128)(2,1)} async-done(((bf16[96,4096]{1,0:T(8,128)(2,1)}), bf16[768,4096]{1,0:T(8,128)(2,1)}) %all-gather.6.cloned.1.call-update) | async-done | bytes 6291472 | tf_op jit(solution)/shard_map/while/body/eval_jaxpr/all_gather | solution.py:40
  3974.4 116.3 %reduce-scatter.16.cloned.1.call-done = bf16[96,4096]{1,0:T(8,128)(2,1)} async-done(((bf16[768,4096]{1,0:T(8,128)(2,1)}), bf16[96,4096]{1,0:T(8,128)(2,1)}) %reduce-scatter.16.cloned.1.call-update) | async-done | bytes 786448 | tf_op jit(solution)/shard_map/while/body/eval_jaxpr/reduce_scatter | solution.py:44
  4095.3 36.2 all-reduce.13
  4179.3 154.3 %all-gather.8.cloned.1.call-done = bf16[1536,4096]{1,0:T(8,128)(2,1)} async-done(((bf16[192,4096]{1,0:T(8,128)(2,1)}), bf16[1536,4096]{1,0:T(8,128)(2,1)}) %all-gather.8.cloned.1.call-update) | async-done | bytes 12582928 | tf_op jit(solution)/shard_map/while/body/eval_jaxpr/all_gather | solution.py:40
  (455 shorter events, 832.5 us)
Async XLA Ops:
  12.2 597.0 %copy-start.3 = (bf16[64,64,2]{0,1,2:T(8,128)(2,1)}, bf16[64,64,2]{0,1,2:T(8,128)(2,1)S(1)}, u32[]{:S(2)}) copy-start(bf16[64,64,2]{0,1,2:T(8,128)(2,1)S(1)} %get-tuple-element.1098) | copy-start | bytes 49156 | tf_op jit(solution)/shard_map/while
  12.2 585.9 %reduce-scatter.12.cloned.1.call-start = ((), (), s32[]{:S(2)}) async-start(), calls=%async_computation.4 | async-start | bytes 37748736 | tf_op jit(solution)/shard_map/while/body/eval_jaxpr/reduce_scatter | solution.py:118
  52.0 697.2 %all-gather.4.cloned.1.call-start = ((), (), s32[]{:S(2)}) async-start(), calls=%async_computation.5 | async-start | bytes 7077888 | tf_op jit(solution)/shard_map/while/body/eval_jaxpr/all_gather | solution.py:40
  52.4 555.0 %copy-start.1 = (f32[64,64]{0,1:T(8,128)}, f32[64,64]{0,1:T(8,128)S(1)}, u32[]{:S(2)}) copy-start(f32[64,64]{0,1:T(8,128)S(1)} %fusion.167) | copy-start | bytes 49156 | tf_op jit(solution)/shard_map/while
  652.8 237.1 %reduce-scatter.14.cloned.1.call-start = ((), (), s32[]{:S(2)}) async-start(), calls=%async_computation.6 | async-start | bytes 7077888 | tf_op jit(solution)/shard_map/while/body/eval_jaxpr/reduce_scatter | solution.py:44
  773.6 289.6 %all-gather.6.cloned.1.call-start = ((), (), s32[]{:S(2)}) async-start(), calls=%async_computation.7 | async-start | bytes 7077888 | tf_op jit(solution)/shard_map/while/body/eval_jaxpr/all_gather | solution.py:40
  966.8 240.2 %reduce-scatter.16.cloned.1.call-start = ((), (), s32[]{:S(2)}) async-start(), calls=%async_computation.8 | async-start | bytes 7077888 | tf_op jit(solution)/shard_map/while/body/eval_jaxpr/reduce_scatter | solution.py:44
  1090.6 359.5 %all-gather.8.cloned.1.call-start = ((), (), s32[]{:S(2)}) async-start(), calls=%async_computation.9 | async-start | bytes 14155776 | tf_op jit(solution)/shard_map/while/body/eval_jaxpr/all_gather | solution.py:40
  1458.7 592.7 %copy-start.3 = (bf16[64,64,2]{0,1,2:T(8,128)(2,1)}, bf16[64,64,2]{0,1,2:T(8,128)(2,1)S(1)}, u32[]{:S(2)}) copy-start(bf16[64,64,2]{0,1,2:T(8,128)(2,1)S(1)} %get-tuple-element.1098) | copy-start | bytes 49156 | tf_op jit(solution)/shard_map/while
  1458.7 581.6 %reduce-scatter.12.cloned.1.call-start = ((), (), s32[]{:S(2)}) async-start(), calls=%async_computation.4 | async-start | bytes 37748736 | tf_op jit(solution)/shard_map/while/body/eval_jaxpr/reduce_scatter | solution.py:118
  1498.5 692.7 %all-gather.4.cloned.1.call-start = ((), (), s32[]{:S(2)}) async-start(), calls=%async_computation.5 | async-start | bytes 7077888 | tf_op jit(solution)/shard_map/while/body/eval_jaxpr/all_gather | solution.py:40
  1498.9 550.7 %copy-start.1 = (f32[64,64]{0,1:T(8,128)}, f32[64,64]{0,1:T(8,128)S(1)}, u32[]{:S(2)}) copy-start(f32[64,64]{0,1:T(8,128)S(1)} %fusion.167) | copy-start | bytes 49156 | tf_op jit(solution)/shard_map/while
  2094.9 237.1 %reduce-scatter.14.cloned.1.call-start = ((), (), s32[]{:S(2)}) async-start(), calls=%async_computation.6 | async-start | bytes 7077888 | tf_op jit(solution)/shard_map/while/body/eval_jaxpr/reduce_scatter | solution.py:44
  2215.7 289.6 %all-gather.6.cloned.1.call-start = ((), (), s32[]{:S(2)}) async-start(), calls=%async_computation.7 | async-start | bytes 7077888 | tf_op jit(solution)/shard_map/while/body/eval_jaxpr/all_gather | solution.py:40
  2408.9 240.1 %reduce-scatter.16.cloned.1.call-start = ((), (), s32[]{:S(2)}) async-start(), calls=%async_computation.8 | async-start | bytes 7077888 | tf_op jit(solution)/shard_map/while/body/eval_jaxpr/reduce_scatter | solution.py:44
  2532.7 359.2 %all-gather.8.cloned.1.call-start = ((), (), s32[]{:S(2)}) async-start(), calls=%async_computation.9 | async-start | bytes 14155776 | tf_op jit(solution)/shard_map/while/body/eval_jaxpr/all_gather | solution.py:40
  2900.4 592.4 %copy-start.3 = (bf16[64,64,2]{0,1,2:T(8,128)(2,1)}, bf16[64,64,2]{0,1,2:T(8,128)(2,1)S(1)}, u32[]{:S(2)}) copy-start(bf16[64,64,2]{0,1,2:T(8,128)(2,1)S(1)} %get-tuple-element.1098) | copy-start | bytes 49156 | tf_op jit(solution)/shard_map/while
  2900.4 581.3 %reduce-scatter.12.cloned.1.call-start = ((), (), s32[]{:S(2)}) async-start(), calls=%async_computation.4 | async-start | bytes 37748736 | tf_op jit(solution)/shard_map/while/body/eval_jaxpr/reduce_scatter | solution.py:118
  2940.3 692.6 %all-gather.4.cloned.1.call-start = ((), (), s32[]{:S(2)}) async-start(), calls=%async_computation.5 | async-start | bytes 7077888 | tf_op jit(solution)/shard_map/while/body/eval_jaxpr/all_gather | solution.py:40
  3536.5 237.1 %reduce-scatter.14.cloned.1.call-start = ((), (), s32[]{:S(2)}) async-start(), calls=%async_computation.6 | async-start | bytes 7077888 | tf_op jit(solution)/shard_map/while/body/eval_jaxpr/reduce_scatter | solution.py:44
  3657.3 289.6 %all-gather.6.cloned.1.call-start = ((), (), s32[]{:S(2)}) async-start(), calls=%async_computation.7 | async-start | bytes 7077888 | tf_op jit(solution)/shard_map/while/body/eval_jaxpr/all_gather | solution.py:40
  3850.4 240.2 %reduce-scatter.16.cloned.1.call-start = ((), (), s32[]{:S(2)}) async-start(), calls=%async_computation.8 | async-start | bytes 7077888 | tf_op jit(solution)/shard_map/while/body/eval_jaxpr/reduce_scatter | solution.py:44
  3974.3 359.3 %all-gather.8.cloned.1.call-start = ((), (), s32[]{:S(2)}) async-start(), calls=%async_computation.9 | async-start | bytes 14155776 | tf_op jit(solution)/shard_map/while/body/eval_jaxpr/all_gather | solution.py:40
  4343.5 40.1 all-reduce.16.cloned.1.call-start
  (107 other events, 3828.4 us)
Sparse Core Ops, SparseCore 0:
  52.2 545.8 reduce-scatter.11
  652.9 96.2 all-gather.3
  773.7 116.1 reduce-scatter.13
  966.9 96.1 all-gather.5
  1090.8 116.1 reduce-scatter.15
  1276.5 173.6 all-gather.7
  1498.6 541.5 reduce-scatter.11
  2095.0 96.2 all-gather.3
  2215.8 116.1 reduce-scatter.13
  2409.0 96.1 all-gather.5
  2532.9 116.0 reduce-scatter.15
  2718.2 173.6 all-gather.7
  2940.4 541.2 reduce-scatter.11
  3536.6 96.2 all-gather.3
  3657.4 116.1 reduce-scatter.13
  3850.6 96.2 all-gather.5
  3974.5 116.1 reduce-scatter.15
  4159.9 173.6 all-gather.7
Sparse Core Ops, SparseCore 1:
  4348.1 35.5 all-reduce.15
where the time goes:
time: 4400 us; the launch traced here: 4390 us
  waiting for transfers between devices  3390 us (77%)
  blocking collectives  428 us (10%)
  local copies, waits for them, and re-layouts  232 us (5%)
  matrix products  227 us (5%)
  other arithmetic  96.8 us (2%)
    reduce_scatter x3, waiting for transfers between devices, hidden_step(): lax.psum_scatter(partial_terms, 'tensor', scatter_dimension=0, tiled=True)  1630 us
    all_gather x9, waiting for transfers between devices, whole_rows(): return lax.all_gather(values, 'tensor', axis=0, tiled=True)  1040 us
    reduce_scatter x6, waiting for transfers between devices, unit_total(): lax.psum_scatter(values.astype(jnp.bfloat16), 'tensor', scatter_dimension...  692 us
    psum x12, blocking collectives, pair_sums(): lax.psum(second.astype(jnp.bfloat16), 'tensor').astype(jnp.float32)  422 us
    dot_general x24, matrix products, contract(): lax.dot_general(left_arr, right_arr, (((left_dim,), (right_dim,)), ((), (...  194 us
  transfers between devices with their start and end apart: 19, of which 19 were waited for; matrix products, arithmetic and copies ran while one was open for 1% of the time, Pallas kernels for 0%

commit v1 on v0

v1 whole, which is shorter than its diff:
```python
import math

import jax
import jax.numpy as jnp
import numpy as np
from jax import lax
from jax.experimental import pallas as pl
from jax.experimental.pallas import tpu as pltpu
from jax.sharding import PartitionSpec as P

EPSILON = 1e-12
MESH = pl.DeviceIdType.MESH
BF = jnp.bfloat16
F32 = jnp.float32


def token_tables(length, group):
    half = length // (2 * group)
    n = np.arange(length, dtype=np.int64)

    def wave(k):
        angle = (n[:, None] * k[None, :] % length) * (2.0 * math.pi / length)
        return np.cos(angle), np.sin(angle)

    cos, sin = wave(np.arange(length // 2))
    main = np.stack(
        [cos.reshape(length, group, half), sin.reshape(length, group, half)], axis=2
    ).reshape(length, length)
    edge_cos, edge_sin = wave(half * (np.arange(group) + 1))
    edge = np.zeros((length, 128))
    edge[:, 0 : 2 * group : 2] = edge_cos
    edge[:, 1 : 2 * group : 2] = np.where(np.abs(edge_sin) < 1e-9, 0.0, edge_sin)
    return main.astype(BF), edge.astype(BF)


def hidden_tables(width):
    ids = np.arange(width, dtype=np.int64)
    angle = (ids[:, None] * ids[None, :] % width) * (2.0 * math.pi / width)
    return np.cos(angle).astype(BF), np.sin(angle).astype(BF)


class Place:
    def __init__(self, n_dp, n_tensor):
        self.n_dp, self.n_tensor = n_dp, n_tensor
        self.slices = n_tensor // 2
        self.group = 2 * n_dp
        self.dp = lax.axis_index("dp")
        self.tensor = lax.axis_index("tensor")
        self.z = self.tensor // 2
        self.y = self.tensor % 2
        self.g = self.dp * 2 + self.y
        self.block = self.block_of(self.dp, self.y)

    def block_of(self, dp, y):
        return ((dp % (self.n_dp // 2)) * 2 + dp // (self.n_dp // 2)) * 2 + y

    def dp_of(self, z):
        return (z % 2) * (self.n_dp // 2) + z // 2

    def peer(self, offset):
        g = self.g ^ offset
        return (g // 2, self.z * 2 + g % 2), g


def start_all(moves):
    for src, dst, send, recv, device, own in moves:
        if device is None:
            pltpu.make_async_copy(src, dst, recv).start()
        elif own is None:
            pltpu.make_async_remote_copy(src, dst, send, recv, device, MESH).start()
        else:
            @pl.when(own)
            def _():
                pltpu.make_async_copy(src, dst, recv).start()

            @pl.when(jnp.logical_not(own))
            def _():
                pltpu.make_async_remote_copy(src, dst, send, recv, device, MESH).start()


def wait_sent(moves):
    for src, dst, send, recv, device, own in moves:
        if device is None:
            continue
        if own is None:
            pltpu.make_async_copy(src, src, send).wait()
        else:
            @pl.when(jnp.logical_not(own))
            def _():
                pltpu.make_async_copy(src, src, send).wait()


def wait_arrived(arrivals):
    for ref, recv in arrivals:
        pltpu.make_async_copy(ref, ref, recv).wait()


def greet(sources, n_targets):
    barrier = pltpu.get_barrier_semaphore()
    count = 0
    for device, own in sources:
        if own is None:
            pl.semaphore_signal(barrier, inc=1, device_id=device, device_id_type=MESH)
        else:
            @pl.when(jnp.logical_not(own))
            def _():
                pl.semaphore_signal(barrier, inc=1, device_id=device, device_id_type=MESH)
    total = 0
    for own in n_targets:
        total = total + (1 if own is None else jnp.where(own, 0, 1))
    pl.semaphore_wait(barrier, total)


ANY = pl.BlockSpec(memory_space=pl.ANY)


def exchange(body, ins, outs, n_sems, collective_id):
    return pl.pallas_call(
        body,
        out_shape=outs,
        in_specs=[ANY] * len(ins),
        out_specs=[ANY] * len(outs),
        scratch_shapes=[pltpu.SemaphoreType.DMA((n_sems,)), pltpu.SemaphoreType.DMA((n_sems,))],
        compiler_params=pltpu.CompilerParams(collective_id=collective_id, has_side_effects=True),
    )(*ins)


def on_device(
    words, w_in, b_in, w_out, b_out, gain_one, shift_one, gain_two, shift_two, cotangent, valid
):
    seqs, columns, length = words.shape
    width = w_in.shape[1]
    n_dp, n_tensor = lax.axis_size("dp"), lax.axis_size("tensor")
    assert n_tensor == 2 * n_dp
    group = 2 * n_dp
    half = length // (2 * group)
    mix_scale = 1.0 / math.sqrt(length * width)
    table, edge_table = token_tables(length, group)
    hid_cos, hid_sin = hidden_tables(width)

    def to_slice_body(x_ref, o_ref, send, recv):
        at = Place(n_dp, n_tensor)
        moves, sources = [], []
        target_dp = at.dp_of(at.z)
        for j in range(seqs):
            z = (at.dp + j) % at.slices
            own = jnp.logical_and(target_dp == at.dp, z == at.z)
            moves.append((x_ref.at[j], o_ref.at[j], send.at[j], recv.at[j], (target_dp, z * 2 + at.y), own))
            sources.append((((at.z - j + at.n_dp) % at.n_dp, at.block), own))
        greet(sources, [m[5] for m in moves])
        start_all(moves)
        wait_sent(moves)
        wait_arrived([(m[1], m[3]) for m in moves])

    (x_col,) = exchange(
        to_slice_body, [words], [jax.ShapeDtypeStruct(words.shape, BF)], seqs, 1
    )

    spectrum = jnp.einsum("jcl,lk->jck", x_col, table, preferred_element_type=F32).astype(BF)
    edges = jnp.einsum("jcl,lk->jck", x_col, edge_table, preferred_element_type=F32).astype(BF)

    def to_tokens_body(x_ref, u_ref, e_ref, xo_ref, uo_ref, eo_ref, send, recv):
        at = Place(n_dp, n_tensor)
        rows = pl.ds(pl.multiple_of(at.block * columns, 16), columns)
        moves, sources = [], []
        k = 0
        for offset in range(group):
            device, g = at.peer(offset)
            if offset == 0:
                device = None
            else:
                sources.append((device, None))
            first = pl.ds(pl.multiple_of(g * half, 128), half)
            last = pl.ds(pl.multiple_of(length - (g + 1) * half, 128), half)
            mine = pl.ds(pl.multiple_of(g * 2 * half, 128), 2 * half)
            for j in range(seqs):
                for src, dst in (
                    (x_ref.at[j, :, first], xo_ref.at[j, rows, pl.ds(0, half)]),
                    (x_ref.at[j, :, last], xo_ref.at[j, rows, pl.ds(half, half)]),
                    (u_ref.at[j, :, mine], uo_ref.at[j, rows]),
                    (e_ref.at[j], eo_ref.at[j, rows]),
                ):
                    moves.append((src, dst, send.at[k], recv.at[k], device, None))
                    k += 1
        greet(sources, [None] * len(sources))
        start_all(moves)
        wait_sent(moves)
        wait_arrived([(m[1], m[3]) for m in moves])

    x_tok, u_tok, e_tok = exchange(
        to_tokens_body,
        [x_col, spectrum, edges],
        [
            jax.ShapeDtypeStruct((seqs, width, 2 * half), BF),
            jax.ShapeDtypeStruct((seqs, width, 2 * half), BF),
            jax.ShapeDtypeStruct((seqs, width, 128), BF),
        ],
        group * seqs * 4,
        2,
    )

    def cot_body(c_ref, o_ref, send, recv):
        at = Place(n_dp, n_tensor)
        rows = pl.ds(pl.multiple_of(at.tensor * columns, 16), columns)
        moves, sources, owns, arrivals = [], [], [], []
        k = 0
        for offset in range(group):
            g = at.g ^ offset
            first = pl.ds(pl.multiple_of(g * half, 128), half)
            last = pl.ds(pl.multiple_of(length - (g + 1) * half, 128), half)
            for j in range(seqs):
                z = (at.dp + j) % at.slices
                device = (g // 2, z * 2 + g % 2)
                own = (z == at.z) if offset == 0 else None
                key = (j * n_tensor + at.tensor) * 2
                moves.append((c_ref.at[j, :, first], o_ref.at[j, rows, pl.ds(0, half)], send.at[k], recv.at[key], device, own))
                moves.append((c_ref.at[j, :, last], o_ref.at[j, rows, pl.ds(half, half)], send.at[k + 1], recv.at[key + 1], device, own))
                k += 2
                owns.append(own)
        for j in range(seqs):
            src_dp = (at.z - j + at.n_dp) % at.n_dp
            for b in range(n_tensor):
                own = jnp.logical_and(src_dp == at.dp, at.tensor == b)
                sources.append(((src_dp, b), own))
                their = pl.ds(b * columns, columns)
                key = (j * n_tensor + b) * 2
                arrivals.append((o_ref.at[j, their, pl.ds(0, half)], recv.at[key]))
                arrivals.append((o_ref.at[j, their, pl.ds(half, half)], recv.at[key + 1]))
        greet(sources, owns)
        start_all(moves)
        wait_sent(moves)
        wait_arrived(arrivals)

    (cot_tok,) = exchange(
        cot_body, [cotangent], [jax.ShapeDtypeStruct((seqs, width, 2 * half), BF)], group * seqs * 2, 3
    )

    w_in_all = lax.all_gather(w_in, "tensor", axis=0, tiled=True)
    w_out_all = lax.all_gather(w_out, "tensor", axis=0, tiled=True)
    b_in_all = lax.all_gather(b_in, "tensor", axis=0, tiled=True)
    small = lax.all_gather(
        jnp.stack([b_out, gain_one, shift_one, gain_two, shift_two], 0), "tensor", axis=1, tiled=True
    )
    b_out_all, g1, s1, g2, s2 = [small[i][:, None] for i in range(5)]
    g = lax.axis_index("dp") * 2 + lax.axis_index("tensor") % 2
    z = lax.axis_index("tensor") // 2
    keep_all = lax.all_gather(valid.astype(F32), "dp", axis=0, tiled=False)

    lane = jnp.arange(half)
    turn = ((lane[:, None] + lane[None, :]) == half).astype(BF)
    edge_lane = jnp.arange(128)
    pick_u = ((edge_lane[:, None] == 2 * g) & (lane[None, :] == 0)).astype(BF)
    pick_v = ((edge_lane[:, None] == 2 * g + 1) & (lane[None, :] == 0)).astype(BF)

    def dot(a, b, da, db):
        return lax.dot_general(a, b, (((da,), (db,)), ((), ())), preferred_element_type=F32)

    def norm(v):
        center = jnp.mean(v, axis=0, keepdims=True)
        off = v - center
        inverse = lax.rsqrt(jnp.mean(off * off, axis=0, keepdims=True) + EPSILON)
        return off * inverse, inverse

    def norm_back(gh, h, inverse):
        return inverse * (
            gh - jnp.mean(gh, axis=0, keepdims=True) - h * jnp.mean(gh * h, axis=0, keepdims=True)
        )

    acts, gus, ges, gfs = [], [], [], []
    totals = None
    for j in range(seqs):
        u, v = u_tok[j, :, :half], u_tok[j, :, half:]
        u_turned = (dot(u, turn, 1, 0) + dot(e_tok[j], pick_u, 1, 0)).astype(BF)
        v_turned = (dot(v, turn, 1, 0) + dot(e_tok[j], pick_v, 1, 0)).astype(BF)
        mixed_a = dot(hid_cos, u, 1, 0) - dot(hid_sin, v, 1, 0)
        mixed_b = dot(hid_cos, u_turned, 1, 0) + dot(hid_sin, v_turned, 1, 0)
        mixed = jnp.concatenate([mixed_a, mixed_b], axis=1)
        first = x_tok[j].astype(F32) + mixed * mix_scale
        h1, inv1 = norm(first)
        normed = h1 * g1 + s1
        normed_low = normed.astype(BF)
        inner = dot(w_in_all, normed_low, 1, 0) + b_in_all[:, None]
        active, gelu_back = jax.vjp(lambda q: jax.nn.gelu(q, approximate=True), inner)
        active_low = active.astype(BF)
        outer = dot(w_out_all, active_low, 0, 0) + b_out_all
        h2, inv2 = norm(normed + outer)
        acts.append((h2 * g2 + s2).astype(BF))
        src_dp = (z - j + n_dp) % n_dp
        go = cot_tok[j].astype(F32) * keep_all[src_dp, j]
        g_second = norm_back(go * g2, h2, inv2)
        g_low = g_second.astype(BF)
        g_w_out = dot(active_low, g_low, 1, 1)
        (g_inner,) = gelu_back(dot(w_out_all, g_low, 1, 0))
        inner_low = g_inner.astype(BF)
        g_w_in = dot(inner_low, normed_low, 1, 1)
        g_normed = g_second + dot(w_in_all, inner_low, 0, 0)
        g_first = norm_back(g_normed * g1, h1, inv1)
        gm = (g_first * mix_scale).astype(BF)
        gm_a, gm_b = gm[:, :half], gm[:, half:]
        gm_t = dot(gm_b, turn, 1, 0)
        even = (gm_t + gm_a.astype(F32)).astype(BF)
        odd = (gm_t - gm_a.astype(F32)).astype(BF)
        gu = dot(hid_cos, even, 1, 0)
        gv = dot(hid_sin, odd, 1, 0)
        ge = dot(hid_cos, dot(gm_b, pick_u, 1, 1).astype(BF), 1, 0) + dot(
            hid_sin, dot(gm_b, pick_v, 1, 1).astype(BF), 1, 0
        )
        gus.append(jnp.concatenate([gu, gv], axis=1).astype(BF))
        ges.append(ge.astype(BF))
        gfs.append(g_first.astype(BF))
        updates = (
            g_w_in,
            jnp.sum(g_inner, axis=1),
            g_w_out,
            jnp.sum(g_second, axis=1),
            jnp.sum(g_normed * h1, axis=1),
            jnp.sum(g_normed, axis=1),
            jnp.sum(go * h2, axis=1),
            jnp.sum(go, axis=1),
        )
        totals = updates if totals is None else tuple(a + b for a, b in zip(totals, updates))
    act_tok, gu_tok, ge_tok, gf_tok = [jnp.stack(q) for q in (acts, gus, ges, gfs)]

    def act_body(a_ref, o_ref, send, recv):
        at = Place(n_dp, n_tensor)
        first = pl.ds(pl.multiple_of(at.g * half, 128), half)
        last = pl.ds(pl.multiple_of(length - (at.g + 1) * half, 128), half)
        moves, sources, owns, arrivals = [], [], [], []
        k = 0
        for offset in range(n_tensor):
            b = at.tensor ^ offset
            rows = pl.ds(pl.multiple_of(b * columns, 16), columns)
            for j in range(seqs):
                dp = (at.z - j + at.n_dp) % at.n_dp
                own = (dp == at.dp) if offset == 0 else None
                key = (j * group + at.g) * 2
                moves.append((a_ref.at[j, rows, pl.ds(0, half)], o_ref.at[j, :, first], send.at[k], recv.at[key], (dp, b), own))
                moves.append((a_ref.at[j, rows, pl.ds(half, half)], o_ref.at[j, :, last], send.at[k + 1], recv.at[key + 1], (dp, b), own))
                k += 2
                owns.append(own)
        for j in range(seqs):
            src_z = (at.dp + j) % at.slices
            for g_ in range(group):
                own = jnp.logical_and(src_z == at.z, at.g == g_)
                sources.append(((g_ // 2, src_z * 2 + g_ % 2), own))
                their_first = pl.ds(g_ * half, half)
                their_last = pl.ds(length - (g_ + 1) * half, half)
                key = (j * group + g_) * 2
                arrivals.append((o_ref.at[j, :, their_first], recv.at[key]))
                arrivals.append((o_ref.at[j, :, their_last], recv.at[key + 1]))
        greet(sources, owns)
        start_all(moves)
        wait_sent(moves)
        wait_arrived(arrivals)

    (activations,) = exchange(
        act_body, [act_tok], [jax.ShapeDtypeStruct(words.shape, BF)], n_tensor * seqs * 2, 4
    )

    def to_columns_body(u_ref, e_ref, f_ref, uo_ref, eo_ref, fo_ref, send, recv):
        at = Place(n_dp, n_tensor)
        first = pl.ds(pl.multiple_of(at.g * half, 128), half)
        last = pl.ds(pl.multiple_of(length - (at.g + 1) * half, 128), half)
        mine = pl.ds(pl.multiple_of(at.g * 2 * half, 128), 2 * half)
        moves, sources = [], []
        k = 0
        for offset in range(group):
            device, g_ = at.peer(offset)
            rows = pl.ds(pl.multiple_of(at.block_of(g_ // 2, g_ % 2) * columns, 16), columns)
            if offset == 0:
                device = None
            else:
                sources.append((device, None))
            for j in range(seqs):
                for src, dst in (
                    (u_ref.at[j, rows], uo_ref.at[j, :, mine]),
                    (e_ref.at[j, rows], eo_ref.at[at.g, j]),
                    (f_ref.at[j, rows, pl.ds(0, half)], fo_ref.at[j, :, first]),
                    (f_ref.at[j, rows, pl.ds(half, half)], fo_ref.at[j, :, last]),
                ):
                    moves.append((src, dst, send.at[k], recv.at[k], device, None))
                    k += 1
        greet(sources, [None] * len(sources))
        start_all(moves)
        wait_sent(moves)
        wait_arrived([(m[1], m[3]) for m in moves])

    gu_col, ge_col, gf_col = exchange(
        to_columns_body,
        [gu_tok, ge_tok, gf_tok],
        [
            jax.ShapeDtypeStruct((seqs, columns, length), BF),
            jax.ShapeDtypeStruct((group, seqs, columns, 128), BF),
            jax.ShapeDtypeStruct((seqs, columns, length), BF),
        ],
        group * seqs * 4,
        5,
    )
    ge_sum = jnp.sum(ge_col.astype(F32), axis=0).astype(BF)
    gw_col = (
        gf_col.astype(F32)
        + jnp.einsum("jck,lk->jcl", gu_col, table, preferred_element_type=F32)
        + jnp.einsum("jck,lk->jcl", ge_sum, edge_table, preferred_element_type=F32)
    ).astype(BF)

    def home_body(x_ref, o_ref, send, recv):
        at = Place(n_dp, n_tensor)
        moves, sources = [], []
        target_dp = at.dp_of(at.z)
        for j in range(seqs):
            z_ = (at.dp + j) % at.slices
            own = jnp.logical_and(target_dp == at.dp, z_ == at.z)
            moves.append((x_ref.at[j], o_ref.at[j], send.at[j], recv.at[j], ((at.z - j + at.n_dp) % at.n_dp, at.block), own))
            sources.append(((target_dp, z_ * 2 + at.y), own))
        greet(sources, [m[5] for m in moves])
        start_all(moves)
        wait_sent(moves)
        wait_arrived([(m[1], m[3]) for m in moves])

    (gw,) = exchange(home_body, [gw_col], [jax.ShapeDtypeStruct(words.shape, BF)], seqs, 6)
    grad_words = gw.astype(F32)

    def reduce_weight(v):
        part = lax.psum_scatter(v.astype(BF), "tensor", scatter_dimension=0, tiled=True)
        return lax.psum(part, "dp").astype(F32)

    grad_w_in = reduce_weight(totals[0])
    grad_w_out = reduce_weight(totals[2])
    grad_b_in = lax.psum(lax.psum_scatter(totals[1], "tensor", scatter_dimension=0, tiled=True), "dp")
    rest = jnp.stack(totals[3:], 0)
    rest = lax.psum(lax.psum_scatter(rest, "tensor", scatter_dimension=1, tiled=True), "dp")
    return (
        activations,
        grad_words,
        grad_w_in,
        grad_b_in,
        grad_w_out,
        rest[0],
        rest[1],
        rest[2],
        rest[3],
        rest[4],
    )


def solution(mesh):
    spec = (
        P("dp", "tensor", None),
        P("tensor", None),
        P("tensor"),
        P("tensor", None),
        P("tensor"),
        P("tensor"),
        P("tensor"),
        P("tensor"),
        P("tensor"),
        P("dp", "tensor", None),
        P("dp"),
    )
    out = (
        P("dp", "tensor", None),
        P("dp", "tensor", None),
        P("tensor", None),
        P("tensor"),
        P("tensor", None),
        P("tensor"),
        P("tensor"),
        P("tensor"),
        P("tensor"),
        P("tensor"),
    )
    return jax.shard_map(on_device, mesh=mesh, in_specs=spec, out_specs=out, check_vma=False)
```

time: 4400 us -> 896 us (0.20)
  waiting for transfers between devices: 3390 us -> 19 us
  Pallas kernels: 0 us -> 453 us
  blocking collectives: 428 us -> 115 us
  local copies, waits for them, and re-layouts: 232 us -> 13.7 us
  other arithmetic: 96.8 us -> 40 us
    reduce_scatter x9 -> x2, waiting for transfers between devices: 2320 us -> 17.5 us  [reduce_weight(): lax.psum_scatter(v.astype(BF), 'tensor', scatter_dimension=0, tiled=True)]
    all_gather x9 -> x2, waiting for transfers between devices: 1040 us -> 0.02 us  [the longest x1 0.02 us: on_device(): w_in_all = lax.all_gather(w_in, 'tensor', axis=0, tiled=True)]
    pallas_call x0 -> x6, Pallas kernels: none -> 453 us  [exchange(): pl.pallas_call(body, out_shape=outs, in_specs=[ANY] * len(ins), out_specs...]
    psum x13 -> x1, blocking collectives: 428 us -> 6.43 us  [on_device(): lax.psum(lax.psum_scatter(totals[1], 'tensor', scatter_dimension=0, tiled...]
    reshape x3 -> x0, local copies, waits for them, and re-layouts: 85.6 us -> none  [hidden_step(): contract(hidden_table, tokens, 0, 0)]
    while x216 -> x0, local copies, waits for them, and re-layouts: 71.8 us -> none
    all_gather x0 -> x2, blocking collectives: none -> 57.5 us  [the longest x1 31 us: on_device(): lax.all_gather(jnp.stack([b_out, gain_one, shift_one, gain_two, shift_two...]
    convert_element_type x13 -> x0, local copies, waits for them, and re-layouts: 53.3 us -> none  [the longest x6 38.7 us: section_backward(): return grad_spectrum.reshape(2 * width_now, length).astype(jnp.bfloat16)]
  transfers between devices with their start and end apart: 19 -> 6, of which waited for: 19 -> 1; matrix products, arithmetic and copies ran while one was open for 1% -> 23% of each run, Pallas kernels for 0% -> 51%
where the time goes in v1:
time: 896 us; the launch traced here: 890 us
  Pallas kernels  453 us (51%)
  matrix products  232 us (26%)
  blocking collectives  115 us (13%)
  other arithmetic  40 us (4%)
  waiting for transfers between devices  19 us (2%)
  between operations  16.9 us (2%)
  local copies, waits for them, and re-layouts  13.7 us (2%)
    pallas_call x6, Pallas kernels, exchange(): pl.pallas_call(body, out_shape=outs, in_specs=[ANY] * len(ins), out_specs...  453 us
    dot_general x51, matrix products, dot(): lax.dot_general(a, b, (((da,), (db,)), ((), ())), preferred_element_type=...  189 us
    unnamed x2, blocking collectives  50.7 us
    all_gather x1, blocking collectives, on_device(): lax.all_gather(jnp.stack([b_out, gain_one, shift_one, gain_two, shift_two...  31 us
    all_gather x1, blocking collectives, on_device(): b_in_all = lax.all_gather(b_in, 'tensor', axis=0, tiled=True)  26.5 us
    dot_general x1, matrix products, on_device(): jnp.einsum('jck,lk->jcl', gu_col, table, preferred_element_type=F32)  19 us
  transfers between devices with their start and end apart: 6, of which 1 were waited for; matrix products, arithmetic and copies ran while one was open for 23% of the time, Pallas kernels for 51%

profile of v1, /device:TPU:0, one launch (start us, length us, event | category | flops | bytes accessed | tf_op | source)
XLA Modules:
  0.0 890.2 jit_solution(6327015713441677538)
XLA Ops:
  11.5 8.3 all-reduce
  20.6 26.5 %all-gather.2 = f32[8,1,384]{2,1,0:T(1,128)S(1)} all-gather(f32[1,1,384]{2,1,0:T(1,128)S(1)} %reshape.378), channel_id=1, replica_groups=mesh['dp'=4,'tensor'=8] {'tensor'}, dimensions={0}, use_global_device_ids=true | all-gather | bytes 13824 | tf_op jit(solution)/shard_map/all_gather | solution.py:240
  47.8 31.0 %all-gather.1 = f32[8,96,5]{1,2,0:T(8,128)S(1)} all-gather(f32[1,96,5]{1,2,0:T(8,128)S(1)} %bitcast.360), channel_id=1, replica_groups=mesh['dp'=4,'tensor'=8] {'tensor'}, dimensions={0}, use_global_device_ids=true | all-gather | bytes 17280 | tf_op jit(solution)/shard_map/all_gather | solution.py:241
  78.9 84.5 %shard_map.243 = bf16[3,768,512]{2,1,0:T(8,128)(2,1)} custom-call(bf16[3,96,4096]{2,1,0:T(8,128)(2,1)} %c_ref.1), custom_call_target="tpu_custom_call" | custom-call | tf_op jit(solution)/shard_map/pallas_call | solution.py:118
  163.4 70.2 %shard_map.240.x_ref = bf16[3,96,4096]{2,1,0:T(8,128)(2,1)} custom-call(bf16[3,96,4096]{2,1,0:T(8,128)(2,1)} %x_ref.1), custom_call_target="tpu_custom_call" | custom-call | tf_op jit(solution)/shard_map/pallas_call | solution.py:118
  236.9 16.9 %fusion.31.u_ref = bf16[3,96,4096]{2,1,0:T(8,128)(2,1)} fusion(bf16[4096,4096,1]{1,0,2:T(8,128)(2,1)} %constant.132, bf16[3,96,4096]{2,1,0:T(8,128)(2,1)S(1)} %copy-done.7), kind=kOutput, calls=%fused_computation.51 | convolution fusion | flops 9664856064 | bytes 38273024 | tf_op jit(solution)/shard_map/jcl,lk->jck/dot_general | solution.py:159
  253.7 82.8 %shard_map.241 = (bf16[3,768,512]{2,1,0:T(8,128)(2,1)}, bf16[3,768,512]{2,1,0:T(8,128)(2,1)}, bf16[3,768,128]{2,1,0:T(8,128)(2,1)}) custom-call(bf16[3,96,4096]{2,1,0:T(8,128)(2,1)} %shard_map.240.x_ref, bf16[3,96,4096]{2,1,0:T(8,128)(2,1)} %fusion.31.u_ref, bf16[3,96,128]{2,1,0:T(8,128)(2,1)} %fusion.94.e_ref), custom_call_target="tpu_custom_call" | custom-call | tf_op jit(solution)/shard_map/pallas_call | solution.py:118
  378.9 9.1 %fusion.293 = f32[512,3072]{1,0:T(8,128)} fusion(bf16[3072,768]{1,0:T(8,128)(2,1)} %all-gather.6.cloned.1.call-done, f32[768,512]{1,0:T(8,128)} %copy-done.10, f32[512]{0:T(512)S(1)} %add_rsqrt_fusion.3, f32[512]{0:T(512)S(1)} %broadcast_multiply_fusion.15, f32[768]{0:T(1024)S(1)} %get-tuple-element.53, f32[768]{0:T(1024)S(1)} %get-tuple-element.54), kind=kOutput, calls=%fused_computation.390 | convolution fusion | flops 2417885184 | bytes 12593152 | tf_op jit(solution)/shard_map/dot_general | solution.py:256
  388.0 8.3 fusion.314
  409.2 6.9 fusion.313
  424.2 10.9 %fusion.133 = f32[3072,768]{1,0:T(8,128)} fusion(f32[768,512]{1,0:T(8,128)S(1)} %get-tuple-element.60, f32[512,3072]{1,0:T(8,128)} %fusion.293, f32[3072]{0:T(1024)S(1)} %bitcast.353), kind=kOutput, calls=%fused_computation.239 | convolution fusion | flops 2432040960 | bytes 17313792 | tf_op jit(solution)/shard_map/dot_general | solution.py:256
  439.0 6.8 fusion.136
  445.8 10.4 %add_convert_fusion = bf16[3072,768]{1,0:T(8,128)(2,1)} fusion(f32[3072,768]{1,0:T(8,128)} %fusion.136, f32[3072,768]{1,0:T(8,128)} %fusion.133, f32[768,512]{1,0:T(8,128)S(1)} %get-tuple-element.78, f32[512,3072]{1,0:T(8,128)S(1)} %fusion.290, f32[3072]{0:T(1024)S(1)} %bitcast.355), kind=kOutput, calls=%fused_computation | convolution fusion | flops 2439118848 | bytes 31469568 | tf_op jit(solution)/shard_map/dot_general | solution.py:256
  458.9 10.4 %fusion.318 = (f32[3072]{0:T(1024)}, bf16[3072,512]{0,1:T(8,128)(2,1)S(1)}) fusion(f32[512,3072]{1,0:T(8,128)} %fusion.293, f32[3072]{0:T(1024)S(1)} %bitcast.356, bf16[3072,768]{1,0:T(8,128)(2,1)} %all-gather.8.cloned.1.call-done, f32[768,512]{1,0:T(8,128)S(1)} %copy-done.36), kind=kOutput, calls=%fused_computation.403 | convolution fusion | flops 2450912256 | bytes 15753216 | tf_op jit(solution)/shard_map/dot_general | solution.py:256
  474.0 10.3 %fusion.317 = (f32[3072]{0:T(1024)}, bf16[3072,512]{0,1:T(8,128)(2,1)S(1)}) fusion(f32[512,3072]{1,0:T(8,128)} %fusion.296, f32[3072]{0:T(1024)S(1)} %bitcast.357, bf16[3072,768]{1,0:T(8,128)(2,1)} %all-gather.8.cloned.1.call-done, f32[768,512]{1,0:T(8,128)S(1)} %copy-done.33), kind=kOutput, calls=%fused_computation.402 | convolution fusion | flops 2450912256 | bytes 15753216 | tf_op jit(solution)/shard_map/dot_general | solution.py:256
  491.6 8.6 fusion.316
  500.3 10.6 %add_convert_fusion.1 = bf16[3072,768]{1,0:T(8,128)(2,1)} fusion(f32[3072,768]{1,0:T(8,128)} %fusion.49, f32[3072,768]{1,0:T(8,128)S(1)} %fusion.43, bf16[3072,512]{0,1:T(8,128)(2,1)} %get-tuple-element.120, f32[768,512]{1,0:T(8,128)S(1)} %copy-done.6, f32[512]{0:T(512)S(1)} %add_rsqrt_fusion.1, f32[512]{0:T(512)S(1)} %broadcast_multiply_fusion.13, ...), kind=kOutput, calls=%fused_computation.1 | convolution fusion | flops 2424963072 | bytes 28321792 | tf_op jit(solution)/shard_map/dot_general | solution.py:256
  512.9 6.7 bitcast_add_fusion.1
  564.7 78.8 %shard_map.244 = (bf16[3,96,4096]{2,1,0:T(8,128)(2,1)}, bf16[8,3,96,128]{3,2,1,0:T(8,128)(2,1)}, bf16[3,96,4096]{2,1,0:T(8,128)(2,1)}) custom-call(bf16[3,768,512]{2,1,0:T(8,128)(2,1)} %maximum_maximum_fusion.u_ref, bf16[3,768,128]{2,1,0:T(8,128)(2,1)} %pad_maximum_fusion.2.e_ref, bf16[3,768,512]{2,1,0:T(8,128)(2,1)} %pad_maximum_fusion.1.f_ref), custom_call_target="tpu_custom_call" | custom-call | tf_op jit(solution)/shard_map/pallas_call | solution.py:118
  643.5 19.0 %convolution_add_fusion.1 = f32[3,96,4096]{2,1,0:T(8,128)} fusion(bf16[3,96,4096]{2,1,0:T(8,128)(2,1)} %get-tuple-element.20, bf16[4096,4096,1]{1,0,2:T(8,128)(2,1)} %constant.132, bf16[3,96,4096]{2,1,0:T(8,128)(2,1)} %get-tuple-element.19), kind=kOutput, calls=%fused_computation.48 | convolution fusion | flops 9666035712 | bytes 42991616 | tf_op jit(solution)/shard_map/jck,lk->jcl/dot_general | solution.py:402
  667.2 17.5 %reduce-scatter.6.cloned.1.call-done = bf16[384,768]{1,0:T(8,128)(2,1)} async-done(((bf16[3072,768]{1,0:T(8,128)(2,1)}), bf16[384,768]{1,0:T(8,128)(2,1)}) %reduce-scatter.6.cloned.1.call-update) | async-done | bytes 589840 | tf_op jit(solution)/shard_map/reduce_scatter | solution.py:424
  686.4 49.4 %shard_map.242 = bf16[3,96,4096]{2,1,0:T(8,128)(2,1)} custom-call(bf16[3,768,512]{2,1,0:T(8,128)(2,1)} %pad_maximum_fusion.a_ref), custom_call_target="tpu_custom_call" | custom-call | tf_op jit(solution)/shard_map/pallas_call | solution.py:118
  735.8 87.6 %shard_map.245 = bf16[3,96,4096]{2,1,0:T(8,128)(2,1)} custom-call(bf16[3,96,4096]{2,1,0:T(8,128)(2,1)} %fusion.30.x_ref), custom_call_target="tpu_custom_call" | custom-call | tf_op jit(solution)/shard_map/pallas_call | solution.py:118
  827.9 42.4 %all-reduce.1 = f32[3072]{0:T(1024)S(1)} all-reduce(f32[3072]{0:T(1024)S(1)} %add_add_fusion), channel_id=4, replica_groups=mesh['dp'=4,'tensor'=8] {'tensor'}, use_global_device_ids=true, to_apply=%region_30.31.clone | all-reduce | flops 3072 | bytes 24576
  (298 shorter events, 159.3 us)
Async XLA Ops:
  7.2 371.7 %all-gather.6.cloned.1.call-start = ((), (), s32[]{:S(2)}) async-start(), calls=%async_computation.3 | async-start | bytes 5308416 | tf_op jit(solution)/shard_map/all_gather | solution.py:238
  7.9 380.1 %all-gather.8.cloned.1.call-start = ((), (), s32[]{:S(2)}) async-start(), calls=%async_computation.4 | async-start | bytes 5308416 | tf_op jit(solution)/shard_map/all_gather | solution.py:239
  8.7 658.5 %reduce-scatter.8.cloned.1.call-start = ((), (), s32[]{:S(2)}) async-start(), calls=%async_computation.6 | async-start | bytes 5308416 | tf_op jit(solution)/shard_map/reduce_scatter | solution.py:424
  8.8 345.4 %copy-start.54 = (pred[128]{0:T(512)(128)(4,1)}, pred[128]{0:T(512)(128)(4,1)S(1)}, u32[]{:S(2)}) copy-start(pred[128]{0:T(512)(128)(4,1)S(1)} %iota_compare_fusion.2) | copy-start | bytes 388
  163.4 70.2 %copy-start.21 = (bf16[4096,128,1]{1,0,2:T(8,128)(2,1)S(1)}, bf16[4096,128,1]{1,0,2:T(8,128)(2,1)}, u32[]{:S(2)}) copy-start(bf16[4096,128,1]{1,0,2:T(8,128)(2,1)} %constant.133) | copy-start | bytes 3145732
  337.2 33.8 %copy-start.50 = (pred[256]{0:T(512)(128)(4,1)}, pred[256]{0:T(512)(128)(4,1)S(1)}, u32[]{:S(2)}) copy-start(pred[256]{0:T(512)(128)(4,1)S(1)} %iota_compare_fusion) | copy-start | bytes 772
  337.2 33.8 %copy-start.56 = (pred[128]{0:T(512)(128)(4,1)}, pred[128]{0:T(512)(128)(4,1)S(1)}, u32[]{:S(2)}) copy-start(pred[128]{0:T(512)(128)(4,1)S(1)} %iota_compare_fusion.1) | copy-start | bytes 388
  377.7 21.9 %copy-start.5 = (f32[768,512]{1,0:T(8,128)}, f32[768,512]{1,0:T(8,128)S(1)}, u32[]{:S(2)}) copy-start(f32[768,512]{1,0:T(8,128)S(1)} %get-tuple-element.86) | copy-start | bytes 4718596
  377.7 26.2 %copy-start.8 = (f32[768,512]{1,0:T(8,128)}, f32[768,512]{1,0:T(8,128)S(1)}, u32[]{:S(2)}) copy-start(f32[768,512]{1,0:T(8,128)S(1)} %get-tuple-element.66) | copy-start | bytes 4718596
  378.0 147.2 %copy-start.52 = (f32[512]{0:T(512)}, f32[512]{0:T(512)S(1)}, u32[]{:S(2)}) copy-start(f32[512]{0:T(512)S(1)} %broadcast_multiply_fusion.15) | copy-start | bytes 6148
  378.0 147.1 %copy-start.61 = (f32[512]{0:T(512)}, f32[512]{0:T(512)S(1)}, u32[]{:S(2)}) copy-start(f32[512]{0:T(512)S(1)} %add_rsqrt_fusion.5) | copy-start | bytes 6148
  378.9 146.3 %copy-start.53 = (f32[512]{0:T(512)}, f32[512]{0:T(512)S(1)}, u32[]{:S(2)}) copy-start(f32[512]{0:T(512)S(1)} %add_rsqrt_fusion.1) | copy-start | bytes 6148
  378.9 146.3 %copy-start.62 = (f32[512]{0:T(512)}, f32[512]{0:T(512)S(1)}, u32[]{:S(2)}) copy-start(f32[512]{0:T(512)S(1)} %add_rsqrt_fusion.3) | copy-start | bytes 6148
  399.6 46.2 %copy-start.20 = (f32[512,3072]{1,0:T(8,128)}, f32[512,3072]{1,0:T(8,128)S(1)}, u32[]{:S(2)}) copy-start(f32[512,3072]{1,0:T(8,128)S(1)} %fusion.290) | copy-start | bytes 18874372
  420.6 18.4 %slice-start.10 = ((s8[6291456]{0:T(1024)(128)(4,1)}), s8[4194304]{0:T(1024)(128)(4,1)S(1)}, s32[]{:S(2)}) async-start(s8[6291456]{0:T(1024)(128)(4,1)} %bitcast.374), calls=%async_computation.19 | async-start | bytes 8388608
  456.2 228.5 %reduce-scatter.6.cloned.1.call-start = ((), (), s32[]{:S(2)}) async-start(), calls=%async_computation.5 | async-start | bytes 5308416 | tf_op jit(solution)/shard_map/reduce_scatter | solution.py:424
  470.9 20.6 %slice-start = ((s8[6291456]{0:T(1024)(128)(4,1)}), s8[2097152]{0:T(1024)(128)(4,1)S(1)}, s32[]{:S(2)}) async-start(s8[6291456]{0:T(1024)(128)(4,1)} %bitcast.346), calls=%async_computation.9 | async-start | bytes 4194304
  470.9 20.6 %slice-start.8 = ((s8[4718592]{0:T(1024)(128)(4,1)}), s8[4194304]{0:T(1024)(128)(4,1)S(1)}, s32[]{:S(2)}) async-start(s8[4718592]{0:T(1024)(128)(4,1)} %bitcast.372), calls=%async_computation.17 | async-start | bytes 8388608
  510.9 359.5 %reduce-scatter.10.cloned.1.call-start = ((), (), s32[]{:S(2)}) async-start(), calls=%async_computation.7 | async-start | bytes 442368
  558.9 319.4 %all-reduce.6.cloned.1.call-start = ((), (), s32[]{:S(2)}) async-start(), calls=%async_computation.8 | async-start | bytes 2359296 | tf_op jit(solution)/shard_map/psum | solution.py:425
  643.5 19.0 %copy-start.49 = (bf16[8,3,96,128]{3,2,1,0:T(8,128)(2,1)S(1)}, bf16[8,3,96,128]{3,2,1,0:T(8,128)(2,1)}, u32[]{:S(2)}) copy-start(bf16[8,3,96,128]{3,2,1,0:T(8,128)(2,1)} %get-tuple-element.21) | copy-start | bytes 1769476
  643.5 19.1 %copy-start.22 = (bf16[4096,128,1]{1,0,2:T(8,128)(2,1)S(1)}, bf16[4096,128,1]{1,0,2:T(8,128)(2,1)}, u32[]{:S(2)}) copy-start(bf16[4096,128,1]{1,0,2:T(8,128)(2,1)} %constant.133) | copy-start | bytes 3145732
  662.5 22.2 %copy-start.24 = (bf16[1,768,512]{2,1,0:T(8,128)(2,1)S(1)}, bf16[1,768,512]{2,1,0:T(8,128)(2,1)}, u32[]{:S(2)}) copy-start(bf16[1,768,512]{2,1,0:T(8,128)(2,1)} %get-tuple-element.90) | copy-start | bytes 2359300
  662.6 22.2 %copy-start.28 = (bf16[1,768,512]{2,1,0:T(8,128)(2,1)S(1)}, bf16[1,768,512]{2,1,0:T(8,128)(2,1)}, u32[]{:S(2)}) copy-start(bf16[1,768,512]{2,1,0:T(8,128)(2,1)} %get-tuple-element.91) | copy-start | bytes 2359300
  (61 other events, 318.0 us)
Sparse Core Ops, SparseCore 0:
  10.2 95.7 all-gather.5
  108.2 141.1 all-gather.7
  456.4 97.0 reduce-scatter.7
  557.0 127.6 reduce-scatter.5
  687.8 120.8 reduce-scatter.9
  810.9 50.1 all-reduce.5

commit v2 on v1

v2 whole, which is shorter than its diff:
```python
import math

import jax
import jax.numpy as jnp
import numpy as np
from jax import lax
from jax.experimental import pallas as pl
from jax.experimental.pallas import tpu as pltpu
from jax.sharding import PartitionSpec as P

EPSILON = 1e-12
MESH = pl.DeviceIdType.MESH
BF = jnp.bfloat16
F32 = jnp.float32


def token_tables(length, group):
    half = length // (2 * group)
    n = np.arange(length, dtype=np.int64)

    def wave(k):
        angle = (n[:, None] * k[None, :] % length) * (2.0 * math.pi / length)
        return np.cos(angle), np.sin(angle)

    cos, sin = wave(np.arange(length // 2))
    main = np.stack(
        [cos.reshape(length, group, half), sin.reshape(length, group, half)], axis=2
    ).reshape(length, length)
    edge_cos, edge_sin = wave(half * (np.arange(group) + 1))
    edge = np.zeros((length, 128))
    edge[:, 0 : 2 * group : 2] = edge_cos
    edge[:, 1 : 2 * group : 2] = np.where(np.abs(edge_sin) < 1e-9, 0.0, edge_sin)
    return main.astype(BF), edge.astype(BF)


def hidden_tables(width):
    ids = np.arange(width, dtype=np.int64)
    angle = (ids[:, None] * ids[None, :] % width) * (2.0 * math.pi / width)
    return np.cos(angle).astype(BF), np.sin(angle).astype(BF)


class Place:
    def __init__(self, n_dp, n_tensor):
        self.n_dp, self.n_tensor = n_dp, n_tensor
        self.slices = n_tensor // 2
        self.group = 2 * n_dp
        self.dp = lax.axis_index("dp")
        self.tensor = lax.axis_index("tensor")
        self.z = self.tensor // 2
        self.y = self.tensor % 2
        self.g = self.dp * 2 + self.y
        self.block = self.block_of(self.dp, self.y)

    def block_of(self, dp, y):
        return ((dp % (self.n_dp // 2)) * 2 + dp // (self.n_dp // 2)) * 2 + y

    def dp_of(self, z):
        return (z % 2) * (self.n_dp // 2) + z // 2

    def peer(self, offset):
        g = self.g ^ offset
        return (g // 2, self.z * 2 + g % 2), g


def start_all(moves):
    for src, dst, send, recv, device, own in moves:
        if device is None:
            pltpu.make_async_copy(src, dst, recv).start()
        elif own is None:
            pltpu.make_async_remote_copy(src, dst, send, recv, device, MESH).start()
        else:
            @pl.when(own)
            def _():
                pltpu.make_async_copy(src, dst, recv).start()

            @pl.when(jnp.logical_not(own))
            def _():
                pltpu.make_async_remote_copy(src, dst, send, recv, device, MESH).start()


def wait_sent(moves):
    for src, dst, send, recv, device, own in moves:
        if device is None:
            continue
        if own is None:
            pltpu.make_async_copy(src, src, send).wait()
        else:
            @pl.when(jnp.logical_not(own))
            def _():
                pltpu.make_async_copy(src, src, send).wait()


def wait_arrived(arrivals):
    for ref, recv in arrivals:
        pltpu.make_async_copy(ref, ref, recv).wait()


def greet(sources, n_targets):
    barrier = pltpu.get_barrier_semaphore()
    count = 0
    for device, own in sources:
        if own is None:
            pl.semaphore_signal(barrier, inc=1, device_id=device, device_id_type=MESH)
        else:
            @pl.when(jnp.logical_not(own))
            def _():
                pl.semaphore_signal(barrier, inc=1, device_id=device, device_id_type=MESH)
    total = 0
    for own in n_targets:
        total = total + (1 if own is None else jnp.where(own, 0, 1))
    pl.semaphore_wait(barrier, total)


ANY = pl.BlockSpec(memory_space=pl.ANY)


def exchange(body, ins, outs, n_sems, collective_id):
    return pl.pallas_call(
        body,
        out_shape=outs,
        in_specs=[ANY] * len(ins),
        out_specs=[ANY] * len(outs),
        scratch_shapes=[pltpu.SemaphoreType.DMA((n_sems,)), pltpu.SemaphoreType.DMA((n_sems,))],
        compiler_params=pltpu.CompilerParams(collective_id=collective_id, has_side_effects=True),
    )(*ins)


def on_device(
    words, w_in, b_in, w_out, b_out, gain_one, shift_one, gain_two, shift_two, cotangent, valid
):
    seqs, columns, length = words.shape
    width = w_in.shape[1]
    n_dp, n_tensor = lax.axis_size("dp"), lax.axis_size("tensor")
    assert n_tensor == 2 * n_dp
    group = 2 * n_dp
    half = length // (2 * group)
    mix_scale = 1.0 / math.sqrt(length * width)
    table, edge_table = token_tables(length, group)
    hid_cos, hid_sin = hidden_tables(width)

    def to_slice_body(x_ref, o_ref, send, recv):
        at = Place(n_dp, n_tensor)
        moves, sources = [], []
        target_dp = at.dp_of(at.z)
        for j in range(seqs):
            z = (at.dp + j) % at.slices
            own = jnp.logical_and(target_dp == at.dp, z == at.z)
            moves.append((x_ref.at[j], o_ref.at[j], send.at[j], recv.at[j], (target_dp, z * 2 + at.y), own))
            sources.append((((at.z - j + at.n_dp) % at.n_dp, at.block), own))
        greet(sources, [m[5] for m in moves])
        start_all(moves)
        wait_sent(moves)
        wait_arrived([(m[1], m[3]) for m in moves])

    (x_col,) = exchange(
        to_slice_body, [words], [jax.ShapeDtypeStruct(words.shape, BF)], seqs, 1
    )

    spectrum = jnp.einsum("jcl,lk->jck", x_col, table, preferred_element_type=F32).astype(BF)
    edges = jnp.einsum("jcl,lk->jck", x_col, edge_table, preferred_element_type=F32).astype(BF)

    def to_tokens_body(x_ref, u_ref, e_ref, xo_ref, uo_ref, eo_ref, send, recv):
        at = Place(n_dp, n_tensor)
        rows = pl.ds(pl.multiple_of(at.block * columns, 16), columns)
        moves, sources = [], []
        k = 0
        for offset in range(group):
            device, g = at.peer(offset)
            if offset == 0:
                device = None
            else:
                sources.append((device, None))
            first = pl.ds(pl.multiple_of(g * half, 128), half)
            last = pl.ds(pl.multiple_of(length - (g + 1) * half, 128), half)
            mine = pl.ds(pl.multiple_of(g * 2 * half, 128), 2 * half)
            for j in range(seqs):
                for src, dst in (
                    (x_ref.at[j, :, first], xo_ref.at[j, rows, pl.ds(0, half)]),
                    (x_ref.at[j, :, last], xo_ref.at[j, rows, pl.ds(half, half)]),
                    (u_ref.at[j, :, mine], uo_ref.at[j, rows]),
                    (e_ref.at[j], eo_ref.at[j, rows]),
                ):
                    moves.append((src, dst, send.at[k], recv.at[k], device, None))
                    k += 1
        greet(sources, [None] * len(sources))
        start_all(moves)
        wait_sent(moves)
        wait_arrived([(m[1], m[3]) for m in moves])

    x_tok, u_tok, e_tok = exchange(
        to_tokens_body,
        [x_col, spectrum, edges],
        [
            jax.ShapeDtypeStruct((seqs, width, 2 * half), BF),
            jax.ShapeDtypeStruct((seqs, width, 2 * half), BF),
            jax.ShapeDtypeStruct((seqs, width, 128), BF),
        ],
        group * seqs * 4,
        2,
    )

    w_in_all = lax.all_gather(w_in, "tensor", axis=0, tiled=True)
    w_out_all = lax.all_gather(w_out, "tensor", axis=0, tiled=True)
    b_in_all = lax.all_gather(b_in, "tensor", axis=0, tiled=True)
    small = lax.all_gather(
        jnp.stack([b_out, gain_one, shift_one, gain_two, shift_two], 0), "tensor", axis=1, tiled=True
    )
    vectors = jnp.pad(small.T, ((0, 0), (0, 3)))
    keep_all = lax.all_gather(valid.astype(F32), "dp", axis=0, tiled=True)
    units = w_in_all.shape[0]
    tokens = 2 * half

    def dot(a, b, da, db):
        return lax.dot_general(a, b, (((da,), (db,)), ((), ())), preferred_element_type=F32)

    def layer_body(
        x_ref, u_ref, e_ref, c_ref, win_ref, wout_ref, cos_ref, sin_ref, vec, b_in_v, keep,
        act_o, gu_o, ge_o, gf_o, gin_o, gout_o, gb_o, gv_o,
        win, wout, cos, sin, xb, ub, eb, cb, ab, a_all, m_all, nl, gl, f1, f2, f3, tile, bacc, vacc, gtile,
        load, cot_send, cot_own, cot_recv, act_send, act_own, act_recv, col_send, col_recv, out_sem,
    ):
        at = Place(n_dp, n_tensor)
        tokens = 2 * half
        barrier = pltpu.get_barrier_semaphore()
        count = 0
        for j in range(seqs):
            src_dp = (at.z - j + at.n_dp) % at.n_dp
            for b in range(n_tensor):
                own = jnp.logical_and(src_dp == at.dp, at.tensor == b)

                @pl.when(jnp.logical_not(own))
                def _():
                    pl.semaphore_signal(barrier, inc=1, device_id=(src_dp, b), device_id_type=MESH)

                count = count + jnp.where(own, 0, 1)
        for j in range(seqs):
            z = (at.dp + j) % at.slices
            for g_ in range(group):
                own = jnp.logical_and(z == at.z, at.g == g_)

                @pl.when(jnp.logical_not(own))
                def _():
                    pl.semaphore_signal(barrier, inc=1, device_id=(g_ // 2, z * 2 + g_ % 2), device_id_type=MESH)

                count = count + jnp.where(own, 0, 1)
        for offset in range(1, group):
            device, _ = at.peer(offset)
            pl.semaphore_signal(barrier, inc=1, device_id=device, device_id_type=MESH)
            count = count + 1
        pl.semaphore_wait(barrier, count)

        def wait(ref, sem):
            pltpu.make_async_copy(ref, ref, sem).wait()

        def lanes(g):
            return (
                pl.ds(pl.multiple_of(g * half, 128), half),
                pl.ds(pl.multiple_of(length - (g + 1) * half, 128), half),
            )

        parts = (pl.ds(0, half), pl.ds(half, half))
        rows_of = lambda b: pl.ds(pl.multiple_of(b * columns, 16), columns)

        def cot_start(j):
            z = (at.dp + j) % at.slices
            for offset in range(group):
                g = at.g ^ offset
                for p in range(2):
                    src = c_ref.at[j, :, lanes(g)[p]]
                    dst = cb.at[j, rows_of(at.tensor), parts[p]]
                    device = (g // 2, z * 2 + g % 2)
                    if offset:
                        pltpu.make_async_remote_copy(src, dst, cot_send.at[j], cot_recv.at[j], device, MESH).start()
                    else:
                        @pl.when(z == at.z)
                        def _():
                            pltpu.make_async_copy(src, dst, cot_recv.at[j]).start()

                        @pl.when(z != at.z)
                        def _():
                            pltpu.make_async_remote_copy(src, dst, cot_own.at[j], cot_recv.at[j], device, MESH).start()

        def cot_finish(j):
            z = (at.dp + j) % at.slices
            wait(c_ref.at[j, :, pl.ds(0, length - 2 * half)], cot_send.at[j])

            @pl.when(z != at.z)
            def _():
                wait(c_ref.at[j, :, pl.ds(0, 2 * half)], cot_own.at[j])

        def act_start(j):
            dp = (at.z - j + at.n_dp) % at.n_dp
            for offset in range(n_tensor):
                b = at.tensor ^ offset
                for p in range(2):
                    src = ab.at[j, rows_of(b), parts[p]]
                    dst = act_o.at[j, :, lanes(at.g)[p]]
                    if offset:
                        pltpu.make_async_remote_copy(src, dst, act_send.at[j], act_recv.at[j], (dp, b), MESH).start()
                    else:
                        @pl.when(dp == at.dp)
                        def _():
                            pltpu.make_async_copy(src, dst, act_recv.at[j]).start()

                        @pl.when(dp != at.dp)
                        def _():
                            pltpu.make_async_remote_copy(src, dst, act_own.at[j], act_recv.at[j], (dp, b), MESH).start()

        def act_finish(j):
            dp = (at.z - j + at.n_dp) % at.n_dp
            wait(ab.at[j, pl.ds(0, width - columns)], act_send.at[j])

            @pl.when(dp != at.dp)
            def _():
                wait(ab.at[j, pl.ds(0, columns)], act_own.at[j])

            wait(act_o.at[j], act_recv.at[j])

        def col_moves(j):
            for offset in range(group):
                device, g_ = at.peer(offset)
                rows = rows_of(at.block_of(g_ // 2, g_ % 2))
                for i, (src, dst) in enumerate((
                    (ub.at[j, rows], gu_o.at[j, :, pl.ds(pl.multiple_of(at.g * tokens, 128), tokens)]),
                    (eb.at[j, rows], ge_o.at[at.g, j]),
                    (xb.at[j, rows, parts[0]], gf_o.at[j, :, lanes(at.g)[0]]),
                    (xb.at[j, rows, parts[1]], gf_o.at[j, :, lanes(at.g)[1]]),
                )):
                    kind = min(i, 2)
                    if offset:
                        yield pltpu.make_async_remote_copy(
                            src, dst, col_send.at[j, kind], col_recv.at[j, kind], device, MESH)
                    else:
                        yield pltpu.make_async_copy(src, dst, col_recv.at[j, kind])

        def col_finish(j):
            rest = pl.ds(0, width - columns)
            wait(ub.at[j, rest], col_send.at[j, 0])
            wait(eb.at[j, rest], col_send.at[j, 1])
            wait(xb.at[j, rest], col_send.at[j, 2])
            wait(gu_o.at[j], col_recv.at[j, 0])
            wait(ge_o.at[:, j], col_recv.at[j, 1])
            wait(gf_o.at[j], col_recv.at[j, 2])

        loads = {}
        def load_start(key, src, dst):
            loads[key] = pltpu.make_async_copy(src, dst, load.at[len(loads)])
            loads[key].start()

        for j in range(seqs):
            load_start(("u", j), u_ref.at[j], ub.at[j])
            load_start(("e", j), e_ref.at[j], eb.at[j])
            load_start(("x", j), x_ref.at[j], xb.at[j])
            if j == 0:
                load_start("cos", cos_ref, cos)
                load_start("sin", sin_ref, sin)
                load_start("win", win_ref, win)
                load_start("wout", wout_ref, wout)

        for j in range(seqs):
            cot_start(j)

        lane0 = lax.broadcasted_iota(jnp.int32, (half, half), 0)
        lane1 = lax.broadcasted_iota(jnp.int32, (half, half), 1)
        turn = jnp.where(lane0 + lane1 == half, 1.0, 0.0).astype(BF)
        edge0 = lax.broadcasted_iota(jnp.int32, (128, half), 0)
        edge1 = lax.broadcasted_iota(jnp.int32, (128, half), 1)
        pick_u = jnp.where((edge0 == 2 * at.g) & (edge1 == 0), 1.0, 0.0).astype(BF)
        pick_v = jnp.where((edge0 == 2 * at.g + 1) & (edge1 == 0), 1.0, 0.0).astype(BF)
        A, B = parts
        block = 256
        step = 32

        def over(rows, size, body, carry=None, unroll=2):
            def inner(i, c):
                r = pl.ds(pl.multiple_of(i * size, size), size)
                return body(r, c)
            return lax.fori_loop(0, rows // size, inner, carry, unroll=unroll)

        def fold(v):
            return jnp.sum(v.reshape(v.shape[0] // 8, 8, v.shape[1]), axis=0)

        def lane_fold(v):
            return sum(v[:, k * 128 : (k + 1) * 128] for k in range(v.shape[1] // 128))

        zeros8 = jnp.zeros((8, tokens), F32)

        def mean_of(total):
            return jnp.sum(total, axis=0, keepdims=True) / width

        def statistics(ref):
            total = over(width, step, lambda r, c: c + fold(ref[r, :]), zeros8)
            center = mean_of(total)
            def spread(r, c):
                off = ref[r, :] - center
                return c + fold(off * off)
            var = mean_of(over(width, step, spread, zeros8))
            return center, lax.rsqrt(var + EPSILON)

        bacc[...] = jnp.zeros_like(bacc)
        vacc[...] = jnp.zeros_like(vacc)

        def forward_mix(j):
            for key in ("u", "e", "x"):
                loads[(key, j)].wait()
            if j == 0:
                loads["cos"].wait()
                loads["sin"].wait()
            def turned(r, c):
                e = eb[j, r, :]
                tile[r, A] = (dot(ub[j, r, A], turn, 1, 0) + dot(e, pick_u, 1, 0)).astype(BF)
                tile[r, B] = (dot(ub[j, r, B], turn, 1, 0) + dot(e, pick_v, 1, 0)).astype(BF)
                return c
            over(width, block, turned, 0, unroll=1)
            def mixed(r, c):
                f1[r, A] = xb[j, r, A].astype(F32) + mix_scale * (
                    dot(cos[r, :], ub[j, :, A], 1, 0) - dot(sin[r, :], ub[j, :, B], 1, 0))
                f1[r, B] = xb[j, r, B].astype(F32) + mix_scale * (
                    dot(cos[r, :], tile[:, A], 1, 0) + dot(sin[r, :], tile[:, B], 1, 0))
                return c
            over(width, block, mixed, 0, unroll=1)
            center, inverse = statistics(f1)
            def scale(r, c):
                h = (f1[r, :] - center) * inverse
                f1[r, :] = h
                n = h * vec[r, 1:2] + vec[r, 2:3]
                f2[r, :] = n
                nl[j, r, :] = n.astype(BF)
                return c
            over(width, step, scale, 0)
            return inverse

        c0 = math.sqrt(2.0 / math.pi)
        c1 = c0 * 0.044715

        def forward_mlp(j):
            if j == 0:
                loads["win"].wait()
                loads["wout"].wait()
            def inner(r, c):
                v = dot(win[r, :], nl[j], 1, 0) + b_in_v[r, :]
                v2 = v * v
                p = 0.5 + 0.5 * jnp.tanh(v * (c0 + c1 * v2))
                a = v * p
                a_all[j, r, :] = a.astype(BF)
                m_all[j, r, :] = (p + a * (1.0 - p) * (2.0 * c0 + 6.0 * c1 * v2)).astype(BF)
                return c
            over(units, block, inner, 0, unroll=1)
            def outer(r, c):
                f2[r, :] = f2[r, :] + dot(wout[:, r], a_all[j], 0, 0) + vec[r, 0:1]
                return c
            for k in range(width // block):
                outer(pl.ds(k * block, block), 0)

        def second_norm(j):
            center, inverse = statistics(f2)
            flag = keep[((at.z - j + at.n_dp) % at.n_dp) * seqs + j]
            def result(r, c):
                h = (f2[r, :] - center) * inverse
                f2[r, :] = h
                ab[j, r, :] = (h * vec[r, 3:4] + vec[r, 4:5]).astype(BF)
                return c
            over(width, step, result, 0)
            act_start(j)
            wait(cb.at[j], cot_recv.at[j])
            def sums(r, c):
                go = cb[j, r, :].astype(F32) * flag
                h = f2[r, :]
                goh = go * h
                vacc[3, r, :] += lane_fold(goh)
                vacc[4, r, :] += lane_fold(go)
                gh = go * vec[r, 3:4]
                return c[0] + fold(gh), c[1] + fold(gh * h)
            m1, m2 = over(width, step, sums, (zeros8, zeros8))
            m1, m2 = mean_of(m1), mean_of(m2)
            def back(r, c):
                gh = cb[j, r, :].astype(F32) * flag * vec[r, 3:4]
                gs = inverse * (gh - m1 - f2[r, :] * m2)
                vacc[0, r, :] += lane_fold(gs)
                f3[r, :] = gs
                gl[j, r, :] = gs.astype(BF)
                return c
            over(width, step, back, 0)

        def backward_mlp(j):
            def inner(r, c):
                gi = dot(wout[r, :], gl[j], 1, 0) * m_all[j, r, :].astype(F32)
                bacc[r, :] += lane_fold(gi)
                m_all[j, r, :] = gi.astype(BF)
                return c
            over(units, block, inner, 0, unroll=1)
            for k in range(width // block):
                r = pl.ds(k * block, block)
                f3[r, :] = f3[r, :] + dot(win[:, r], m_all[j], 0, 0)

        def first_back(j, inverse):
            def sums(r, c):
                gn = f3[r, :]
                h = f1[r, :]
                gnh = gn * h
                vacc[1, r, :] += lane_fold(gnh)
                vacc[2, r, :] += lane_fold(gn)
                gh = gn * vec[r, 1:2]
                return c[0] + fold(gh), c[1] + fold(gh * h)
            m1, m2 = over(width, step, sums, (zeros8, zeros8))
            m1, m2 = mean_of(m1), mean_of(m2)
            def back(r, c):
                gf = inverse * (f3[r, :] * vec[r, 1:2] - m1 - f1[r, :] * m2)
                xb[j, r, :] = gf.astype(BF)
                tile[r, :] = (gf * mix_scale).astype(BF)
                return c
            over(width, step, back, 0)
            def fold_pairs(r, c):
                a = tile[r, A].astype(F32)
                b = tile[r, B]
                t = dot(b, turn, 1, 0)
                ub[j, r, A] = (t + a).astype(BF)
                ub[j, r, B] = (t - a).astype(BF)
                eb[j, r, :] = dot(b, pick_u + pick_v, 1, 1).astype(BF)
                return c
            over(width, block, fold_pairs, 0, unroll=1)
            even, odd, edge = ub[j, :, A], ub[j, :, B], eb[j]
            is_cos = lax.broadcasted_iota(jnp.int32, (block, 128), 1) % 2 == 0
            for k in range(width // block):
                r = pl.ds(k * block, block)
                f1[r, A] = dot(cos[r, :], even, 1, 0)
                f1[r, B] = dot(sin[r, :], odd, 1, 0)
                f2[r, 0:128] = jnp.where(is_cos, dot(cos[r, :], edge, 1, 0), dot(sin[r, :], edge, 1, 0))
            def pack(r, c):
                ub[j, r, :] = f1[r, :].astype(BF)
                eb[j, r, :] = f2[r, 0:128].astype(BF)
                return c
            over(width, step, pack, 0)
            for move in col_moves(j):
                move.start()

        for j in range(seqs):
            inverse = forward_mix(j)
            forward_mlp(j)
            second_norm(j)
            backward_mlp(j)
            first_back(j, inverse)

        n_tiles = units // block
        def weight_step(i, c):
            r = pl.ds(pl.multiple_of(i * block, block), block)
            slot = i % 2
            @pl.when(i >= 2)
            def _():
                wait(gin_o.at[pl.ds(0, block)], out_sem.at[slot, 0])
                wait(gin_o.at[pl.ds(0, block)], out_sem.at[slot, 1])
            tin = gtile.at[slot, 0]
            tout = gtile.at[slot, 1]
            s_in = jnp.zeros((block, width), F32)
            s_out = jnp.zeros((block, width), F32)
            for j in range(seqs):
                s_in = s_in + dot(m_all[j, r, :], nl[j], 1, 1)
                s_out = s_out + dot(a_all[j, r, :], gl[j], 1, 1)
            tin[...] = s_in.astype(BF)
            tout[...] = s_out.astype(BF)
            pltpu.make_async_copy(tin, gin_o.at[r], out_sem.at[slot, 0]).start()
            pltpu.make_async_copy(tout, gout_o.at[r], out_sem.at[slot, 1]).start()
            return c
        lax.fori_loop(0, n_tiles, weight_step, 0)
        for slot in range(2):
            wait(gin_o.at[pl.ds(0, block)], out_sem.at[slot, 0])
            wait(gin_o.at[pl.ds(0, block)], out_sem.at[slot, 1])
        gb_o[...] = bacc[...]
        gv_o[...] = vacc[...]
        for j in range(seqs):
            cot_finish(j)
            act_finish(j)
            col_finish(j)

    shape = jax.ShapeDtypeStruct
    dma = pltpu.SemaphoreType.DMA
    whole_vmem = pl.BlockSpec(memory_space=pltpu.VMEM)
    activations, gu_col, ge_col, gf_col, g_in, g_out, g_b, g_v = pl.pallas_call(
        layer_body,
        out_shape=[
            shape(words.shape, BF),
            shape((seqs, columns, length), BF),
            shape((group, seqs, columns, 128), BF),
            shape((seqs, columns, length), BF),
            shape((units, width), BF),
            shape((units, width), BF),
            shape((units, 128), F32),
            shape((5, width, 128), F32),
        ],
        in_specs=[ANY] * 8 + [whole_vmem, whole_vmem, pl.BlockSpec(memory_space=pltpu.SMEM)],
        out_specs=[ANY] * 6 + [whole_vmem, whole_vmem],
        scratch_shapes=[
            pltpu.VMEM((units, width), BF),
            pltpu.VMEM((units, width), BF),
            pltpu.VMEM((width, width), BF),
            pltpu.VMEM((width, width), BF),
            pltpu.VMEM((seqs, width, tokens), BF),
            pltpu.VMEM((seqs, width, tokens), BF),
            pltpu.VMEM((seqs, width, 128), BF),
            pltpu.VMEM((seqs, width, tokens), BF),
            pltpu.VMEM((seqs, width, tokens), BF),
            pltpu.VMEM((seqs, units, tokens), BF),
            pltpu.VMEM((seqs, units, tokens), BF),
            pltpu.VMEM((seqs, width, tokens), BF),
            pltpu.VMEM((seqs, width, tokens), BF),
            pltpu.VMEM((width, tokens), F32),
            pltpu.VMEM((width, tokens), F32),
            pltpu.VMEM((width, tokens), F32),
            pltpu.VMEM((width, tokens), BF),
            pltpu.VMEM((units, 128), F32),
            pltpu.VMEM((5, width, 128), F32),
            pltpu.VMEM((2, 2, 256, width), BF),
            dma((3 * seqs + 4,)),
            dma((seqs,)),
            dma((seqs,)),
            dma((seqs,)),
            dma((seqs,)),
            dma((seqs,)),
            dma((seqs,)),
            dma((seqs, 3)),
            dma((seqs, 3)),
            dma((2, 2)),
        ],
        compiler_params=pltpu.CompilerParams(
            collective_id=3, has_side_effects=True, vmem_limit_bytes=64 * 1024 * 1024
        ),
    )(
        x_tok, u_tok, e_tok, cotangent, w_in_all, w_out_all,
        jnp.asarray(hid_cos), jnp.asarray(hid_sin), vectors, b_in_all[:, None], keep_all,
    )
    ge_sum = jnp.sum(ge_col.astype(F32), axis=0).astype(BF)
    gw_col = (
        gf_col.astype(F32)
        + jnp.einsum("jck,lk->jcl", gu_col, table, preferred_element_type=F32)
        + jnp.einsum("jck,lk->jcl", ge_sum, edge_table, preferred_element_type=F32)
    ).astype(BF)

    def home_body(x_ref, o_ref, send, recv):
        at = Place(n_dp, n_tensor)
        moves, sources = [], []
        target_dp = at.dp_of(at.z)
        for j in range(seqs):
            z_ = (at.dp + j) % at.slices
            own = jnp.logical_and(target_dp == at.dp, z_ == at.z)
            moves.append((x_ref.at[j], o_ref.at[j], send.at[j], recv.at[j], ((at.z - j + at.n_dp) % at.n_dp, at.block), own))
            sources.append(((target_dp, z_ * 2 + at.y), own))
        greet(sources, [m[5] for m in moves])
        start_all(moves)
        wait_sent(moves)
        wait_arrived([(m[1], m[3]) for m in moves])

    (gw,) = exchange(home_body, [gw_col], [jax.ShapeDtypeStruct(words.shape, BF)], seqs, 6)
    grad_words = gw.astype(F32)

    def reduce_weight(v):
        part = lax.psum_scatter(v.astype(BF), "tensor", scatter_dimension=0, tiled=True)
        return lax.psum(part, "dp").astype(F32)

    grad_w_in = reduce_weight(g_in)
    grad_w_out = reduce_weight(g_out)
    g_b = jnp.sum(g_b, axis=1)
    rest = jnp.sum(g_v, axis=2)
    grad_b_in = lax.psum(lax.psum_scatter(g_b, "tensor", scatter_dimension=0, tiled=True), "dp")
    rest = lax.psum(lax.psum_scatter(rest, "tensor", scatter_dimension=1, tiled=True), "dp")
    return (
        activations,
        grad_words,
        grad_w_in,
        grad_b_in,
        grad_w_out,
        rest[0],
        rest[1],
        rest[2],
        rest[3],
        rest[4],
    )


def solution(mesh):
    spec = (
        P("dp", "tensor", None),
        P("tensor", None),
        P("tensor"),
        P("tensor", None),
        P("tensor"),
        P("tensor"),
        P("tensor"),
        P("tensor"),
        P("tensor"),
        P("dp", "tensor", None),
        P("dp"),
    )
    out = (
        P("dp", "tensor", None),
        P("dp", "tensor", None),
        P("tensor", None),
        P("tensor"),
        P("tensor", None),
        P("tensor"),
        P("tensor"),
        P("tensor"),
        P("tensor"),
        P("tensor"),
    )
    return jax.shard_map(on_device, mesh=mesh, in_specs=spec, out_specs=out, check_vma=False)
```

time: 896 us -> 761 us (0.85)
  matrix products: 232 us -> 41.5 us
  waiting for transfers between devices: 19 us -> 178 us
  Pallas kernels: 453 us -> 362 us
  other arithmetic: 40 us -> 12.2 us
  blocking collectives: 115 us -> 135 us
    pallas_call x6 -> x3, Pallas kernels: 453 us -> 214 us  [exchange(): pl.pallas_call(body, out_shape=outs, in_specs=[ANY] * len(ins), out_specs...]
    dot_general x51 -> x0, matrix products: 189 us -> none  [dot(): lax.dot_general(a, b, (((da,), (db,)), ((), ())), preferred_element_type=...]
    reduce_scatter x2, waiting for transfers between devices: 17.5 us -> 175 us  [reduce_weight(): lax.psum_scatter(v.astype(BF), 'tensor', scatter_dimension=0, tiled=True)]
    pallas_call x0 -> x1, Pallas kernels: none -> 148 us  [on_device(): pl.pallas_call(layer_body, out_shape=[shape(words.shape, BF), shape((seqs...]
    all_gather x1, blocking collectives: 26.5 us -> 44.4 us  [on_device(): b_in_all = lax.all_gather(b_in, 'tensor', axis=0, tiled=True)]
    reduce_sum x10 -> x2, other arithmetic: 18.5 us -> 2.61 us  [the longest x1 2.03 us: on_device(): g_b = jnp.sum(g_b, axis=1)]
    another operation x5 -> x0, other arithmetic: 12.6 us -> none  [on_device(): jnp.stack(q)]
  transfers between devices with their start and end apart: 6 -> 6, of which waited for: 1 -> 3; matrix products, arithmetic and copies ran while one was open for 23% -> 8% of each run, Pallas kernels for 51% -> 28%
where the time goes in v2:
time: 761 us; the launch traced here: 754 us
  Pallas kernels  362 us (48%)
  waiting for transfers between devices  178 us (23%)
  blocking collectives  135 us (18%)
  matrix products  41.5 us (5%)
  between operations  16.1 us (2%)
  other arithmetic  12.2 us (2%)
  local copies, waits for them, and re-layouts  10.2 us (1%)
    pallas_call x3, Pallas kernels, exchange(): pl.pallas_call(body, out_shape=outs, in_specs=[ANY] * len(ins), out_specs...  214 us
    reduce_scatter x2, waiting for transfers between devices, reduce_weight(): lax.psum_scatter(v.astype(BF), 'tensor', scatter_dimension=0, tiled=True)  175 us
    pallas_call x1, Pallas kernels, on_device(): pl.pallas_call(layer_body, out_shape=[shape(words.shape, BF), shape((seqs...  148 us
    unnamed x2, blocking collectives  53.3 us
    all_gather x1, blocking collectives, on_device(): b_in_all = lax.all_gather(b_in, 'tensor', axis=0, tiled=True)  44.4 us
    all_gather x1, blocking collectives, on_device(): lax.all_gather(jnp.stack([b_out, gain_one, shift_one, gain_two, shift_two...  30.5 us
    dot_general x1, matrix products, on_device(): jnp.einsum('jck,lk->jcl', gu_col, table, preferred_element_type=F32)  18.8 us
    dot_general x1, matrix products, on_device(): jnp.einsum('jcl,lk->jck', x_col, table, preferred_element_type=F32)  16.7 us
  transfers between devices with their start and end apart: 6, of which 3 were waited for; matrix products, arithmetic and copies ran while one was open for 8% of the time, Pallas kernels for 28%

profile of v2, /device:TPU:0, one launch (start us, length us, event | category | flops | bytes accessed | tf_op | source)
XLA Modules:
  0.0 754.2 jit_solution(2617170348372098157)
XLA Ops:
  8.7 1.2 dynamic-slice
  11.4 8.8 %all-reduce.1.keep = f32[12]{0:T(128)} all-reduce(f32[12]{0:T(128)S(1)} %convert_dynamic-update-slice_fusion), channel_id=1, replica_groups=mesh['dp'=4,'tensor'=8] {'dp'}, use_global_device_ids=true, to_apply=%add.1 | all-reduce | flops 12 | bytes 96
  20.2 54.3 %shard_map.240.x_ref = bf16[3,96,4096]{2,1,0:T(8,128)(2,1)} custom-call(bf16[3,96,4096]{2,1,0:T(8,128)(2,1)} %x_ref.1), custom_call_target="tpu_custom_call" | custom-call | tf_op jit(solution)/shard_map/pallas_call | solution.py:118
  74.6 44.4 %all-gather.1 = f32[8,1,384]{2,1,0:T(1,128)S(1)} all-gather(f32[1,1,384]{2,1,0:T(1,128)S(1)} %reshape.25), channel_id=1, replica_groups=mesh['dp'=4,'tensor'=8] {'tensor'}, dimensions={0}, use_global_device_ids=true | all-gather | bytes 13824 | tf_op jit(solution)/shard_map/all_gather | solution.py:204
  119.0 1.7 copy.31.b_in_v
  120.7 30.5 %all-gather = f32[8,96,5]{1,2,0:T(8,128)S(1)} all-gather(f32[1,96,5]{1,2,0:T(8,128)S(1)} %bitcast.42), channel_id=1, replica_groups=mesh['dp'=4,'tensor'=8] {'tensor'}, dimensions={0}, use_global_device_ids=true | all-gather | bytes 17280 | tf_op jit(solution)/shard_map/all_gather | solution.py:205
  151.2 0.9 copy.30
  152.1 1.8 pad.4.vec
  153.9 1.4 fusion.2.e_ref
  155.3 16.7 %fusion.1.u_ref = bf16[3,96,4096]{2,1,0:T(8,128)(2,1)} fusion(bf16[4096,4096,1]{1,0,2:T(8,128)(2,1)} %constant.33, bf16[3,96,4096]{2,1,0:T(8,128)(2,1)S(1)} %copy-done), kind=kOutput, calls=%fused_computation.4 | convolution fusion | flops 9664856064 | bytes 38273024 | tf_op jit(solution)/shard_map/jcl,lk->jck/dot_general | solution.py:159
  172.0 84.6 %shard_map.241 = (bf16[3,768,512]{2,1,0:T(8,128)(2,1)}, bf16[3,768,512]{2,1,0:T(8,128)(2,1)}, bf16[3,768,128]{2,1,0:T(8,128)(2,1)}) custom-call(bf16[3,96,4096]{2,1,0:T(8,128)(2,1)} %shard_map.240.x_ref, bf16[3,96,4096]{2,1,0:T(8,128)(2,1)} %fusion.1.u_ref, bf16[3,96,128]{2,1,0:T(8,128)(2,1)} %fusion.2.e_ref), custom_call_target="tpu_custom_call" | custom-call | tf_op jit(solution)/shard_map/pallas_call | solution.py:118
  256.6 147.8 %shard_map.242 = (bf16[3,96,4096]{2,1,0:T(8,128)(2,1)}, bf16[3,96,4096]{2,1,0:T(8,128)(2,1)}, bf16[8,3,96,128]{3,2,1,0:T(8,128)(2,1)}, bf16[3,96,4096]{2,1,0:T(8...) custom-call(bf16[3,768,512]{2,1,0:T(8,128)(2,1)} %get-tuple-element., ...), custom_call_target="tpu_custom_call" | custom-call | tf_op jit(solution)/shard_map/pallas_call | solution.py:578
  408.0 18.8 %convolution_add_fusion.1 = f32[3,96,4096]{2,1,0:T(8,128)} fusion(bf16[3,96,4096]{2,1,0:T(8,128)(2,1)} %get-tuple-element.26, bf16[4096,4096,1]{1,0,2:T(8,128)(2,1)} %constant.33, bf16[3,96,4096]{2,1,0:T(8,128)(2,1)} %get-tuple-element.25), kind=kOutput, calls=%fused_computation.1 | convolution fusion | flops 9666035712 | bytes 42991616 | tf_op jit(solution)/shard_map/jck,lk->jcl/dot_general | solution.py:634
  426.9 76.3 %reduce-scatter.6.cloned.1.call-done = bf16[384,768]{1,0:T(8,128)(2,1)} async-done(((bf16[3072,768]{1,0:T(8,128)(2,1)}), bf16[384,768]{1,0:T(8,128)(2,1)}) %reduce-scatter.6.cloned.1.call-update) | async-done | bytes 589840 | tf_op jit(solution)/shard_map/reduce_scatter | solution.py:656
  503.2 98.5 %reduce-scatter.8.cloned.1.call-done = bf16[384,768]{1,0:T(8,128)(2,1)} async-done(((bf16[3072,768]{1,0:T(8,128)(2,1)}), bf16[384,768]{1,0:T(8,128)(2,1)}) %reduce-scatter.8.cloned.1.call-update) | async-done | bytes 589840 | tf_op jit(solution)/shard_map/reduce_scatter | solution.py:656
  601.8 4.5 fusion.x_ref
  606.3 74.8 %shard_map.243 = bf16[3,96,4096]{2,1,0:T(8,128)(2,1)} custom-call(bf16[3,96,4096]{2,1,0:T(8,128)(2,1)} %fusion.x_ref), custom_call_target="tpu_custom_call" | custom-call | tf_op jit(solution)/shard_map/pallas_call | solution.py:118
  681.2 4.4 convert_element_type.33
  685.6 2.0 reduce_sum.31
  687.6 44.5 %all-reduce.2 = f32[3072]{0:T(1024)S(1)} all-reduce(f32[3072]{0:T(1024)S(1)} %reduce_sum.31), channel_id=3, replica_groups=mesh['dp'=4,'tensor'=8] {'tensor'}, use_global_device_ids=true, to_apply=%region_4.5.clone | all-reduce | flops 3072 | bytes 24576
  733.0 6.9 all-reduce.3
  741.2 2.2 convert_element_type.34
  743.4 2.2 convert_element_type.35
  745.5 1.4 copy.38
  (53 shorter events, 7.6 us)
Async XLA Ops:
  7.2 249.4 %all-gather.5.cloned.1.call-start = ((), (), s32[]{:S(2)}) async-start(), calls=%async_computation.3 | async-start | bytes 5308416 | tf_op jit(solution)/shard_map/all_gather | solution.py:202
  7.9 248.7 %all-gather.7.cloned.1.call-start = ((), (), s32[]{:S(2)}) async-start(), calls=%async_computation.4 | async-start | bytes 5308416 | tf_op jit(solution)/shard_map/all_gather | solution.py:203
  8.7 494.6 %reduce-scatter.6.cloned.1.call-start = ((), (), s32[]{:S(2)}) async-start(), calls=%async_computation.5 | async-start | bytes 5308416 | tf_op jit(solution)/shard_map/reduce_scatter | solution.py:656
  20.2 54.4 %copy-start.6 = (f32[384]{0:T(512)S(1)}, f32[384]{0:T(512)}, u32[]{:S(2)}) copy-start(f32[384]{0:T(512)} %param.19) | copy-start | bytes 4612
  20.2 100.4 %copy-start.7 = (f32[96]{0:T(128)S(1)}, f32[96]{0:T(128)}, u32[]{:S(2)}) copy-start(f32[96]{0:T(128)} %param.21) | copy-start | bytes 1156
  20.2 100.4 %copy-start.8 = (f32[96]{0:T(128)S(1)}, f32[96]{0:T(128)}, u32[]{:S(2)}) copy-start(f32[96]{0:T(128)} %param.22) | copy-start | bytes 1156
  20.2 100.4 %copy-start.9 = (f32[96]{0:T(128)S(1)}, f32[96]{0:T(128)}, u32[]{:S(2)}) copy-start(f32[96]{0:T(128)} %param.23) | copy-start | bytes 1156
  20.2 100.4 %copy-start.10 = (f32[96]{0:T(128)S(1)}, f32[96]{0:T(128)}, u32[]{:S(2)}) copy-start(f32[96]{0:T(128)} %param.24) | copy-start | bytes 1156
  20.2 100.4 %copy-start.11 = (f32[96]{0:T(128)S(1)}, f32[96]{0:T(128)}, u32[]{:S(2)}) copy-start(f32[96]{0:T(128)} %param.25) | copy-start | bytes 1156
  20.2 133.7 %copy-start.1 = (bf16[4096,128,1]{1,0,2:T(8,128)(2,1)S(1)}, bf16[4096,128,1]{1,0,2:T(8,128)(2,1)}, u32[]{:S(2)}) copy-start(bf16[4096,128,1]{1,0,2:T(8,128)(2,1)} %constant.34) | copy-start | bytes 3145732
  74.6 79.3 %copy-start = (bf16[3,96,4096]{2,1,0:T(8,128)(2,1)S(1)}, bf16[3,96,4096]{2,1,0:T(8,128)(2,1)}, u32[]{:S(2)}) copy-start(bf16[3,96,4096]{2,1,0:T(8,128)(2,1)} %shard_map.240.x_ref) | copy-start | bytes 7077892
  404.4 197.4 %reduce-scatter.8.cloned.1.call-start = ((), (), s32[]{:S(2)}) async-start(), calls=%async_computation.6 | async-start | bytes 5308416 | tf_op jit(solution)/shard_map/reduce_scatter | solution.py:656
  404.5 0.7 copy-start.12
  404.5 1.9 copy-start.4
  405.0 327.2 %reduce-scatter.10.cloned.1.call-start = ((), (), s32[]{:S(2)}) async-start(), calls=%async_computation.7 | async-start | bytes 442368
  407.9 333.3 %all-reduce.7.cloned.1.call-start = ((), (), s32[]{:S(2)}) async-start(), calls=%async_computation.8 | async-start | bytes 2359296 | tf_op jit(solution)/shard_map/psum | solution.py:657
  408.0 18.8 %copy-start.5 = (bf16[8,3,96,128]{3,2,1,0:T(8,128)(2,1)S(1)}, bf16[8,3,96,128]{3,2,1,0:T(8,128)(2,1)}, u32[]{:S(2)}) copy-start(bf16[8,3,96,128]{3,2,1,0:T(8,128)(2,1)} %get-tuple-element.27) | copy-start | bytes 1769476
  426.8 175.0 %copy-start.2 = (bf16[4096,128,1]{1,0,2:T(8,128)(2,1)S(1)}, bf16[4096,128,1]{1,0,2:T(8,128)(2,1)}, u32[]{:S(2)}) copy-start(bf16[4096,128,1]{1,0,2:T(8,128)(2,1)} %constant.34) | copy-start | bytes 3145732
  685.6 60.0 %copy-start.3 = (bf16[3,96,4096]{2,1,0:T(8,128)(2,1)S(1)}, bf16[3,96,4096]{2,1,0:T(8,128)(2,1)}, u32[]{:S(2)}) copy-start(bf16[3,96,4096]{2,1,0:T(8,128)(2,1)} %get-tuple-element.51) | copy-start | bytes 7077892
Sparse Core Ops, SparseCore 0:
  10.2 124.0 all-gather.4
  136.4 117.9 all-gather.6
  404.5 98.6 reduce-scatter.5
  506.7 95.0 reduce-scatter.7
  605.5 96.7 reduce-scatter.9
  704.5 36.6 all-reduce.6

commit v3 on v2

v3 whole, which is shorter than its diff:
```python
import math

import jax
import jax.numpy as jnp
import numpy as np
from jax import lax
from jax.experimental import pallas as pl
from jax.experimental.pallas import tpu as pltpu
from jax.sharding import PartitionSpec as P

EPSILON = 1e-12
MESH = pl.DeviceIdType.MESH
BF = jnp.bfloat16
F32 = jnp.float32


def token_tables(length, group):
    half = length // (2 * group)
    n = np.arange(length, dtype=np.int64)

    def wave(k):
        angle = (n[:, None] * k[None, :] % length) * (2.0 * math.pi / length)
        return np.cos(angle), np.sin(angle)

    cos, sin = wave(np.arange(length // 2))
    main = np.stack(
        [cos.reshape(length, group, half), sin.reshape(length, group, half)], axis=2
    ).reshape(length, group, 2 * half)
    main = main.transpose(1, 0, 2).reshape(group * length, 2 * half)
    edge_cos, edge_sin = wave(half * (np.arange(group) + 1))
    edge = np.zeros((length, 128))
    edge[:, 0 : 2 * group : 2] = edge_cos
    edge[:, 1 : 2 * group : 2] = np.where(np.abs(edge_sin) < 1e-9, 0.0, edge_sin)
    return main.astype(BF), edge.astype(BF)


def hidden_tables(width):
    ids = np.arange(width, dtype=np.int64)
    angle = (ids[:, None] * ids[None, :] % width) * (2.0 * math.pi / width)
    return np.cos(angle).astype(BF), np.sin(angle).astype(BF)


class Place:
    def __init__(self, n_dp, n_tensor):
        self.n_dp, self.n_tensor = n_dp, n_tensor
        self.slices = n_tensor // 2
        self.group = 2 * n_dp
        self.dp = lax.axis_index("dp")
        self.tensor = lax.axis_index("tensor")
        self.z = self.tensor // 2
        self.y = self.tensor % 2
        self.g = self.dp * 2 + self.y
        self.block = self.block_of(self.dp, self.y)

    def block_of(self, dp, y):
        return ((dp % (self.n_dp // 2)) * 2 + dp // (self.n_dp // 2)) * 2 + y

    def dp_of(self, z):
        return (z % 2) * (self.n_dp // 2) + z // 2

    def peer(self, offset):
        g = self.g ^ offset
        return (g // 2, self.z * 2 + g % 2), g


ANY = pl.BlockSpec(memory_space=pl.ANY)


def on_device(
    words, w_in, b_in, w_out, b_out, gain_one, shift_one, gain_two, shift_two, cotangent, valid
):
    seqs, columns, length = words.shape
    width = w_in.shape[1]
    n_dp, n_tensor = lax.axis_size("dp"), lax.axis_size("tensor")
    assert n_tensor == 2 * n_dp
    group = 2 * n_dp
    half = length // (2 * group)
    mix_scale = 1.0 / math.sqrt(length * width)
    table, edge_table = token_tables(length, group)
    hid_cos, hid_sin = hidden_tables(width)

    table = jnp.asarray(table)
    edge_table = jnp.asarray(edge_table)
    units = w_in.shape[0] * n_tensor
    tokens = 2 * half

    def dot(a, b, da, db):
        return lax.dot_general(a, b, (((da,), (db,)), ((), ())), preferred_element_type=F32)

    wide = 512
    pad = lambda v: jnp.pad(v, (0, wide - v.shape[0]))
    rows_in = jnp.stack(
        [pad(v) for v in (b_in, b_out, gain_one, shift_one, gain_two, shift_two, valid.astype(F32))]
        + [jnp.zeros((wide,), F32)]
    )

    def layer_body(
        x_ref, c_ref, win_ref, wout_ref, cos_ref, sin_ref, table_ref, edge_ref, rows_ref,
        act_o, gu_o, ge_o, gf_o, gw_o, gin_o, gout_o, vec_o,
        win, wout, cos, sin, xb, ub, eb, cb, ab, a_all, m_all, nl, gl, f, tile, edge_v,
        bacc, vacc, b_in_v, vec, vrows, drows, grows, drows2, spare,
        load, slice_send, slice_recv, tok_send, tok_recv, vec_send, vec_recv, gather_send, gather_recv,
        cot_send, cot_own, cot_recv, act_send, act_own, act_recv, col_send, col_recv,
        ready, rs_send, rs_recv, table_sem, home_send, home_recv, more_send, more_recv, more_free,
        vg_send, vg_recv,
    ):
        at = Place(n_dp, n_tensor)
        barrier = pltpu.get_barrier_semaphore()
        count = 0
        for j in range(seqs):
            src_dp = (at.z - j + at.n_dp) % at.n_dp
            for b in range(n_tensor):
                mine_ = jnp.logical_and(src_dp == at.dp, at.tensor == b)

                @pl.when(jnp.logical_not(mine_))
                def _():
                    pl.semaphore_signal(barrier, inc=1, device_id=(src_dp, b), device_id_type=MESH)

                count = count + jnp.where(mine_, 0, 1)
        for j in range(seqs):
            z = (at.dp + j) % at.slices
            for g_ in range(group):
                mine_ = jnp.logical_and(z == at.z, at.g == g_)

                @pl.when(jnp.logical_not(mine_))
                def _():
                    pl.semaphore_signal(barrier, inc=1, device_id=(g_ // 2, z * 2 + g_ % 2), device_id_type=MESH)

                count = count + jnp.where(mine_, 0, 1)
        for offset in range(1, group):
            device, _ = at.peer(offset)
            pl.semaphore_signal(barrier, inc=1, device_id=device, device_id_type=MESH)
            count = count + 1
        for offset in range(1, n_tensor):
            pl.semaphore_signal(
                barrier, inc=1, device_id=(at.dp, at.tensor ^ offset), device_id_type=MESH)
            count = count + 1
        pl.semaphore_wait(barrier, count)

        def wait(ref, sem):
            pltpu.make_async_copy(ref, ref, sem).wait()

        def lanes(g):
            return (
                pl.ds(pl.multiple_of(g * half, 128), half),
                pl.ds(pl.multiple_of(length - (g + 1) * half, 128), half),
            )

        parts = (pl.ds(0, half), pl.ds(half, half))
        own = lambda j: pl.ds(j * tokens, tokens)
        f1, f2, f3 = [f.at[pl.ds(k * width, width)] for k in range(3)]
        rows_of = lambda b: pl.ds(pl.multiple_of(b * columns, 16), columns)

        def cot_start(j):
            z = (at.dp + j) % at.slices
            for offset in range(group):
                g = at.g ^ offset
                for p in range(2):
                    src = c_ref.at[j, :, lanes(g)[p]]
                    dst = cb.at[pl.ds(pl.multiple_of(j * width + at.tensor * columns, 16), columns), parts[p]]
                    device = (g // 2, z * 2 + g % 2)
                    if offset:
                        pltpu.make_async_remote_copy(src, dst, cot_send.at[j], cot_recv.at[j], device, MESH).start()
                    else:
                        @pl.when(z == at.z)
                        def _():
                            pltpu.make_async_copy(src, dst, cot_recv.at[j]).start()

                        @pl.when(z != at.z)
                        def _():
                            pltpu.make_async_remote_copy(src, dst, cot_own.at[j], cot_recv.at[j], device, MESH).start()

        def cot_finish(j):
            z = (at.dp + j) % at.slices
            wait(c_ref.at[j, :, pl.ds(0, length - 2 * half)], cot_send.at[j])

            @pl.when(z != at.z)
            def _():
                wait(c_ref.at[j, :, pl.ds(0, 2 * half)], cot_own.at[j])

        def act_start(j):
            dp = (at.z - j + at.n_dp) % at.n_dp
            for offset in range(n_tensor):
                b = at.tensor ^ offset
                for p in range(2):
                    src = ab.at[j, rows_of(b), parts[p]]
                    dst = act_o.at[j, :, lanes(at.g)[p]]
                    if offset:
                        pltpu.make_async_remote_copy(src, dst, act_send.at[j], act_recv.at[j], (dp, b), MESH).start()
                    else:
                        @pl.when(dp == at.dp)
                        def _():
                            pltpu.make_async_copy(src, dst, act_recv.at[j]).start()

                        @pl.when(dp != at.dp)
                        def _():
                            pltpu.make_async_remote_copy(src, dst, act_own.at[j], act_recv.at[j], (dp, b), MESH).start()

        def act_finish(j):
            dp = (at.z - j + at.n_dp) % at.n_dp
            wait(ab.at[j, pl.ds(0, width - columns)], act_send.at[j])

            @pl.when(dp != at.dp)
            def _():
                wait(ab.at[j, pl.ds(0, columns)], act_own.at[j])

            wait(act_o.at[j], act_recv.at[j])

        def col_moves(j):
            for offset in range(group):
                device, g_ = at.peer(offset)
                rows = rows_of(at.block_of(g_ // 2, g_ % 2))
                for i, (src, dst) in enumerate((
                    (ub.at[j, rows], gu_o.at[at.g, pl.ds(j * columns, columns)]),
                    (eb.at[j, rows], ge_o.at[at.g, pl.ds(j * columns, columns)]),
                    (xb.at[j, rows, parts[0]], gf_o.at[j, :, lanes(at.g)[0]]),
                    (xb.at[j, rows, parts[1]], gf_o.at[j, :, lanes(at.g)[1]]),
                )):
                    kind = min(i, 2)
                    if offset:
                        yield pltpu.make_async_remote_copy(
                            src, dst, col_send.at[j, kind], col_recv.at[j, kind], device, MESH)
                    else:
                        yield pltpu.make_async_copy(src, dst, col_recv.at[j, kind])

        def col_finish(j):
            rest = pl.ds(0, width - columns)
            wait(ub.at[j, rest], col_send.at[j, 0])
            wait(eb.at[j, rest], col_send.at[j, 1])
            wait(xb.at[j, rest], col_send.at[j, 2])

        def col_arrived(j):
            wait(gu_o.at[:, pl.ds(j * columns, columns)], col_recv.at[j, 0])
            wait(ge_o.at[:, pl.ds(j * columns, columns)], col_recv.at[j, 1])
            wait(gf_o.at[j], col_recv.at[j, 2])

        two = own(2)
        n_pieces = length // tokens

        def slice_at(j):
            z = (at.dp + j) % at.slices
            dp = at.dp_of(at.z)
            return (dp, z * 2 + at.y), jnp.logical_and(dp == at.dp, z == at.z)

        def slice_start(j):
            device, here = slice_at(j)
            for k in range(n_pieces):
                src = x_ref.at[j, :, pl.ds(k * tokens, tokens)]
                dst = a_all.at[pl.ds(j * width + k * columns, columns), two]

                @pl.when(here)
                def _():
                    pltpu.make_async_copy(src, dst, slice_recv.at[j]).start()

                @pl.when(jnp.logical_not(here))
                def _():
                    pltpu.make_async_remote_copy(src, dst, slice_send.at[j], slice_recv.at[j], device, MESH).start()

        def slice_finish(j):
            _, here = slice_at(j)

            @pl.when(jnp.logical_not(here))
            def _():
                wait(x_ref.at[j], slice_send.at[j])

        depth = min(1024, length // 2)
        n_chunks = length // depth
        per = depth // tokens
        def front_slot(i):
            ref = (a_all, m_all)[i % 2]
            return ref.at[pl.ds(i // 2 * depth, depth), own(1)]

        def table_rows(c, g):
            return table_ref.at[pl.ds(pl.multiple_of(g * length + c * depth, 16), depth)]

        order = [(offset, c) for offset in reversed(range(group)) for c in range(n_chunks)]
        def front_load(i):
            offset, c = order[i]
            return pltpu.make_async_copy(table_rows(c, at.g ^ offset), front_slot(i % 6), table_sem.at[i % 6])

        def to_tokens(js, offset, kinds):
            device, g = at.peer(offset)
            rows = rows_of(at.block)
            for j in js:
                moves = []
                if "u" in kinds:
                    moves.append((m_all.at[pl.ds(j * width + offset * columns, columns), two], ub.at[j, rows], 0))
                if "e" in kinds:
                    moves.append((m_all.at[pl.ds(seqs * width + j * columns, columns), pl.ds(2 * tokens, 128)], eb.at[j, rows], 1))
                if "x" in kinds:
                    for p, i in ((0, g), (1, 2 * group - 1 - g)):
                        moves.append((
                            a_all.at[pl.ds(pl.multiple_of(j * width + i // 2 * columns, 16), columns),
                                     pl.ds(pl.multiple_of(2 * tokens + i % 2 * half, 128), half)],
                            xb.at[j, rows, parts[p]], 2))
                for src, dst, kind in moves:
                    if offset:
                        pltpu.make_async_remote_copy(
                            src, dst, tok_send.at[j, kind], tok_recv.at[j, kind], device, MESH).start()
                    else:
                        pltpu.make_async_copy(src, dst, tok_recv.at[j, kind]).start()

        def front_prefetch():
            for i in range(6):
                front_load(i).start()

        def front_pass(js):
            m = len(js) * columns
            def piece(k):
                vals = [a_all[j * width + k * columns : j * width + (k + 1) * columns, 2 * tokens : 3 * tokens] for j in js]
                return vals[0] if len(vals) == 1 else jnp.concatenate(vals, axis=0)
            for offset in range(1, group):
                to_tokens(js, offset, "x")
            edge = jnp.zeros((m, 128), F32)
            for k in range(n_pieces):
                edge = edge + dot(piece(k), edge_v[k * tokens : (k + 1) * tokens, :], 1, 0)
            for i, j in enumerate(js):
                m_all[seqs * width + j * columns : seqs * width + (j + 1) * columns, 2 * tokens : 2 * tokens + 128] = (
                    edge[i * columns : (i + 1) * columns].astype(BF))
            for n, (offset, c) in enumerate(order):
                if c == 0:
                    total = jnp.zeros((m, tokens), F32)
                front_load(n).wait()
                slot = front_slot(n % 6)
                for s_ in range(per):
                    total = total + dot(piece(c * per + s_), slot[pl.ds(s_ * tokens, tokens), :], 1, 0)
                if n + 6 < len(order):
                    front_load(n + 6).start()
                if c == n_chunks - 1:
                    for i, j in enumerate(js):
                        m_all[j * width + offset * columns : j * width + (offset + 1) * columns, 2 * tokens : 3 * tokens] = (
                            total[i * columns : (i + 1) * columns].astype(BF))
                    to_tokens(js, offset, "ue" if offset else "uex")

        def tokens_arrived(j):
            wait(ub.at[j], tok_recv.at[j, 0])
            wait(eb.at[j], tok_recv.at[j, 1])
            wait(xb.at[j], tok_recv.at[j, 2])

        def tokens_sent(j):
            rest = pl.ds(0, width - columns)
            wait(ub.at[j, rest], tok_send.at[j, 0])
            wait(eb.at[j, rest], tok_send.at[j, 1])
            wait(xb.at[j, rest], tok_send.at[j, 2])

        bt = units // n_tensor
        hb, qb = bt // 2, bt // 4
        slices = at.slices
        core, x = at.dp % 2, at.dp // 2 % 2
        flip = lambda bit: (at.dp ^ bit, at.tensor)
        core_peer, x_peer, y_peer = flip(1), flip(2), (at.dp, at.tensor ^ 1)
        z_peer = lambda offset: (at.dp, (at.z ^ offset) * 2 + at.y)
        w_refs, w_bufs = (win_ref, wout_ref), (win, wout)
        n_far = slices - 1

        def piece_rows(o, y, n_quarters, xx):
            start = ((at.z ^ o) * 2 + y) * bt + core * hb + xx * qb
            return pl.ds(pl.multiple_of(start, 16), n_quarters * qb)

        def pass_on(level, arr, rows, key, device):
            ref = w_bufs[arr].at[rows]
            pltpu.make_async_remote_copy(
                ref, ref, gather_send.at[level, arr], gather_recv.at[level, arr, key], device, MESH).start()

        def arrive(level, arr, rows, key):
            wait(w_bufs[arr].at[rows], gather_recv.at[level, arr, key])

        def gather_start():
            mine = pl.ds(pl.multiple_of(core * hb + x * qb, 16), qb)
            half_rows = pl.ds(pl.multiple_of(core * hb, 16), hb)
            for arr in range(2):
                for o in range(1, slices):
                    pltpu.make_async_remote_copy(
                        w_refs[arr].at[mine], w_bufs[arr].at[piece_rows(0, at.y, 1, x)],
                        gather_send.at[0, arr], gather_recv.at[0, arr, o - 1], z_peer(o), MESH).start()
            for arr in range(2):
                pltpu.make_async_remote_copy(
                    w_refs[arr].at[half_rows], w_bufs[arr].at[piece_rows(0, at.y, 2, 0)],
                    gather_send.at[2, arr], gather_recv.at[2, arr, 0], y_peer, MESH).start()
                pltpu.make_async_copy(
                    w_refs[arr], w_bufs[arr].at[pl.ds(pl.multiple_of(at.tensor * bt, 16), bt)], load.at[arr]).start()

        def gather_two():
            for arr in range(2):
                for o in range(1, slices):
                    rows = piece_rows(o, at.y, 1, x)
                    arrive(0, arr, rows, o - 1)
                    pass_on(1, arr, rows, o - 1, x_peer)
                    pass_on(2, arr, rows, 2 * o - 1, y_peer)
                    pass_on(3, arr, rows, 2 * o - 2, core_peer)

        def gather_three():
            for arr in range(2):
                for o in range(1, slices):
                    rows = piece_rows(o, at.y, 1, 1 - x)
                    arrive(1, arr, rows, o - 1)
                    pass_on(2, arr, rows, 2 * o, y_peer)
                    pass_on(3, arr, rows, 2 * o - 1, core_peer)

        def gather_four(arr):
            other = 1 - at.y
            keys = [(0, 2, 0, 0)] + [(o, 1, q, 2 * o - 1 + q) for o in range(1, slices) for q in range(2)]
            for o, n, q, key in keys:
                xx = 0 if n == 2 else (1 - x if q else x)
                rows = piece_rows(o, other, n, xx)
                arrive(2, arr, rows, key)
                pass_on(3, arr, rows, 2 * n_far + key, core_peer)

        def gather_last(arr):
            def theirs(o, y, n, xx):
                start = ((at.z ^ o) * 2 + y) * bt + (1 - core) * hb + xx * qb
                return pl.ds(pl.multiple_of(start, 16), n * qb)
            pltpu.make_async_copy(
                w_refs[arr], w_bufs[arr].at[pl.ds(pl.multiple_of(at.tensor * bt, 16), bt)], load.at[arr]).wait()
            for o in range(1, slices):
                for q in range(2):
                    arrive(3, arr, theirs(o, at.y, 1, 1 - x if q else x), 2 * o - 2 + q)
            arrive(3, arr, theirs(0, 1 - at.y, 2, 0), 2 * n_far)
            for o in range(1, slices):
                for q in range(2):
                    arrive(3, arr, theirs(o, 1 - at.y, 1, 1 - x if q else x), 2 * n_far + 2 * o - 1 + q)

        def gather_sent():
            for arr in range(2):
                g = w_bufs[arr]
                for level, quarters in enumerate((n_far, n_far, 2 + 2 * n_far, 2 * n_far + 2 + 2 * n_far)):
                    wait(g.at[pl.ds(0, quarters * qb)], gather_send.at[level, arr])

        def vectors_start():
            pltpu.make_async_copy(rows_ref, vrows.at[pl.ds(pl.multiple_of(at.tensor * 8, 8), 8)], vec_recv.at[0]).start()
            pltpu.make_async_copy(rows_ref, drows.at[pl.ds(pl.multiple_of(at.dp * 8, 8), 8)], vec_recv.at[1]).start()
            for offset in range(1, n_tensor):
                pltpu.make_async_remote_copy(
                    rows_ref, vrows.at[pl.ds(pl.multiple_of(at.tensor * 8, 8), 8)],
                    vec_send.at[0], vec_recv.at[0], (at.dp, at.tensor ^ offset), MESH).start()
            for offset in range(1, n_dp):
                pltpu.make_async_remote_copy(
                    rows_ref, drows.at[pl.ds(pl.multiple_of(at.dp * 8, 8), 8)],
                    vec_send.at[1], vec_recv.at[1], (at.dp ^ offset, at.tensor), MESH).start()

        def vectors_arrived():
            wait(vrows.at[pl.ds(0, 8 * n_tensor)], vec_recv.at[0])
            wait(drows, vec_recv.at[1])
            wait(vrows.at[pl.ds(0, 8 * (n_tensor - 1))], vec_send.at[0])
            wait(drows.at[pl.ds(0, 8 * (n_dp - 1))], vec_send.at[1])
            turned = vrows[...].T
            for t in range(n_tensor):
                b_in_v[t * bt : (t + 1) * bt, :] = turned[0:bt, 8 * t : 8 * t + 1]
                vec[t * columns : (t + 1) * columns, :] = turned[0:columns, 8 * t + 1 : 8 * t + 6]

        lane0 = lax.broadcasted_iota(jnp.int32, (half, half), 0)
        lane1 = lax.broadcasted_iota(jnp.int32, (half, half), 1)
        turn = jnp.where(lane0 + lane1 == half, 1.0, 0.0).astype(BF)
        edge0 = lax.broadcasted_iota(jnp.int32, (128, half), 0)
        edge1 = lax.broadcasted_iota(jnp.int32, (128, half), 1)
        pick_u = jnp.where((edge0 == 2 * at.g) & (edge1 == 0), 1.0, 0.0).astype(BF)
        pick_v = jnp.where((edge0 == 2 * at.g + 1) & (edge1 == 0), 1.0, 0.0).astype(BF)
        A, B = parts
        block = 256
        step = 32

        def over(rows, size, body, carry=None, unroll=2):
            def inner(i, c):
                r = pl.ds(pl.multiple_of(i * size, size), size)
                return body(r, c)
            return lax.fori_loop(0, rows // size, inner, carry, unroll=unroll)

        def fold(v):
            return jnp.sum(v.reshape(v.shape[0] // 8, 8, v.shape[1]), axis=0)

        def lane_fold(v):
            return sum(v[:, k * 128 : (k + 1) * 128] for k in range(v.shape[1] // 128))

        zeros8 = jnp.zeros((8, tokens), F32)

        def mean_of(total):
            return jnp.sum(total, axis=0, keepdims=True) / width

        def statistics(ref):
            total = over(width, step, lambda r, c: c + fold(ref[r, :]), zeros8)
            center = mean_of(total)
            def spread(r, c):
                off = ref[r, :] - center
                return c + fold(off * off)
            var = mean_of(over(width, step, spread, zeros8))
            return center, lax.rsqrt(var + EPSILON)

        bacc[...] = jnp.zeros_like(bacc)
        vacc[...] = jnp.zeros_like(vacc)

        def forward_mix(j):
            tokens_arrived(j)
            def turned(r, c):
                e = eb[j, r, :]
                tile[r, A] = (dot(ub[j, r, A], turn, 1, 0) + dot(e, pick_u, 1, 0)).astype(BF)
                tile[r, B] = (dot(ub[j, r, B], turn, 1, 0) + dot(e, pick_v, 1, 0)).astype(BF)
                return c
            over(width, block, turned, 0, unroll=1)
            def mixed(r, c):
                f1[r, A] = xb[j, r, A].astype(F32) + mix_scale * (
                    dot(cos[r, :], ub[j, :, A], 1, 0) - dot(sin[r, :], ub[j, :, B], 1, 0))
                f1[r, B] = xb[j, r, B].astype(F32) + mix_scale * (
                    dot(cos[r, :], tile[:, A], 1, 0) + dot(sin[r, :], tile[:, B], 1, 0))
                return c
            over(width, block, mixed, 0, unroll=1)
            center, inverse = statistics(f1)
            def scale(r, c):
                h = (f1[r, :] - center) * inverse
                f1[r, :] = h
                n = h * vec[r, 1:2] + vec[r, 2:3]
                f2[r, :] = n
                nl[r, own(j)] = n.astype(BF)
                return c
            over(width, step, scale, 0)
            return inverse

        c0 = math.sqrt(2.0 / math.pi)
        c1 = c0 * 0.044715

        def forward_mlp(j):
            def inner(r, c):
                v = dot(win[r, :], nl[:, own(j)], 1, 0) + b_in_v[r, :]
                v2 = v * v
                p = 0.5 + 0.5 * jnp.tanh(v * (c0 + c1 * v2))
                a = v * p
                a_all[r, own(j)] = a.astype(BF)
                m_all[r, own(j)] = (p + a * (1.0 - p) * (2.0 * c0 + 6.0 * c1 * v2)).astype(BF)
                return c
            over(units, block, inner, 0, unroll=1)
            def outer(r, c):
                f2[r, :] = f2[r, :] + dot(wout[:, r], a_all[:, own(j)], 0, 0) + vec[r, 0:1]
                return c
            for k in range(width // block):
                outer(pl.ds(k * block, block), 0)

        def second_norm(j):
            center, inverse = statistics(f2)
            flag = drows[pl.ds(pl.multiple_of((at.z - j + at.n_dp) % at.n_dp * 8, 8), 8), 0:128][6:7, j : j + 1]
            def result(r, c):
                h = (f2[r, :] - center) * inverse
                f2[r, :] = h
                ab[j, r, :] = (h * vec[r, 3:4] + vec[r, 4:5]).astype(BF)
                return c
            over(width, step, result, 0)
            act_start(j)
            wait(cb.at[pl.ds(j * width, width)], cot_recv.at[j])
            def sums(r, c):
                go = cb[pl.ds(pl.multiple_of(j * width + r.start, 16), r.size), :].astype(F32) * flag
                h = f2[r, :]
                goh = go * h
                vacc[3, r, :] += lane_fold(goh)
                vacc[4, r, :] += lane_fold(go)
                gh = go * vec[r, 3:4]
                return c[0] + fold(gh), c[1] + fold(gh * h)
            m1, m2 = over(width, step, sums, (zeros8, zeros8))
            m1, m2 = mean_of(m1), mean_of(m2)
            def back(r, c):
                gh = cb[pl.ds(pl.multiple_of(j * width + r.start, 16), r.size), :].astype(F32) * flag * vec[r, 3:4]
                gs = inverse * (gh - m1 - f2[r, :] * m2)
                vacc[0, r, :] += lane_fold(gs)
                f3[r, :] = gs
                gl[r, own(j)] = gs.astype(BF)
                return c
            over(width, step, back, 0)

        def backward_inner(j):
            def inner(r, c):
                gi = dot(wout[r, :], gl[:, own(j)], 1, 0) * m_all[r, own(j)].astype(F32)
                bacc[r, :] += lane_fold(gi)
                m_all[r, own(j)] = gi.astype(BF)
                return c
            over(units, block, inner, 0, unroll=1)

        def backward_outer(j):
            for k in range(width // block):
                r = pl.ds(k * block, block)
                f3[r, :] = f3[r, :] + dot(win[:, r], m_all[:, own(j)], 0, 0)

        def first_back(j, inverse):
            def sums(r, c):
                gn = f3[r, :]
                h = f1[r, :]
                gnh = gn * h
                vacc[1, r, :] += lane_fold(gnh)
                vacc[2, r, :] += lane_fold(gn)
                gh = gn * vec[r, 1:2]
                return c[0] + fold(gh), c[1] + fold(gh * h)
            m1, m2 = over(width, step, sums, (zeros8, zeros8))
            m1, m2 = mean_of(m1), mean_of(m2)
            def back(r, c):
                gf = inverse * (f3[r, :] * vec[r, 1:2] - m1 - f1[r, :] * m2)
                xb[j, r, :] = gf.astype(BF)
                tile[r, :] = (gf * mix_scale).astype(BF)
                return c
            over(width, step, back, 0)
            def fold_pairs(r, c):
                a = tile[r, A].astype(F32)
                b = tile[r, B]
                t = dot(b, turn, 1, 0)
                ub[j, r, A] = (t + a).astype(BF)
                ub[j, r, B] = (t - a).astype(BF)
                eb[j, r, :] = dot(b, pick_u + pick_v, 1, 1).astype(BF)
                return c
            over(width, block, fold_pairs, 0, unroll=1)
            even, odd, edge = ub[j, :, A], ub[j, :, B], eb[j]
            is_cos = lax.broadcasted_iota(jnp.int32, (block, 128), 1) % 2 == 0
            for k in range(width // block):
                r = pl.ds(k * block, block)
                f1[r, A] = dot(cos[r, :], even, 1, 0)
                f1[r, B] = dot(sin[r, :], odd, 1, 0)
                f2[r, 0:128] = jnp.where(is_cos, dot(cos[r, :], edge, 1, 0), dot(sin[r, :], edge, 1, 0))
            def pack(r, c):
                ub[j, r, :] = f1[r, :].astype(BF)
                eb[j, r, :] = f2[r, 0:128].astype(BF)
                return c
            over(width, step, pack, 0)
            for move in col_moves(j):
                move.start()

        grads = (wout, win)
        if seqs * tokens >= 2 * width:
            land = lambda rows, arr: a_all.at[rows, pl.ds(arr * width, width)]
        else:
            land = lambda rows, arr: spare.at[rows, pl.ds(arr * width, width)]
        at2 = n_tensor * hb
        at3 = at2 + slices * hb
        at4 = at3 + slices * qb
        at5 = at4 + (slices - 1) * qb
        land1 = lambda arr, k: land(pl.ds(pl.multiple_of(k * hb, 16), hb), arr)
        land2 = lambda arr, k, n: land(pl.ds(at2 + k * n, n), arr)
        land3 = lambda arr, k: land(pl.ds(at3 + k * qb, qb), arr)
        land4 = lambda arr, k: land(pl.ds(at4 + k * qb, qb), arr)
        land5 = lambda arr: land(pl.ds(at5, qb), arr)
        def block_at(k):
            y = jnp.where(k < slices, 1 - at.y, at.y)
            return (k % slices) * 2 + y
        def rows_half(k, c):
            return pl.ds(pl.multiple_of(block_at(k) * bt + c * hb, 16), hb)
        def rows_quarter(k, xx):
            return pl.ds(pl.multiple_of(block_at(k) * bt + core * hb + xx * qb, 16), qb)

        def send(src, dst, level, arr, k, device):
            pltpu.make_async_remote_copy(
                src, dst, rs_send.at[level, arr], rs_recv.at[level, arr, k], device, MESH).start()

        def ready_signal():
            for i, device in enumerate([core_peer, x_peer, y_peer] + [z_peer(o) for o in range(1, slices)]
                                       + [flip(1 << b) for b in range(2, n_dp.bit_length() - 1)]):
                pl.semaphore_signal(ready.at[i], inc=1, device_id=device, device_id_type=MESH)

        def weight_grads(arr, left, right):
            def tile_step(k, c):
                r = pl.ds(pl.multiple_of(block_at(k) * bt, 16), bt)
                grads[arr][r, :] = dot(left[r, :], right[...], 1, 1).astype(BF)
                return c
            lax.fori_loop(0, n_tensor, tile_step, 0)

        def level1(arr):
            def go(k, c):
                send(grads[arr].at[rows_half(k, 1 - core)], land1(arr, k), 0, arr, k, core_peer)
                return c
            lax.fori_loop(0, n_tensor, go, 0)

        def add(arr, rows, landed, level, k):
            wait(landed, rs_recv.at[level, arr, k])
            ref = grads[arr].at[rows]
            n = ref.shape[0]
            def go(i, c):
                r = pl.ds(pl.multiple_of(i * 16, 16), 16)
                ref[r, :] = (ref[r, :].astype(F32) + landed[r, :].astype(F32)).astype(BF)
                return c
            lax.fori_loop(0, n // 16, go, 0, unroll=2)

        def after1(arr):
            def go(k, c):
                add(arr, rows_half(k, core), land1(arr, k), 0, k)
                if arr == 0:
                    @pl.when(k < slices)
                    def _():
                        send(grads[arr].at[rows_half(k, core)], land2(arr, k, hb), 1, arr, k, y_peer)
                else:
                    send(grads[arr].at[rows_quarter(k, 1 - x)], land2(arr, k, qb), 1, arr, k, x_peer)
                return c
            lax.fori_loop(0, n_tensor, go, 0)

        def after2(arr):
            if arr == 0:
                def go(k, c):
                    add(arr, rows_half(slices + k, core), land2(arr, k, hb), 1, k)
                    send(grads[arr].at[rows_quarter(slices + k, 1 - x)], land3(arr, k), 2, arr, k, x_peer)
                    return c
                lax.fori_loop(0, slices, go, 0)
            else:
                def go(k, c):
                    add(arr, rows_quarter(k, x), land2(arr, k, qb), 1, k)
                    @pl.when(k < slices)
                    def _():
                        send(grads[arr].at[rows_quarter(k, x)], land3(arr, k), 2, arr, k, y_peer)
                    return c
                lax.fori_loop(0, n_tensor, go, 0)

        def after3(arr):
            for offset in range(slices):
                k = at.z ^ offset
                add(arr, rows_quarter(slices + k, x), land3(arr, k), 2, k)
                if offset:
                    send(grads[arr].at[rows_quarter(slices + k, x)], land4(arr, offset - 1), 3, arr, offset - 1, z_peer(offset))

        def after4(arr):
            mine = rows_quarter(slices + at.z, x)
            for offset in range(1, slices):
                add(arr, mine, land4(arr, offset - 1), 3, offset - 1)
            for b in range(2, n_dp.bit_length() - 1):
                k = b - 2
                peer_ = flip(1 << b)
                pltpu.make_async_remote_copy(
                    grads[arr].at[mine], land5(arr), more_send.at[arr, k], more_recv.at[arr, k], peer_, MESH).start()
                wait(grads[arr].at[mine], more_send.at[arr, k])
                wait(land5(arr), more_recv.at[arr, k])
                ref = grads[arr].at[mine]
                ref[...] = (ref[...].astype(F32) + land5(arr)[...].astype(F32)).astype(BF)
                if b + 1 < n_dp.bit_length() - 1:
                    pl.semaphore_signal(more_free, inc=1, device_id=peer_, device_id_type=MESH)
                    pl.semaphore_wait(more_free, 1)
            home = pl.ds(pl.multiple_of(core * hb + x * qb, 16), qb)
            out = (gout_o, gin_o)[arr]
            pltpu.make_async_copy(grads[arr].at[mine], out.at[home], rs_recv.at[4, arr, 0]).start()
            for q in range(1, 4):
                pltpu.make_async_remote_copy(
                    grads[arr].at[mine], out.at[home], rs_send.at[4, arr], rs_recv.at[4, arr, q], flip(q), MESH).start()

        def rs_finish(arr):
            g = grads[arr]
            n = n_tensor * hb
            wait(g.at[pl.ds(0, n)], rs_send.at[0, arr])
            wait(g.at[pl.ds(0, slices * hb)], rs_send.at[1, arr])
            wait(g.at[pl.ds(0, slices * qb)], rs_send.at[2, arr])
            wait(g.at[pl.ds(0, (slices - 1) * qb)], rs_send.at[3, arr])
            wait(g.at[pl.ds(0, 3 * qb)], rs_send.at[4, arr])
            for q in range(4):
                wait((gout_o, gin_o)[arr].at[pl.ds(0, qb)], rs_recv.at[4, arr, q])

        every = seqs * columns
        n_slots = 6
        slot_ref = lambda i: m_all.at[pl.ds(i // 2 * depth, depth), pl.ds((1 + i % 2) * tokens, tokens)]
        def table_start(i):
            c, g = i // group, i % group
            rows = pl.ds(g * length + c * depth, depth)
            return pltpu.make_async_copy(table_ref.at[rows], slot_ref(i % n_slots), table_sem.at[i % n_slots])

        def words_back():
            steps = [(c, g) for c in range(n_chunks) for g in range(group)]
            for i in range(n_slots):
                table_start(i).start()
            for j in range(seqs):
                col_arrived(j)
            for g in range(group):
                pltpu.make_async_copy(gu_o.at[g], cb.at[pl.ds(g * every, every)], table_sem.at[n_slots + 1]).start()
            for g in range(group):
                pltpu.make_async_copy(ge_o.at[g], m_all.at[pl.ds(g * every, every), pl.ds(0, 128)], table_sem.at[n_slots + 2]).start()
            for j in range(seqs):
                for k in range(length // tokens):
                    pltpu.make_async_copy(
                        gf_o.at[j, :, pl.ds(k * tokens, tokens)], nl.at[pl.ds(k * columns, columns), own(j)],
                        table_sem.at[n_slots + 3]).start()
            wait(cb, table_sem.at[n_slots + 1])
            wait(m_all.at[pl.ds(0, group * every), pl.ds(0, 128)], table_sem.at[n_slots + 2])
            wait(nl, table_sem.at[n_slots + 3])
            edge = m_all[0:every, 0:128].astype(F32)
            for g in range(1, group):
                edge = edge + m_all[g * every : (g + 1) * every, 0:128].astype(F32)
            edge = edge.astype(BF)
            for c in range(n_chunks):
                for s_ in range(per):
                    k = c * per + s_
                    acc = pl.ds(k * every, every)
                    f[acc, :] = dot(edge, edge_v[k * tokens : (k + 1) * tokens, :], 1, 1)
                for g in range(group):
                    i = c * group + g
                    table_start(i).wait()
                    for s_ in range(per):
                        acc = pl.ds((c * per + s_) * every, every)
                        f[acc, :] += dot(cb[pl.ds(g * every, every), :], slot_ref(i % n_slots)[pl.ds(s_ * tokens, tokens), :], 1, 1)
                    if i + n_slots < n_chunks * group:
                        table_start(i + n_slots).start()
                for s_ in range(per):
                    k = c * per + s_
                    for j in range(seqs):
                        rows = pl.ds(k * columns, columns)
                        gl[rows, own(j)] = (
                            f[pl.ds(k * every + j * columns, columns), :] + nl[rows, own(j)].astype(F32)).astype(BF)
                        home_start(j, k)

        def home_at(j):
            dp = (at.z - j + at.n_dp) % at.n_dp
            return dp, jnp.logical_and(dp == at.dp, at.block == at.tensor)

        def home_start(j, k):
            dp, here = home_at(j)
            src = gl.at[pl.ds(k * columns, columns), own(j)]
            dst = gw_o.at[j, :, pl.ds(k * tokens, tokens)]

            @pl.when(here)
            def _():
                pltpu.make_async_copy(src, dst, home_recv.at[j]).start()

            @pl.when(jnp.logical_not(here))
            def _():
                pltpu.make_async_remote_copy(src, dst, home_send.at[j], home_recv.at[j], (dp, at.block), MESH).start()

        def home_finish(j):
            dp, here = home_at(j)

            @pl.when(jnp.logical_not(here))
            def _():
                wait(gw_o.at[j], home_send.at[j])

            wait(gw_o.at[j], home_recv.at[j])

        def vector_grads():
            cols = pl.ds(0, 128)
            vrows[...] = jnp.zeros_like(vrows)
            turned = jnp.zeros((wide, 128), F32)
            scratch = f1.at[pl.ds(0, wide), cols]
            scratch[...] = turned
            for t in range(n_tensor):
                scratch[0:bt, 8 * t : 8 * t + 1] = jnp.sum(bacc[t * bt : (t + 1) * bt, :], axis=1, keepdims=True)
                for i in range(5):
                    scratch[0:columns, 8 * t + 1 + i : 8 * t + 2 + i] = jnp.sum(
                        vacc[i, t * columns : (t + 1) * columns, :], axis=1, keepdims=True)
            vrows[...] = scratch[...].T
            n = 8 * n_tensor
            for offset in range(1, n_dp):
                pltpu.make_async_remote_copy(
                    vrows.at[pl.ds(0, n)], grows.at[pl.ds((offset - 1) * n, n)],
                    vg_send.at[0], vg_recv.at[0], (at.dp ^ offset, at.tensor), MESH).start()

        def vector_grads_two():
            n = 8 * n_tensor
            wait(grows.at[pl.ds(0, (n_dp - 1) * n)], vg_recv.at[0])
            wait(grows.at[pl.ds(0, (n_dp - 1) * n)], vg_send.at[0])
            total = vrows[0:n, :]
            for offset in range(1, n_dp):
                total = total + grows[(offset - 1) * n : offset * n, :]
            vrows[0:n, :] = total
            for offset in range(1, n_tensor):
                t = at.tensor ^ offset
                pltpu.make_async_remote_copy(
                    vrows.at[pl.ds(pl.multiple_of(t * 8, 8), 8)], drows2.at[pl.ds((offset - 1) * 8, 8)],
                    vg_send.at[1], vg_recv.at[1], (at.dp, t), MESH).start()

        def vector_grads_three():
            n = 8 * (n_tensor - 1)
            wait(drows2.at[pl.ds(0, n)], vg_recv.at[1])
            wait(drows2.at[pl.ds(0, n)], vg_send.at[1])
            total = vrows[pl.ds(pl.multiple_of(at.tensor * 8, 8), 8), :]
            for offset in range(1, n_tensor):
                total = total + drows2[(offset - 1) * 8 : offset * 8, :]
            vec_o[...] = total

        tables = [
            pltpu.make_async_copy(src, dst, load.at[2 + i])
            for i, (src, dst) in enumerate(((edge_ref, edge_v), (cos_ref, cos), (sin_ref, sin)))
        ]
        slice_start(0)
        vectors_start()
        gather_start()
        for move in tables:
            move.start()
        front_prefetch()
        wait(a_all.at[pl.ds(0, width), two], slice_recv.at[0])
        for j in range(1, seqs):
            slice_start(j)
        tables[0].wait()
        front_pass([0])
        front_prefetch()
        gather_two()
        for j in range(seqs):
            cot_start(j)
        gather_three()
        tables[1].wait()
        tables[2].wait()
        vectors_arrived()
        for j in range(seqs):
            if j == 0:
                inverse = forward_mix(0)
                for arr in range(2):
                    gather_four(arr)
                for arr in range(2):
                    gather_last(arr)
            else:
                inverse = forward_mix(j)
            if j == 2:
                for i in range(seqs):
                    tokens_sent(i)
            forward_mlp(j)
            if j == 0:
                for i in range(1, seqs):
                    wait(a_all.at[pl.ds(i * width, width), two], slice_recv.at[i])
                front_pass(list(range(1, seqs)))
            second_norm(j)
            backward_inner(j)
            if j == seqs - 1:
                gather_sent()
                weight_grads(0, a_all, gl)
                ready_signal()
                pl.semaphore_wait(ready.at[0], 1)
                level1(0)
            backward_outer(j)
            if j == seqs - 1:
                weight_grads(1, m_all, nl)
                level1(1)
            first_back(j, inverse)
        vector_grads()
        for i in range(1, 3 + slices - 1 + max(0, n_dp.bit_length() - 3)):
            pl.semaphore_wait(ready.at[i], 1)
        after1(0)
        after1(1)
        vector_grads_two()
        words_back()
        after2(0)
        after2(1)
        after3(0)
        after3(1)
        after4(0)
        after4(1)
        for j in range(seqs):
            slice_finish(j)
            cot_finish(j)
            act_finish(j)
            col_finish(j)
            home_finish(j)
        vector_grads_three()
        rs_finish(0)
        rs_finish(1)

    shape = jax.ShapeDtypeStruct
    dma = pltpu.SemaphoreType.DMA
    whole_vmem = pl.BlockSpec(memory_space=pltpu.VMEM)
    need_spare = seqs * tokens < 2 * width
    regular = pltpu.SemaphoreType.REGULAR
    activations, _, _, _, gw, g_in, g_out, vec_g = pl.pallas_call(
        layer_body,
        out_shape=[
            shape(words.shape, BF),
            shape((group, seqs * columns, tokens), BF),
            shape((group, seqs * columns, 128), BF),
            shape((seqs, columns, length), BF),
            shape((seqs, columns, length), BF),
            shape(w_in.shape, BF),
            shape(w_in.shape, BF),
            shape((8, wide), F32),
        ],
        in_specs=[ANY] * 9,
        out_specs=[ANY] * 7 + [whole_vmem],
        scratch_shapes=[
            pltpu.VMEM((units, width), BF),
            pltpu.VMEM((units, width), BF),
            pltpu.VMEM((width, width), BF),
            pltpu.VMEM((width, width), BF),
            pltpu.VMEM((seqs, width, tokens), BF),
            pltpu.VMEM((seqs, width, tokens), BF),
            pltpu.VMEM((seqs, width, 128), BF),
            pltpu.VMEM((group * seqs * columns, tokens), BF),
            pltpu.VMEM((seqs, width, tokens), BF),
            pltpu.VMEM((units, seqs * tokens), BF),
            pltpu.VMEM((units, seqs * tokens), BF),
            pltpu.VMEM((width, seqs * tokens), BF),
            pltpu.VMEM((width, seqs * tokens), BF),
            pltpu.VMEM((3 * width, tokens), F32),
            pltpu.VMEM((width, tokens), BF),
            pltpu.VMEM((length, 128), BF),
            pltpu.VMEM((units, 128), F32),
            pltpu.VMEM((5, width, 128), F32),
            pltpu.VMEM((units, 1), F32),
            pltpu.VMEM((width, 5), F32),
            pltpu.VMEM((128, wide), F32),
            pltpu.VMEM((8 * n_dp, wide), F32),
            pltpu.VMEM((8 * n_tensor * (n_dp - 1), wide), F32),
            pltpu.VMEM((8 * (n_tensor - 1), wide), F32),
            pltpu.VMEM((units, 2 * width) if need_spare else (16, 128), BF),
            dma((5,)),
            dma((seqs,)),
            dma((seqs,)),
            dma((seqs, 3)),
            dma((seqs, 3)),
            dma((2,)),
            dma((2,)),
            dma((4, 2)),
            dma((4, 2, 2 * n_tensor)),
            dma((seqs,)),
            dma((seqs,)),
            dma((seqs,)),
            dma((seqs,)),
            dma((seqs,)),
            dma((seqs,)),
            dma((seqs, 3)),
            dma((seqs, 3)),
            regular((3 + n_tensor // 2 + n_dp,)),
            dma((5, 2)),
            dma((5, 2, n_tensor)),
            dma((10,)),
            dma((seqs,)),
            dma((seqs,)),
            dma((2, n_dp)),
            dma((2, n_dp)),
            regular,
            dma((2,)),
            dma((2,)),
        ],
        compiler_params=pltpu.CompilerParams(
            collective_id=1, has_side_effects=True, vmem_limit_bytes=64 * 1024 * 1024
        ),
    )(
        words, cotangent, w_in, w_out, jnp.asarray(hid_cos), jnp.asarray(hid_sin), table, edge_table, rows_in
    )
    grad_words = gw.astype(F32)

    grad_w_in = g_in.astype(F32)
    grad_w_out = g_out.astype(F32)
    return (
        activations,
        grad_words,
        grad_w_in,
        vec_g[0, : w_in.shape[0]],
        grad_w_out,
        vec_g[1, :columns],
        vec_g[2, :columns],
        vec_g[3, :columns],
        vec_g[4, :columns],
        vec_g[5, :columns],
    )


def solution(mesh):
    spec = (
        P("dp", "tensor", None),
        P("tensor", None),
        P("tensor"),
        P("tensor", None),
        P("tensor"),
        P("tensor"),
        P("tensor"),
        P("tensor"),
        P("tensor"),
        P("dp", "tensor", None),
        P("dp"),
    )
    out = (
        P("dp", "tensor", None),
        P("dp", "tensor", None),
        P("tensor", None),
        P("tensor"),
        P("tensor", None),
        P("tensor"),
        P("tensor"),
        P("tensor"),
        P("tensor"),
        P("tensor"),
    )
    return jax.shard_map(on_device, mesh=mesh, in_specs=spec, out_specs=out, check_vma=False)
```

time: 761 us -> 446 us (0.59)
  waiting for transfers between devices: 178 us -> 0 us
  blocking collectives: 135 us -> 0 us
  Pallas kernels: 362 us -> 424 us
  matrix products: 41.5 us -> 0 us
  between operations: 16.1 us -> 1.1 us
    reduce_scatter x2 -> x0, waiting for transfers between devices: 175 us -> none  [reduce_weight(): lax.psum_scatter(v.astype(BF), 'tensor', scatter_dimension=0, tiled=True)]
    all_gather x2 -> x0, blocking collectives: 74.8 us -> none  [the longest x1 44.4 us: on_device(): b_in_all = lax.all_gather(b_in, 'tensor', axis=0, tiled=True)]
    pallas_call x4 -> x1, Pallas kernels: 362 us -> 424 us  [on_device(): pl.pallas_call(layer_body, out_shape=[shape(words.shape, BF), shape((grou...]
    unnamed x2 -> x0, blocking collectives: 53.3 us -> none
    dot_general x4 -> x0, matrix products: 41.5 us -> none  [the longest x1 18.8 us: on_device(): jnp.einsum('jck,lk->jcl', gu_col, table, preferred_element_type=F32)]
  transfers between devices with their start and end apart: 6 -> 0, of which waited for: 3 -> 0; matrix products, arithmetic and copies ran while one was open for 8% -> 0% of each run, Pallas kernels for 28% -> 0%
where the time goes in v3:
time: 446 us; the launch traced here: 441 us
  Pallas kernels  424 us (95%)
  local copies, waits for them, and re-layouts  8.73 us (2%)
  other arithmetic  7.35 us (2%)
    pallas_call x1, Pallas kernels, on_device(): pl.pallas_call(layer_body, out_shape=[shape(words.shape, BF), shape((grou...  424 us

profile of v3, /device:TPU:0, one launch (start us, length us, event | category | flops | bytes accessed | tf_op | source)
XLA Modules:
  0.0 440.8 jit_solution(1460250079212346084)
XLA Ops:
  0.6 0.7 convert_element_type.22
  1.3 0.7 pad.24
  2.0 0.7 pad.25
  2.7 0.7 pad.26
  3.3 0.7 pad.27
  4.0 0.7 pad.28
  4.6 0.7 pad.29
  5.3 0.6 stack.31.rows_ref
  5.9 423.6 %shard_map.222 = (bf16[3,96,4096]{2,1,0:T(8,128)(2,1)}, bf16[8,288,512]{2,1,0:T(8,128)(2,1)}, bf16[8,288,128]{2,1,0:T(8,128)(2,1)}, bf16[3,96,4096]{2,1,0:T(8,12...) custom-call(bf16[3,96,4096]{2,1,0:T(8,128)(2,1)} %x_ref.1, ...), custom_call_target="tpu_custom_call" | custom-call | tf_op jit(solution)/shard_map/pallas_call | solution.py:942
  429.6 1.4 slice_bitcast_fusion
  431.0 1.3 slice_reduce_fusion
  432.3 0.0 copy-start.2
  432.3 0.0 copy-start.1
  432.3 4.5 %convert_element_type.23 = f32[3,96,4096]{2,1,0:T(8,128)} convert(bf16[3,96,4096]{2,1,0:T(8,128)(2,1)} %get-tuple-element.16) | non-fusion elementwise | flops 1179648 | bytes 7077888 | tf_op jit(solution)/shard_map/convert_element_type | solution.py:1017
  436.8 0.0 copy-start
  436.8 0.0 copy-done.2
  436.8 1.1 convert_element_type.24
  437.9 0.0 copy-done.1
  437.9 1.1 convert_element_type.25
  439.0 0.0 copy-done
  439.0 1.4 copy.26
  (2 shorter events, 0.0 us)
Async XLA Ops:
  432.3 4.5 %copy-start.2 = (bf16[384,768]{1,0:T(8,128)(2,1)S(1)}, bf16[384,768]{1,0:T(8,128)(2,1)}, u32[]{:S(2)}) copy-start(bf16[384,768]{1,0:T(8,128)(2,1)} %get-tuple-element.17) | copy-start | bytes 1769476
  432.3 5.6 %copy-start.1 = (bf16[384,768]{1,0:T(8,128)(2,1)S(1)}, bf16[384,768]{1,0:T(8,128)(2,1)}, u32[]{:S(2)}) copy-start(bf16[384,768]{1,0:T(8,128)(2,1)} %get-tuple-element.19) | copy-start | bytes 1769476
  436.8 2.2 copy-start

commit v4 on v3

--- a/solution.py
+++ b/solution.py
@@ -16,22 +16,21 @@
 
 def token_tables(length, group):
     half = length // (2 * group)
-    n = np.arange(length, dtype=np.int64)
-
-    def wave(k):
+
+    def wave(n, k):
         angle = (n[:, None] * k[None, :] % length) * (2.0 * math.pi / length)
         return np.cos(angle), np.sin(angle)
 
-    cos, sin = wave(np.arange(length // 2))
-    main = np.stack(
-        [cos.reshape(length, group, half), sin.reshape(length, group, half)], axis=2
-    ).reshape(length, group, 2 * half)
-    main = main.transpose(1, 0, 2).reshape(group * length, 2 * half)
-    edge_cos, edge_sin = wave(half * (np.arange(group) + 1))
-    edge = np.zeros((length, 128))
-    edge[:, 0 : 2 * group : 2] = edge_cos
-    edge[:, 1 : 2 * group : 2] = np.where(np.abs(edge_sin) < 1e-9, 0.0, edge_sin)
-    return main.astype(BF), edge.astype(BF)
+    n = np.arange(length, dtype=np.int64)
+    k = np.arange(length // 2).reshape(group, half)
+    columns = np.stack([k[:, 0::2], k[:, 1::2]], axis=1)
+    cos, sin = wave(n[: length // 2], columns.reshape(-1))
+    shape = (length // 2, group, 2, 1, half // 2)
+    main = np.concatenate([cos.reshape(shape), sin.reshape(shape)], axis=3)
+    main = main.reshape(length // 2, group, 2 * half).transpose(1, 0, 2).reshape(-1, 2 * half)
+    edge_cos, edge_sin = wave(half * (np.arange(group) + 1), n)
+    edge = np.stack([edge_cos, np.where(np.abs(edge_sin) < 1e-9, 0.0, edge_sin)], axis=1)
+    return main.astype(BF), edge.reshape(2 * group, length).astype(BF)
 
 
 def hidden_tables(width):
@@ -57,6 +56,13 @@
 
     def dp_of(self, z):
         return (z % 2) * (self.n_dp // 2) + z // 2
+
+    def z_of(self, j):
+        return ((self.dp % 2) * (self.n_dp // 2) + self.dp // 2) ^ j
+
+    def dp_from(self, j):
+        v = self.z ^ j
+        return (v % (self.n_dp // 2)) * 2 + v // (self.n_dp // 2)
 
     def peer(self, offset):
         g = self.g ^ offset
@@ -94,11 +100,13 @@
         + [jnp.zeros((wide,), F32)]
     )
 
+    n_slots = 4
+
     def layer_body(
         x_ref, c_ref, win_ref, wout_ref, cos_ref, sin_ref, table_ref, edge_ref, rows_ref,
         act_o, gu_o, ge_o, gf_o, gw_o, gin_o, gout_o, vec_o,
-        win, wout, cos, sin, xb, ub, eb, cb, ab, a_all, m_all, nl, gl, f, tile, edge_v,
-        bacc, vacc, b_in_v, vec, vrows, drows, grows, drows2, spare,
+        win, wout, cos, sin, xb, ub, eb, cb, ab, a_all, m_all, nl, gl, f, tile, edge_v, slots,
+        perm, e_send, bacc, vacc, b_in_v, vec, vrows, drows, grows, drows2, spare,
         load, slice_send, slice_recv, tok_send, tok_recv, vec_send, vec_recv, gather_send, gather_recv,
         cot_send, cot_own, cot_recv, act_send, act_own, act_recv, col_send, col_recv,
         ready, rs_send, rs_recv, table_sem, home_send, home_recv, more_send, more_recv, more_free,
@@ -106,36 +114,14 @@
     ):
         at = Place(n_dp, n_tensor)
         barrier = pltpu.get_barrier_semaphore()
-        count = 0
-        for j in range(seqs):
-            src_dp = (at.z - j + at.n_dp) % at.n_dp
-            for b in range(n_tensor):
-                mine_ = jnp.logical_and(src_dp == at.dp, at.tensor == b)
-
-                @pl.when(jnp.logical_not(mine_))
-                def _():
-                    pl.semaphore_signal(barrier, inc=1, device_id=(src_dp, b), device_id_type=MESH)
-
-                count = count + jnp.where(mine_, 0, 1)
-        for j in range(seqs):
-            z = (at.dp + j) % at.slices
-            for g_ in range(group):
-                mine_ = jnp.logical_and(z == at.z, at.g == g_)
-
-                @pl.when(jnp.logical_not(mine_))
-                def _():
-                    pl.semaphore_signal(barrier, inc=1, device_id=(g_ // 2, z * 2 + g_ % 2), device_id_type=MESH)
-
-                count = count + jnp.where(mine_, 0, 1)
-        for offset in range(1, group):
-            device, _ = at.peer(offset)
-            pl.semaphore_signal(barrier, inc=1, device_id=device, device_id_type=MESH)
-            count = count + 1
-        for offset in range(1, n_tensor):
+        others = n_dp * n_tensor - 1
+        def greet(i, c):
+            k = (at.dp * n_tensor + at.tensor + i) % (others + 1)
             pl.semaphore_signal(
-                barrier, inc=1, device_id=(at.dp, at.tensor ^ offset), device_id_type=MESH)
-            count = count + 1
-        pl.semaphore_wait(barrier, count)
+                barrier, inc=1, device_id=(k // n_tensor, k % n_tensor), device_id_type=MESH)
+            return c
+        lax.fori_loop(1, others + 1, greet, 0)
+        pl.semaphore_wait(barrier, others)
 
         def wait(ref, sem):
             pltpu.make_async_copy(ref, ref, sem).wait()
@@ -152,7 +138,7 @@
         rows_of = lambda b: pl.ds(pl.multiple_of(b * columns, 16), columns)
 
         def cot_start(j):
-            z = (at.dp + j) % at.slices
+            z = at.z_of(j)
             for offset in range(group):
                 g = at.g ^ offset
                 for p in range(2):
@@ -171,7 +157,7 @@
                             pltpu.make_async_remote_copy(src, dst, cot_own.at[j], cot_recv.at[j], device, MESH).start()
 
         def cot_finish(j):
-            z = (at.dp + j) % at.slices
+            z = at.z_of(j)
             wait(c_ref.at[j, :, pl.ds(0, length - 2 * half)], cot_send.at[j])
 
             @pl.when(z != at.z)
@@ -179,7 +165,7 @@
                 wait(c_ref.at[j, :, pl.ds(0, 2 * half)], cot_own.at[j])
 
         def act_start(j):
-            dp = (at.z - j + at.n_dp) % at.n_dp
+            dp = at.dp_from(j)
             for offset in range(n_tensor):
                 b = at.tensor ^ offset
                 for p in range(2):
@@ -196,8 +182,8 @@
                         def _():
                             pltpu.make_async_remote_copy(src, dst, act_own.at[j], act_recv.at[j], (dp, b), MESH).start()
 
-        def act_finish(j):
-            dp = (at.z - j + at.n_dp) % at.n_dp
+        def act_sent(j):
+            dp = at.dp_from(j)
             wait(ab.at[j, pl.ds(0, width - columns)], act_send.at[j])
 
             @pl.when(dp != at.dp)
@@ -212,7 +198,7 @@
                 rows = rows_of(at.block_of(g_ // 2, g_ % 2))
                 for i, (src, dst) in enumerate((
                     (ub.at[j, rows], gu_o.at[at.g, pl.ds(j * columns, columns)]),
-                    (eb.at[j, rows], ge_o.at[at.g, pl.ds(j * columns, columns)]),
+                    (eb.at[j, pl.ds(pl.multiple_of(at.block_of(g_ // 2, g_ % 2) * er, 16), er)], ge_o.at[at.g, pl.ds(j * er, er)]),
                     (xb.at[j, rows, parts[0]], gf_o.at[j, :, lanes(at.g)[0]]),
                     (xb.at[j, rows, parts[1]], gf_o.at[j, :, lanes(at.g)[1]]),
                 )):
@@ -226,19 +212,19 @@
         def col_finish(j):
             rest = pl.ds(0, width - columns)
             wait(ub.at[j, rest], col_send.at[j, 0])
-            wait(eb.at[j, rest], col_send.at[j, 1])
+            wait(eb.at[j, pl.ds(0, (n_tensor - 1) * er)], col_send.at[j, 1])
             wait(xb.at[j, rest], col_send.at[j, 2])
 
         def col_arrived(j):
             wait(gu_o.at[:, pl.ds(j * columns, columns)], col_recv.at[j, 0])
-            wait(ge_o.at[:, pl.ds(j * columns, columns)], col_recv.at[j, 1])
+            wait(ge_o.at[:, pl.ds(j * er, er)], col_recv.at[j, 1])
             wait(gf_o.at[j], col_recv.at[j, 2])
 
         two = own(2)
         n_pieces = length // tokens
 
         def slice_at(j):
-            z = (at.dp + j) % at.slices
+            z = at.z_of(j)
             dp = at.dp_of(at.z)
             return (dp, z * 2 + at.y), jnp.logical_and(dp == at.dp, z == at.z)
 
@@ -263,20 +249,20 @@
             def _():
                 wait(x_ref.at[j], slice_send.at[j])
 
-        depth = min(1024, length // 2)
-        n_chunks = length // depth
+        n_chunks = length // 2 // depth
         per = depth // tokens
-        def front_slot(i):
-            ref = (a_all, m_all)[i % 2]
-            return ref.at[pl.ds(i // 2 * depth, depth), own(1)]
+        er = 2 * group
+        edge_rows = lambda b: pl.ds(pl.multiple_of(b * er, 16), er)
+        def slot_at(i):
+            return slots.at[pl.ds(i % n_slots * depth, depth)]
 
         def table_rows(c, g):
-            return table_ref.at[pl.ds(pl.multiple_of(g * length + c * depth, 16), depth)]
+            return table_ref.at[pl.ds(pl.multiple_of(g * (length // 2) + c * depth, 16), depth)]
 
         order = [(offset, c) for offset in reversed(range(group)) for c in range(n_chunks)]
         def front_load(i):
             offset, c = order[i]
-            return pltpu.make_async_copy(table_rows(c, at.g ^ offset), front_slot(i % 6), table_sem.at[i % 6])
+            return pltpu.make_async_copy(table_rows(c, at.g ^ offset), slot_at(i), table_sem.at[i % n_slots])
 
         def to_tokens(js, offset, kinds):
             device, g = at.peer(offset)
@@ -286,7 +272,7 @@
                 if "u" in kinds:
                     moves.append((m_all.at[pl.ds(j * width + offset * columns, columns), two], ub.at[j, rows], 0))
                 if "e" in kinds:
-                    moves.append((m_all.at[pl.ds(seqs * width + j * columns, columns), pl.ds(2 * tokens, 128)], eb.at[j, rows], 1))
+                    moves.append((e_send.at[pl.ds(j * er, er)], eb.at[j, edge_rows(at.block)], 1))
                 if "x" in kinds:
                     for p, i in ((0, g), (1, 2 * group - 1 - g)):
                         moves.append((
@@ -301,36 +287,50 @@
                         pltpu.make_async_copy(src, dst, tok_recv.at[j, kind]).start()
 
         def front_prefetch():
-            for i in range(6):
+            for i in range(n_slots):
                 front_load(i).start()
 
-        def front_pass(js):
+        def front_pass(js, first):
             m = len(js) * columns
-            def piece(k):
-                vals = [a_all[j * width + k * columns : j * width + (k + 1) * columns, 2 * tokens : 3 * tokens] for j in js]
-                return vals[0] if len(vals) == 1 else jnp.concatenate(vals, axis=0)
             for offset in range(1, group):
-                to_tokens(js, offset, "x")
-            edge = jnp.zeros((m, 128), F32)
-            for k in range(n_pieces):
-                edge = edge + dot(piece(k), edge_v[k * tokens : (k + 1) * tokens, :], 1, 0)
+                to_tokens(js[:first], offset, "x")
             for i, j in enumerate(js):
-                m_all[seqs * width + j * columns : seqs * width + (j + 1) * columns, 2 * tokens : 2 * tokens + 128] = (
-                    edge[i * columns : (i + 1) * columns].astype(BF))
+                edge = jnp.zeros((er, columns), F32)
+                for k in range(n_pieces // 2):
+                    k2 = k + n_pieces // 2
+                    low = a_all[j * width + k * columns : j * width + (k + 1) * columns, 2 * tokens : 3 * tokens]
+                    high = a_all[j * width + k2 * columns : j * width + (k2 + 1) * columns, 2 * tokens : 3 * tokens]
+                    edge = edge + dot(edge_v[:, k * tokens : (k + 1) * tokens], low, 1, 1)
+                    edge = edge + dot(edge_v[:, k2 * tokens : (k2 + 1) * tokens], high, 1, 1)
+                    low, high = low.astype(F32), high.astype(F32)
+                    rows = pl.ds(k * m + i * columns, columns)
+                    nl[rows, two] = (low + high).astype(BF)
+                    gl[rows, two] = (low - high).astype(BF)
+                e_send[j * er : (j + 1) * er, 0:columns] = edge.astype(BF)
             for n, (offset, c) in enumerate(order):
                 if c == 0:
-                    total = jnp.zeros((m, tokens), F32)
+                    even = jnp.zeros((m, half), F32)
+                    odd = jnp.zeros((m, half), F32)
                 front_load(n).wait()
-                slot = front_slot(n % 6)
+                slot = slot_at(n)
                 for s_ in range(per):
-                    total = total + dot(piece(c * per + s_), slot[pl.ds(s_ * tokens, tokens), :], 1, 0)
-                if n + 6 < len(order):
-                    front_load(n + 6).start()
+                    k = c * per + s_
+                    rows = pl.ds(s_ * tokens, tokens)
+                    even = even + dot(nl[k * m : (k + 1) * m, two], slot[rows, A], 1, 0)
+                    odd = odd + dot(gl[k * m : (k + 1) * m, two], slot[rows, B], 1, 0)
+                if n + n_slots < len(order):
+                    front_load(n + n_slots).start()
                 if c == n_chunks - 1:
                     for i, j in enumerate(js):
-                        m_all[j * width + offset * columns : j * width + (offset + 1) * columns, 2 * tokens : 3 * tokens] = (
-                            total[i * columns : (i + 1) * columns].astype(BF))
-                    to_tokens(js, offset, "ue" if offset else "uex")
+                        rows = pl.ds(j * width + offset * columns, columns)
+                        mine = slice(i * columns, (i + 1) * columns)
+                        m_all[rows, 2 * tokens : 2 * tokens + half] = even[mine].astype(BF)
+                        m_all[rows, 2 * tokens + half : 3 * tokens] = odd[mine].astype(BF)
+                    to_tokens(js[:first], offset, "ue" if offset else "uex")
+
+        def later_tokens(j):
+            for offset in reversed(range(group)):
+                to_tokens([j], offset, "uex")
 
         def tokens_arrived(j):
             wait(ub.at[j], tok_recv.at[j, 0])
@@ -340,7 +340,7 @@
         def tokens_sent(j):
             rest = pl.ds(0, width - columns)
             wait(ub.at[j, rest], tok_send.at[j, 0])
-            wait(eb.at[j, rest], tok_send.at[j, 1])
+            wait(eb.at[j, pl.ds(0, (n_tensor - 1) * er)], tok_send.at[j, 1])
             wait(xb.at[j, rest], tok_send.at[j, 2])
 
         bt = units // n_tensor
@@ -365,14 +365,16 @@
         def arrive(level, arr, rows, key):
             wait(w_bufs[arr].at[rows], gather_recv.at[level, arr, key])
 
-        def gather_start():
+        def gather_one():
             mine = pl.ds(pl.multiple_of(core * hb + x * qb, 16), qb)
-            half_rows = pl.ds(pl.multiple_of(core * hb, 16), hb)
             for arr in range(2):
                 for o in range(1, slices):
                     pltpu.make_async_remote_copy(
                         w_refs[arr].at[mine], w_bufs[arr].at[piece_rows(0, at.y, 1, x)],
                         gather_send.at[0, arr], gather_recv.at[0, arr, o - 1], z_peer(o), MESH).start()
+
+        def gather_start():
+            half_rows = pl.ds(pl.multiple_of(core * hb, 16), hb)
             for arr in range(2):
                 pltpu.make_async_remote_copy(
                     w_refs[arr].at[half_rows], w_bufs[arr].at[piece_rows(0, at.y, 2, 0)],
@@ -448,13 +450,22 @@
                 b_in_v[t * bt : (t + 1) * bt, :] = turned[0:bt, 8 * t : 8 * t + 1]
                 vec[t * columns : (t + 1) * columns, :] = turned[0:columns, 8 * t + 1 : 8 * t + 6]
 
-        lane0 = lax.broadcasted_iota(jnp.int32, (half, half), 0)
-        lane1 = lax.broadcasted_iota(jnp.int32, (half, half), 1)
-        turn = jnp.where(lane0 + lane1 == half, 1.0, 0.0).astype(BF)
-        edge0 = lax.broadcasted_iota(jnp.int32, (128, half), 0)
-        edge1 = lax.broadcasted_iota(jnp.int32, (128, half), 1)
-        pick_u = jnp.where((edge0 == 2 * at.g) & (edge1 == 0), 1.0, 0.0).astype(BF)
-        pick_v = jnp.where((edge0 == 2 * at.g + 1) & (edge1 == 0), 1.0, 0.0).astype(BF)
+        place0 = lax.broadcasted_iota(jnp.int32, (tokens, half), 0)
+        k1 = lax.broadcasted_iota(jnp.int32, (tokens, half), 1)
+        place = lambda k, shift: k // 2 + k % 2 * half + shift * (half // 2)
+        one_hot = lambda hit: jnp.where(hit, 1.0, 0.0).astype(BF)
+        for shift in range(2):
+            perm[:, shift * half : (shift + 1) * half] = one_hot(place0 == place(k1, shift))
+            perm[:, (2 + shift) * half : (3 + shift) * half] = one_hot(
+                (place0 == place(half - k1, shift)) & (k1 > 0))
+        turn0 = lax.broadcasted_iota(jnp.int32, (half, half), 0)
+        turn1 = lax.broadcasted_iota(jnp.int32, (half, half), 1)
+        turn = one_hot(turn0 + turn1 == half)
+        edge0 = lax.broadcasted_iota(jnp.int32, (2 * group, half), 0)
+        edge1 = lax.broadcasted_iota(jnp.int32, (2 * group, half), 1)
+        pick_u = one_hot((edge0 == 2 * at.g) & (edge1 == 0))
+        pick_v = one_hot((edge0 == 2 * at.g + 1) & (edge1 == 0))
+        e_send[...] = jnp.zeros_like(e_send)
         A, B = parts
         block = 256
         step = 32
@@ -490,12 +501,13 @@
 
         def forward_mix(j):
             tokens_arrived(j)
-            def turned(r, c):
-                e = eb[j, r, :]
-                tile[r, A] = (dot(ub[j, r, A], turn, 1, 0) + dot(e, pick_u, 1, 0)).astype(BF)
-                tile[r, B] = (dot(ub[j, r, B], turn, 1, 0) + dot(e, pick_v, 1, 0)).astype(BF)
-                return c
-            over(width, block, turned, 0, unroll=1)
+            for b in range(n_tensor):
+                r = pl.ds(b * columns, columns)
+                e = eb[j, b * er : (b + 1) * er, 0:columns]
+                all_four = dot(ub[j, r, :], perm[...], 1, 0)
+                ub[j, r, :] = all_four[:, : 2 * half].astype(BF)
+                tile[r, A] = (all_four[:, 2 * half : 3 * half] + dot(e, pick_u, 0, 0)).astype(BF)
+                tile[r, B] = (all_four[:, 3 * half :] + dot(e, pick_v, 0, 0)).astype(BF)
             def mixed(r, c):
                 f1[r, A] = xb[j, r, A].astype(F32) + mix_scale * (
                     dot(cos[r, :], ub[j, :, A], 1, 0) - dot(sin[r, :], ub[j, :, B], 1, 0))
@@ -535,7 +547,7 @@
 
         def second_norm(j):
             center, inverse = statistics(f2)
-            flag = drows[pl.ds(pl.multiple_of((at.z - j + at.n_dp) % at.n_dp * 8, 8), 8), 0:128][6:7, j : j + 1]
+            flag = drows[pl.ds(pl.multiple_of(at.dp_from(j) * 8, 8), 8), 0:128][6:7, j : j + 1]
             def result(r, c):
                 h = (f2[r, :] - center) * inverse
                 f2[r, :] = h
@@ -599,21 +611,21 @@
                 t = dot(b, turn, 1, 0)
                 ub[j, r, A] = (t + a).astype(BF)
                 ub[j, r, B] = (t - a).astype(BF)
-                eb[j, r, :] = dot(b, pick_u + pick_v, 1, 1).astype(BF)
                 return c
             over(width, block, fold_pairs, 0, unroll=1)
-            even, odd, edge = ub[j, :, A], ub[j, :, B], eb[j]
-            is_cos = lax.broadcasted_iota(jnp.int32, (block, 128), 1) % 2 == 0
+            edge = dot(pick_u + pick_v, tile[:, B], 1, 1).astype(BF)
+            is_cos = lax.broadcasted_iota(jnp.int32, (er, columns), 0) % 2 == 0
+            for b in range(n_tensor):
+                r = pl.ds(b * columns, columns)
+                eb[j, b * er : (b + 1) * er, 0:columns] = jnp.where(
+                    is_cos, dot(edge, cos[r, :], 1, 1), dot(edge, sin[r, :], 1, 1)).astype(BF)
             for k in range(width // block):
                 r = pl.ds(k * block, block)
-                f1[r, A] = dot(cos[r, :], even, 1, 0)
-                f1[r, B] = dot(sin[r, :], odd, 1, 0)
-                f2[r, 0:128] = jnp.where(is_cos, dot(cos[r, :], edge, 1, 0), dot(sin[r, :], edge, 1, 0))
-            def pack(r, c):
-                ub[j, r, :] = f1[r, :].astype(BF)
-                eb[j, r, :] = f2[r, 0:128].astype(BF)
-                return c
-            over(width, step, pack, 0)
+                tile[r, A] = dot(cos[r, :], ub[j, :, A], 1, 0).astype(BF)
+                tile[r, B] = dot(sin[r, :], ub[j, :, B], 1, 0).astype(BF)
+            for k in range(width // block):
+                r = pl.ds(k * block, block)
+                ub[j, r, :] = dot(tile[r, :], perm[:, : 2 * half], 1, 1).astype(BF)
             for move in col_moves(j):
                 move.start()
 
@@ -648,6 +660,9 @@
                                        + [flip(1 << b) for b in range(2, n_dp.bit_length() - 1)]):
                 pl.semaphore_signal(ready.at[i], inc=1, device_id=device, device_id_type=MESH)
 
+        def ready_wait(i):
+            pl.semaphore_wait(ready.at[i], 1)
+
         def weight_grads(arr, left, right):
             def tile_step(k, c):
                 r = pl.ds(pl.multiple_of(block_at(k) * bt, 16), bt)
@@ -674,30 +689,19 @@
         def after1(arr):
             def go(k, c):
                 add(arr, rows_half(k, core), land1(arr, k), 0, k)
-                if arr == 0:
-                    @pl.when(k < slices)
-                    def _():
-                        send(grads[arr].at[rows_half(k, core)], land2(arr, k, hb), 1, arr, k, y_peer)
-                else:
-                    send(grads[arr].at[rows_quarter(k, 1 - x)], land2(arr, k, qb), 1, arr, k, x_peer)
+
+                @pl.when(k < slices)
+                def _():
+                    send(grads[arr].at[rows_half(k, core)], land2(arr, k, hb), 1, arr, k, y_peer)
                 return c
             lax.fori_loop(0, n_tensor, go, 0)
 
         def after2(arr):
-            if arr == 0:
-                def go(k, c):
-                    add(arr, rows_half(slices + k, core), land2(arr, k, hb), 1, k)
-                    send(grads[arr].at[rows_quarter(slices + k, 1 - x)], land3(arr, k), 2, arr, k, x_peer)
-                    return c
-                lax.fori_loop(0, slices, go, 0)
-            else:
-                def go(k, c):
-                    add(arr, rows_quarter(k, x), land2(arr, k, qb), 1, k)
-                    @pl.when(k < slices)
-                    def _():
-                        send(grads[arr].at[rows_quarter(k, x)], land3(arr, k), 2, arr, k, y_peer)
-                    return c
-                lax.fori_loop(0, n_tensor, go, 0)
+            def go(k, c):
+                add(arr, rows_half(slices + k, core), land2(arr, k, hb), 1, k)
+                send(grads[arr].at[rows_quarter(slices + k, 1 - x)], land3(arr, k), 2, arr, k, x_peer)
+                return c
+            lax.fori_loop(0, slices, go, 0)
 
         def after3(arr):
             for offset in range(slices):
@@ -725,9 +729,15 @@
             home = pl.ds(pl.multiple_of(core * hb + x * qb, 16), qb)
             out = (gout_o, gin_o)[arr]
             pltpu.make_async_copy(grads[arr].at[mine], out.at[home], rs_recv.at[4, arr, 0]).start()
-            for q in range(1, 4):
+            for q in range(1, 3):
                 pltpu.make_async_remote_copy(
                     grads[arr].at[mine], out.at[home], rs_send.at[4, arr], rs_recv.at[4, arr, q], flip(q), MESH).start()
+
+        def after5(arr):
+            out = (gout_o, gin_o)[arr]
+            came = out.at[pl.ds(pl.multiple_of(core * hb + (1 - x) * qb, 16), qb)]
+            wait(came, rs_recv.at[4, arr, 2])
+            pltpu.make_async_remote_copy(came, came, rs_send.at[4, arr], rs_recv.at[4, arr, 3], core_peer, MESH).start()
 
         def rs_finish(arr):
             g = grads[arr]
@@ -737,67 +747,82 @@
             wait(g.at[pl.ds(0, slices * qb)], rs_send.at[2, arr])
             wait(g.at[pl.ds(0, (slices - 1) * qb)], rs_send.at[3, arr])
             wait(g.at[pl.ds(0, 3 * qb)], rs_send.at[4, arr])
-            for q in range(4):
+            for q in (0, 1, 3):
                 wait((gout_o, gin_o)[arr].at[pl.ds(0, qb)], rs_recv.at[4, arr, q])
 
-        every = seqs * columns
-        n_slots = 6
-        slot_ref = lambda i: m_all.at[pl.ds(i // 2 * depth, depth), pl.ds((1 + i % 2) * tokens, tokens)]
         def table_start(i):
             c, g = i // group, i % group
-            rows = pl.ds(g * length + c * depth, depth)
-            return pltpu.make_async_copy(table_ref.at[rows], slot_ref(i % n_slots), table_sem.at[i % n_slots])
-
-        def words_back():
-            steps = [(c, g) for c in range(n_chunks) for g in range(group)]
+            return pltpu.make_async_copy(table_rows(c, g), slot_at(i), table_sem.at[i % n_slots])
+
+        def back_prefetch():
             for i in range(n_slots):
                 table_start(i).start()
-            for j in range(seqs):
+
+        def words_back(js, acc):
+            m = len(js) * columns
+            base = js[0] * width
+            n_edge = len(js) * er
+            some = pl.ds(js[0] * columns, m)
+            some_edges = pl.ds(js[0] * er, n_edge)
+            for j in js:
                 col_arrived(j)
+                act_sent(j)
             for g in range(group):
-                pltpu.make_async_copy(gu_o.at[g], cb.at[pl.ds(g * every, every)], table_sem.at[n_slots + 1]).start()
-            for g in range(group):
-                pltpu.make_async_copy(ge_o.at[g], m_all.at[pl.ds(g * every, every), pl.ds(0, 128)], table_sem.at[n_slots + 2]).start()
-            for j in range(seqs):
-                for k in range(length // tokens):
+                pltpu.make_async_copy(gu_o.at[g, some], cb.at[pl.ds(base + g * m, m)], table_sem.at[n_slots]).start()
+                pltpu.make_async_copy(
+                    ge_o.at[g, some_edges], tile.at[pl.ds(g * n_edge, n_edge), pl.ds(0, 128)],
+                    table_sem.at[n_slots + 1]).start()
+            for j in js:
+                for k in range(n_pieces):
                     pltpu.make_async_copy(
-                        gf_o.at[j, :, pl.ds(k * tokens, tokens)], nl.at[pl.ds(k * columns, columns), own(j)],
-                        table_sem.at[n_slots + 3]).start()
-            wait(cb, table_sem.at[n_slots + 1])
-            wait(m_all.at[pl.ds(0, group * every), pl.ds(0, 128)], table_sem.at[n_slots + 2])
-            wait(nl, table_sem.at[n_slots + 3])
-            edge = m_all[0:every, 0:128].astype(F32)
+                        gf_o.at[j, :, pl.ds(k * tokens, tokens)], ab.at[j, pl.ds(k * columns, columns)],
+                        table_sem.at[n_slots + 2]).start()
+            wait(cb.at[pl.ds(base, group * m)], table_sem.at[n_slots])
+            wait(tile.at[pl.ds(0, group * n_edge), pl.ds(0, 128)], table_sem.at[n_slots + 1])
+            for j in js:
+                wait(ab.at[j], table_sem.at[n_slots + 2])
+            edges = tile[0:n_edge, 0:128].astype(F32)
             for g in range(1, group):
-                edge = edge + m_all[g * every : (g + 1) * every, 0:128].astype(F32)
-            edge = edge.astype(BF)
+                edges = edges + tile[g * n_edge : (g + 1) * n_edge, 0:128].astype(F32)
+            edges = edges.astype(BF)
             for c in range(n_chunks):
-                for s_ in range(per):
-                    k = c * per + s_
-                    acc = pl.ds(k * every, every)
-                    f[acc, :] = dot(edge, edge_v[k * tokens : (k + 1) * tokens, :], 1, 1)
                 for g in range(group):
                     i = c * group + g
                     table_start(i).wait()
                     for s_ in range(per):
-                        acc = pl.ds((c * per + s_) * every, every)
-                        f[acc, :] += dot(cb[pl.ds(g * every, every), :], slot_ref(i % n_slots)[pl.ds(s_ * tokens, tokens), :], 1, 1)
+                        t = slot_at(i)[pl.ds(s_ * tokens, tokens), :]
+                        left = cb[base + g * m : base + (g + 1) * m, :]
+                        even = dot(left[:, :half], t[:, :half], 1, 1)
+                        odd = dot(left[:, half:], t[:, half:], 1, 1)
+                        at_even = pl.ds(s_ * m, m)
+                        at_odd = pl.ds((per + s_) * m, m)
+                        if g:
+                            acc[at_even, :] += even
+                            acc[at_odd, :] += odd
+                        else:
+                            acc[at_even, :] = even
+                            acc[at_odd, :] = odd
                     if i + n_slots < n_chunks * group:
                         table_start(i + n_slots).start()
                 for s_ in range(per):
-                    k = c * per + s_
-                    for j in range(seqs):
-                        rows = pl.ds(k * columns, columns)
-                        gl[rows, own(j)] = (
-                            f[pl.ds(k * every + j * columns, columns), :] + nl[rows, own(j)].astype(F32)).astype(BF)
-                        home_start(j, k)
+                    for sign in range(2):
+                        k = c * per + s_ + sign * (n_pieces // 2)
+                        for n, j in enumerate(js):
+                            rows = pl.ds(k * columns, columns)
+                            even = acc[pl.ds(s_ * m + n * columns, columns), :]
+                            odd = acc[pl.ds((per + s_) * m + n * columns, columns), :]
+                            edge = dot(edges[n * er : (n + 1) * er, 0:columns], edge_v[:, k * tokens : (k + 1) * tokens], 0, 0)
+                            both = even - odd if sign else even + odd
+                            ab[j, rows, :] = (both + edge + ab[j, rows, :].astype(F32)).astype(BF)
+                            home_start(j, k)
 
         def home_at(j):
-            dp = (at.z - j + at.n_dp) % at.n_dp
+            dp = at.dp_from(j)
             return dp, jnp.logical_and(dp == at.dp, at.block == at.tensor)
 
         def home_start(j, k):
             dp, here = home_at(j)
-            src = gl.at[pl.ds(k * columns, columns), own(j)]
+            src = ab.at[j, pl.ds(k * columns, columns)]
             dst = gw_o.at[j, :, pl.ds(k * tokens, tokens)]
 
             @pl.when(here)
@@ -862,81 +887,99 @@
             pltpu.make_async_copy(src, dst, load.at[2 + i])
             for i, (src, dst) in enumerate(((edge_ref, edge_v), (cos_ref, cos), (sin_ref, sin)))
         ]
-        slice_start(0)
+        gather_one()
+        gather_start()
         vectors_start()
-        gather_start()
         for move in tables:
             move.start()
         front_prefetch()
-        wait(a_all.at[pl.ds(0, width), two], slice_recv.at[0])
-        for j in range(1, seqs):
-            slice_start(j)
-        tables[0].wait()
-        front_pass([0])
-        front_prefetch()
         gather_two()
-        for j in range(seqs):
-            cot_start(j)
+        slice_start(0)
         gather_three()
         tables[1].wait()
         tables[2].wait()
         vectors_arrived()
+        tables[0].wait()
+        wait(a_all.at[pl.ds(0, width), two], slice_recv.at[0])
+        front_pass([0], 1)
+        front_prefetch()
+        slice_start(1)
+        for arr in range(2):
+            gather_four(arr)
+        for j in range(2, seqs):
+            slice_start(j)
+        inverse = forward_mix(0)
+        cot_start(0)
+        for arr in range(2):
+            gather_last(arr)
+        last = seqs - 1
         for j in range(seqs):
-            if j == 0:
-                inverse = forward_mix(0)
-                for arr in range(2):
-                    gather_four(arr)
-                for arr in range(2):
-                    gather_last(arr)
-            else:
+            if j:
                 inverse = forward_mix(j)
-            if j == 2:
+            if j == last:
                 for i in range(seqs):
                     tokens_sent(i)
+                back_prefetch()
             forward_mlp(j)
             if j == 0:
-                for i in range(1, seqs):
-                    wait(a_all.at[pl.ds(i * width, width), two], slice_recv.at[i])
-                front_pass(list(range(1, seqs)))
+                wait(a_all.at[pl.ds(width, width), two], slice_recv.at[1])
+                front_pass([1], 1)
+                front_prefetch()
+            if j + 1 < seqs:
+                cot_start(j + 1)
+            if j == last:
+                words_back([0], f3)
+                back_prefetch()
             second_norm(j)
             backward_inner(j)
-            if j == seqs - 1:
+            if j == last:
                 gather_sent()
                 weight_grads(0, a_all, gl)
                 ready_signal()
-                pl.semaphore_wait(ready.at[0], 1)
+                ready_wait(0)
                 level1(0)
             backward_outer(j)
-            if j == seqs - 1:
-                weight_grads(1, m_all, nl)
-                level1(1)
             first_back(j, inverse)
+            if j + 2 < seqs:
+                i = j + 2
+                wait(a_all.at[pl.ds(i * width, width), two], slice_recv.at[i])
+                front_pass([i], 1)
+        ready_wait(2)
+        after1(0)
+        weight_grads(1, m_all, nl)
+        level1(1)
         vector_grads()
-        for i in range(1, 3 + slices - 1 + max(0, n_dp.bit_length() - 3)):
-            pl.semaphore_wait(ready.at[i], 1)
-        after1(0)
         after1(1)
+        for j in range(1, last):
+            words_back([j], f2)
+            back_prefetch()
+        words_back([last], f2)
+        ready_wait(1)
+        after2(0)
+        for i in range(3, 3 + slices - 1 + max(0, n_dp.bit_length() - 3)):
+            ready_wait(i)
+        after3(0)
+        after2(1)
+        after3(1)
         vector_grads_two()
-        words_back()
-        after2(0)
-        after2(1)
-        after3(0)
-        after3(1)
         after4(0)
         after4(1)
+        vector_grads_three()
+        after5(0)
+        after5(1)
         for j in range(seqs):
             slice_finish(j)
             cot_finish(j)
-            act_finish(j)
             col_finish(j)
             home_finish(j)
-        vector_grads_three()
         rs_finish(0)
         rs_finish(1)
+
 
     shape = jax.ShapeDtypeStruct
     dma = pltpu.SemaphoreType.DMA
     whole_vmem = pl.BlockSpec(memory_space=pltpu.VMEM)
+    depth = min(1024, length // 2)
     need_spare = seqs * tokens < 2 * width
     regular = pltpu.SemaphoreType.REGULAR
     activations, _, _, _, gw, g_in, g_out, vec_g = pl.pallas_call(
@@ -944,7 +987,7 @@
         out_shape=[
             shape(words.shape, BF),
             shape((group, seqs * columns, tokens), BF),
-            shape((group, seqs * columns, 128), BF),
+            shape((group, seqs * 2 * group, 128), BF),
             shape((seqs, columns, length), BF),
             shape((seqs, columns, length), BF),
             shape(w_in.shape, BF),
@@ -960,7 +1003,7 @@
             pltpu.VMEM((width, width), BF),
             pltpu.VMEM((seqs, width, tokens), BF),
             pltpu.VMEM((seqs, width, tokens), BF),
-            pltpu.VMEM((seqs, width, 128), BF),
+            pltpu.VMEM((seqs, n_tensor * 2 * group, 128), BF),
             pltpu.VMEM((group * seqs * columns, tokens), BF),
             pltpu.VMEM((seqs, width, tokens), BF),
             pltpu.VMEM((units, seqs * tokens), BF),
@@ -969,7 +1012,10 @@
             pltpu.VMEM((width, seqs * tokens), BF),
             pltpu.VMEM((3 * width, tokens), F32),
             pltpu.VMEM((width, tokens), BF),
-            pltpu.VMEM((length, 128), BF),
+            pltpu.VMEM((2 * group, length), BF),
+            pltpu.VMEM((n_slots * depth, tokens), BF),
+            pltpu.VMEM((tokens, 4 * half), BF),
+            pltpu.VMEM((seqs * 2 * group, 128), BF),
             pltpu.VMEM((units, 128), F32),
             pltpu.VMEM((5, width, 128), F32),
             pltpu.VMEM((units, 1), F32),
@@ -999,7 +1045,7 @@
             regular((3 + n_tensor // 2 + n_dp,)),
             dma((5, 2)),
             dma((5, 2, n_tensor)),
-            dma((10,)),
+            dma((n_slots + 3,)),
             dma((seqs,)),
             dma((seqs,)),
             dma((2, n_dp)),

time: 446 us -> 378 us (0.85)
  Pallas kernels: 424 us -> 356 us
    pallas_call x1, Pallas kernels: 424 us -> 356 us  [on_device(): pl.pallas_call(layer_body, out_shape=[shape(words.shape, BF), shape((grou...]
where the time goes in v4:
time: 378 us; the launch traced here: 373 us
  Pallas kernels  356 us (94%)
  local copies, waits for them, and re-layouts  8.73 us (2%)
  other arithmetic  7.35 us (2%)
    pallas_call x1, Pallas kernels, on_device(): pl.pallas_call(layer_body, out_shape=[shape(words.shape, BF), shape((grou...  356 us

profile of v4, /device:TPU:0, one launch (start us, length us, event | category | flops | bytes accessed | tf_op | source)
XLA Modules:
  0.0 373.1 jit_solution(17466454812670079011)
XLA Ops:
  0.6 0.7 convert_element_type.22
  1.3 0.7 pad.24
  2.0 0.7 pad.25
  2.7 0.7 pad.26
  3.3 0.7 pad.27
  4.0 0.7 pad.28
  4.6 0.7 pad.29
  5.3 0.6 stack.31.rows_ref
  5.9 356.2 %shard_map.222 = (bf16[3,96,4096]{2,1,0:T(8,128)(2,1)}, bf16[8,288,512]{2,1,0:T(8,128)(2,1)}, bf16[8,48,128]{2,1,0:T(8,128)(2,1)}, bf16[3,96,4096]{2,1,0:T(8,128...) custom-call(bf16[3,96,4096]{2,1,0:T(8,128)(2,1)} %x_ref.1, ...), custom_call_target="tpu_custom_call" | custom-call | tf_op jit(solution)/shard_map/pallas_call | solution.py:985
  362.1 1.4 slice_bitcast_fusion
  363.5 1.3 slice_reduce_fusion
  364.8 0.0 copy-start.2
  364.8 0.0 copy-start.1
  364.8 4.5 %convert_element_type.23 = f32[3,96,4096]{2,1,0:T(8,128)} convert(bf16[3,96,4096]{2,1,0:T(8,128)(2,1)} %get-tuple-element.16) | non-fusion elementwise | flops 1179648 | bytes 7077888 | tf_op jit(solution)/shard_map/convert_element_type | solution.py:1063
  369.3 0.0 copy-start
  369.3 0.0 copy-done.2
  369.4 1.1 convert_element_type.24
  370.4 0.0 copy-done.1
  370.4 1.1 convert_element_type.25
  371.5 0.0 copy-done
  371.5 1.4 copy.26
  (2 shorter events, 0.0 us)
Async XLA Ops:
  364.8 4.5 %copy-start.2 = (bf16[384,768]{1,0:T(8,128)(2,1)S(1)}, bf16[384,768]{1,0:T(8,128)(2,1)}, u32[]{:S(2)}) copy-start(bf16[384,768]{1,0:T(8,128)(2,1)} %get-tuple-element.17) | copy-start | bytes 1769476
  364.8 5.6 %copy-start.1 = (bf16[384,768]{1,0:T(8,128)(2,1)S(1)}, bf16[384,768]{1,0:T(8,128)(2,1)}, u32[]{:S(2)}) copy-start(bf16[384,768]{1,0:T(8,128)(2,1)} %get-tuple-element.19) | copy-start | bytes 1769476
  369.3 2.2 copy-start

commit v5 on v4

--- a/solution.py
+++ b/solution.py
@@ -43,30 +43,30 @@
     def __init__(self, n_dp, n_tensor):
         self.n_dp, self.n_tensor = n_dp, n_tensor
         self.slices = n_tensor // 2
-        self.group = 2 * n_dp
+        self.low = self.slices // 2
         self.dp = lax.axis_index("dp")
         self.tensor = lax.axis_index("tensor")
-        self.z = self.tensor // 2
-        self.y = self.tensor % 2
-        self.g = self.dp * 2 + self.y
-        self.block = self.block_of(self.dp, self.y)
-
-    def block_of(self, dp, y):
-        return ((dp % (self.n_dp // 2)) * 2 + dp // (self.n_dp // 2)) * 2 + y
-
-    def dp_of(self, z):
-        return (z % 2) * (self.n_dp // 2) + z // 2
-
-    def z_of(self, j):
-        return ((self.dp % 2) * (self.n_dp // 2) + self.dp // 2) ^ j
+        self.x, self.core = self.dp // 2, self.dp % 2
+        self.z, self.y = self.tensor // 2, self.tensor % 2
+        self.z_high, self.z_low = self.z // self.low, self.z % self.low
+        self.g = (self.z_low * 2 + self.core) * 2 + self.y
+        self.block = self.block_of(self.g)
+
+    def block_of(self, g):
+        return (g // 2 % 2 * self.low + g // 4) * 2 + g % 2
+
+    def member(self, g, z_high):
+        return (self.x * 2 + g // 2 % 2, (z_high * self.low + g // 4) * 2 + g % 2)
+
+    def high_of(self, j):
+        return self.core ^ (j % 2)
 
     def dp_from(self, j):
-        v = self.z ^ j
-        return (v % (self.n_dp // 2)) * 2 + v // (self.n_dp // 2)
+        return self.x * 2 + (self.z_high ^ (j % 2))
 
     def peer(self, offset):
         g = self.g ^ offset
-        return (g // 2, self.z * 2 + g % 2), g
+        return self.member(g, self.z_high), g
 
 
 ANY = pl.BlockSpec(memory_space=pl.ANY)
@@ -78,8 +78,7 @@
     seqs, columns, length = words.shape
     width = w_in.shape[1]
     n_dp, n_tensor = lax.axis_size("dp"), lax.axis_size("tensor")
-    assert n_tensor == 2 * n_dp
-    group = 2 * n_dp
+    group = n_tensor
     half = length // (2 * group)
     mix_scale = 1.0 / math.sqrt(length * width)
     table, edge_table = token_tables(length, group)
@@ -94,19 +93,15 @@
         return lax.dot_general(a, b, (((da,), (db,)), ((), ())), preferred_element_type=F32)
 
     wide = 512
-    pad = lambda v: jnp.pad(v, (0, wide - v.shape[0]))
-    rows_in = jnp.stack(
-        [pad(v) for v in (b_in, b_out, gain_one, shift_one, gain_two, shift_two, valid.astype(F32))]
-        + [jnp.zeros((wide,), F32)]
-    )
 
     n_slots = 4
 
     def layer_body(
-        x_ref, c_ref, win_ref, wout_ref, cos_ref, sin_ref, table_ref, edge_ref, rows_ref,
+        x_ref, c_ref, win_ref, wout_ref, cos_ref, sin_ref, table_ref, edge_ref,
+        b_in_ref, b_out_ref, gain_one_ref, shift_one_ref, gain_two_ref, shift_two_ref, valid_ref,
         act_o, gu_o, ge_o, gf_o, gw_o, gin_o, gout_o, vec_o,
         win, wout, cos, sin, xb, ub, eb, cb, ab, a_all, m_all, nl, gl, f, tile, edge_v, slots,
-        perm, e_send, bacc, vacc, b_in_v, vec, vrows, drows, grows, drows2, spare,
+        perm, e_send, rows_ref, bacc, vacc, b_in_v, vec, vrows, drows, grows, drows2, spare,
         load, slice_send, slice_recv, tok_send, tok_recv, vec_send, vec_recv, gather_send, gather_recv,
         cot_send, cot_own, cot_recv, act_send, act_own, act_recv, col_send, col_recv,
         ready, rs_send, rs_recv, table_sem, home_send, home_recv, more_send, more_recv, more_free,
@@ -138,29 +133,29 @@
         rows_of = lambda b: pl.ds(pl.multiple_of(b * columns, 16), columns)
 
         def cot_start(j):
-            z = at.z_of(j)
+            high = at.high_of(j)
             for offset in range(group):
                 g = at.g ^ offset
                 for p in range(2):
                     src = c_ref.at[j, :, lanes(g)[p]]
                     dst = cb.at[pl.ds(pl.multiple_of(j * width + at.tensor * columns, 16), columns), parts[p]]
-                    device = (g // 2, z * 2 + g % 2)
+                    device = at.member(g, high)
                     if offset:
                         pltpu.make_async_remote_copy(src, dst, cot_send.at[j], cot_recv.at[j], device, MESH).start()
                     else:
-                        @pl.when(z == at.z)
+                        @pl.when(high == at.z_high)
                         def _():
                             pltpu.make_async_copy(src, dst, cot_recv.at[j]).start()
 
-                        @pl.when(z != at.z)
+                        @pl.when(high != at.z_high)
                         def _():
                             pltpu.make_async_remote_copy(src, dst, cot_own.at[j], cot_recv.at[j], device, MESH).start()
 
         def cot_finish(j):
-            z = at.z_of(j)
+            high = at.high_of(j)
             wait(c_ref.at[j, :, pl.ds(0, length - 2 * half)], cot_send.at[j])
 
-            @pl.when(z != at.z)
+            @pl.when(high != at.z_high)
             def _():
                 wait(c_ref.at[j, :, pl.ds(0, 2 * half)], cot_own.at[j])
 
@@ -195,10 +190,10 @@
         def col_moves(j):
             for offset in range(group):
                 device, g_ = at.peer(offset)
-                rows = rows_of(at.block_of(g_ // 2, g_ % 2))
+                rows = rows_of(at.block_of(g_))
                 for i, (src, dst) in enumerate((
                     (ub.at[j, rows], gu_o.at[at.g, pl.ds(j * columns, columns)]),
-                    (eb.at[j, pl.ds(pl.multiple_of(at.block_of(g_ // 2, g_ % 2) * er, 16), er)], ge_o.at[at.g, pl.ds(j * er, er)]),
+                    (eb.at[j, pl.ds(pl.multiple_of(at.block_of(g_) * er, 16), er)], ge_o.at[at.g, pl.ds(j * er, er)]),
                     (xb.at[j, rows, parts[0]], gf_o.at[j, :, lanes(at.g)[0]]),
                     (xb.at[j, rows, parts[1]], gf_o.at[j, :, lanes(at.g)[1]]),
                 )):
@@ -224,9 +219,9 @@
         n_pieces = length // tokens
 
         def slice_at(j):
-            z = at.z_of(j)
-            dp = at.dp_of(at.z)
-            return (dp, z * 2 + at.y), jnp.logical_and(dp == at.dp, z == at.z)
+            high = at.high_of(j)
+            dp = at.x * 2 + at.z_high
+            return (dp, (high * at.low + at.z_low) * 2 + at.y), jnp.logical_and(dp == at.dp, high == at.z_high)
 
         def slice_start(j):
             device, here = slice_at(j)
@@ -351,11 +346,12 @@
         core_peer, x_peer, y_peer = flip(1), flip(2), (at.dp, at.tensor ^ 1)
         z_peer = lambda offset: (at.dp, (at.z ^ offset) * 2 + at.y)
         w_refs, w_bufs = (win_ref, wout_ref), (win, wout)
-        n_far = slices - 1
-
-        def piece_rows(o, y, n_quarters, xx):
-            start = ((at.z ^ o) * 2 + y) * bt + core * hb + xx * qb
-            return pl.ds(pl.multiple_of(start, 16), n_quarters * qb)
+
+        far = [(o, p) for o in range(slices) for p in range(2) if o or p]
+
+        def piece(z, p, cc, xx):
+            start = (z * 2 + (at.y ^ p)) * bt + cc * hb + xx * qb
+            return pl.ds(pl.multiple_of(start, 16), qb)
 
         def pass_on(level, arr, rows, key, device):
             ref = w_bufs[arr].at[rows]
@@ -365,70 +361,84 @@
         def arrive(level, arr, rows, key):
             wait(w_bufs[arr].at[rows], gather_recv.at[level, arr, key])
 
-        def gather_one():
+        ways = [(1, at.z < slices - 1), (-1, at.z > 0)]
+
+        def neighbour(way):
+            return (at.dp, (at.z + way) * 2 + at.y)
+
+        def gather_start(arr):
             mine = pl.ds(pl.multiple_of(core * hb + x * qb, 16), qb)
-            for arr in range(2):
-                for o in range(1, slices):
+            for way, there in ways:
+                @pl.when(there)
+                def _():
                     pltpu.make_async_remote_copy(
-                        w_refs[arr].at[mine], w_bufs[arr].at[piece_rows(0, at.y, 1, x)],
-                        gather_send.at[0, arr], gather_recv.at[0, arr, o - 1], z_peer(o), MESH).start()
-
-        def gather_start():
-            half_rows = pl.ds(pl.multiple_of(core * hb, 16), hb)
-            for arr in range(2):
-                pltpu.make_async_remote_copy(
-                    w_refs[arr].at[half_rows], w_bufs[arr].at[piece_rows(0, at.y, 2, 0)],
-                    gather_send.at[2, arr], gather_recv.at[2, arr, 0], y_peer, MESH).start()
-                pltpu.make_async_copy(
-                    w_refs[arr], w_bufs[arr].at[pl.ds(pl.multiple_of(at.tensor * bt, 16), bt)], load.at[arr]).start()
-
-        def gather_two():
-            for arr in range(2):
-                for o in range(1, slices):
-                    rows = piece_rows(o, at.y, 1, x)
-                    arrive(0, arr, rows, o - 1)
-                    pass_on(1, arr, rows, o - 1, x_peer)
-                    pass_on(2, arr, rows, 2 * o - 1, y_peer)
-                    pass_on(3, arr, rows, 2 * o - 2, core_peer)
-
-        def gather_three():
-            for arr in range(2):
-                for o in range(1, slices):
-                    rows = piece_rows(o, at.y, 1, 1 - x)
-                    arrive(1, arr, rows, o - 1)
-                    pass_on(2, arr, rows, 2 * o, y_peer)
-                    pass_on(3, arr, rows, 2 * o - 1, core_peer)
+                        w_refs[arr].at[mine], w_bufs[arr].at[piece(at.z, 0, core, x)],
+                        gather_send.at[0, arr], gather_recv.at[0, arr, at.z], neighbour(way), MESH).start()
+            pltpu.make_async_remote_copy(
+                w_refs[arr].at[mine], w_bufs[arr].at[piece(at.z, 0, core, x)],
+                gather_send.at[1, arr], gather_recv.at[1, arr, at.z], y_peer, MESH).start()
+            pltpu.make_async_copy(
+                w_refs[arr], w_bufs[arr].at[pl.ds(pl.multiple_of(at.tensor * bt, 16), bt)], load.at[arr]).start()
+
+        def gather_two(arr):
+            for step in range(1, slices):
+                for way, there in ways:
+                    z = at.z - way * step
+
+                    @pl.when((z >= 0) & (z < slices))
+                    def _():
+                        rows = piece(z, 0, core, x)
+                        arrive(0, arr, rows, z)
+
+                        @pl.when(there)
+                        def _():
+                            pass_on(0, arr, rows, z, neighbour(way))
+
+                        pass_on(1, arr, rows, z, y_peer)
+                        pass_on(2, arr, rows, 2 * z, x_peer)
+                        pass_on(3, arr, rows, 4 * z, core_peer)
+
+        def gather_three(arr):
+            for o in range(slices):
+                z = at.z ^ o
+                rows = piece(z, 1, core, x)
+                arrive(1, arr, rows, z)
+                pass_on(2, arr, rows, 2 * z + 1, x_peer)
+                pass_on(3, arr, rows, 4 * z + 2, core_peer)
 
         def gather_four(arr):
-            other = 1 - at.y
-            keys = [(0, 2, 0, 0)] + [(o, 1, q, 2 * o - 1 + q) for o in range(1, slices) for q in range(2)]
-            for o, n, q, key in keys:
-                xx = 0 if n == 2 else (1 - x if q else x)
-                rows = piece_rows(o, other, n, xx)
-                arrive(2, arr, rows, key)
-                pass_on(3, arr, rows, 2 * n_far + key, core_peer)
+            for o, p in far:
+                z = at.z ^ o
+                rows = piece(z, p, core, 1 - x)
+                arrive(2, arr, rows, 2 * z + p)
+                pass_on(3, arr, rows, 2 * (2 * z + p) + 1, core_peer)
 
         def gather_last(arr):
-            def theirs(o, y, n, xx):
-                start = ((at.z ^ o) * 2 + y) * bt + (1 - core) * hb + xx * qb
-                return pl.ds(pl.multiple_of(start, 16), n * qb)
             pltpu.make_async_copy(
                 w_refs[arr], w_bufs[arr].at[pl.ds(pl.multiple_of(at.tensor * bt, 16), bt)], load.at[arr]).wait()
-            for o in range(1, slices):
+            for o, p in far:
+                z = at.z ^ o
                 for q in range(2):
-                    arrive(3, arr, theirs(o, at.y, 1, 1 - x if q else x), 2 * o - 2 + q)
-            arrive(3, arr, theirs(0, 1 - at.y, 2, 0), 2 * n_far)
-            for o in range(1, slices):
-                for q in range(2):
-                    arrive(3, arr, theirs(o, 1 - at.y, 1, 1 - x if q else x), 2 * n_far + 2 * o - 1 + q)
+                    arrive(3, arr, piece(z, p, 1 - core, 1 - x if q else x), 2 * (2 * z + p) + q)
 
         def gather_sent():
             for arr in range(2):
                 g = w_bufs[arr]
-                for level, quarters in enumerate((n_far, n_far, 2 + 2 * n_far, 2 * n_far + 2 + 2 * n_far)):
+                for step in range(slices):
+                    for way, there in ways:
+                        z = at.z - way * step
+
+                        @pl.when((z >= 0) & (z < slices) & there)
+                        def _():
+                            wait(g.at[pl.ds(0, qb)], gather_send.at[0, arr])
+                for level, quarters in ((1, slices), (2, len(far)), (3, 2 * len(far))):
                     wait(g.at[pl.ds(0, quarters * qb)], gather_send.at[level, arr])
 
         def vectors_start():
+            rows_ref[...] = jnp.zeros_like(rows_ref)
+            for i, ref in enumerate(
+                (b_in_ref, b_out_ref, gain_one_ref, shift_one_ref, gain_two_ref, shift_two_ref, valid_ref)):
+                rows_ref[i : i + 1, 0 : ref.shape[1]] = ref[...].astype(F32)
             pltpu.make_async_copy(rows_ref, vrows.at[pl.ds(pl.multiple_of(at.tensor * 8, 8), 8)], vec_recv.at[0]).start()
             pltpu.make_async_copy(rows_ref, drows.at[pl.ds(pl.multiple_of(at.dp * 8, 8), 8)], vec_recv.at[1]).start()
             for offset in range(1, n_tensor):
@@ -449,6 +459,18 @@
             for t in range(n_tensor):
                 b_in_v[t * bt : (t + 1) * bt, :] = turned[0:bt, 8 * t : 8 * t + 1]
                 vec[t * columns : (t + 1) * columns, :] = turned[0:columns, 8 * t + 1 : 8 * t + 6]
+
+        gather_start(0)
+        gather_start(1)
+        slice_start(0)
+        tables = [
+            pltpu.make_async_copy(src, dst, load.at[2 + i])
+            for i, (src, dst) in enumerate(((edge_ref, edge_v), (cos_ref, cos), (sin_ref, sin)))
+        ]
+        for move in tables:
+            move.start()
+        vectors_start()
+        front_prefetch()
 
         place0 = lax.broadcasted_iota(jnp.int32, (tokens, half), 0)
         k1 = lax.broadcasted_iota(jnp.int32, (tokens, half), 1)
@@ -639,7 +661,6 @@
         at4 = at3 + slices * qb
         at5 = at4 + (slices - 1) * qb
         land1 = lambda arr, k: land(pl.ds(pl.multiple_of(k * hb, 16), hb), arr)
-        land2 = lambda arr, k, n: land(pl.ds(at2 + k * n, n), arr)
         land3 = lambda arr, k: land(pl.ds(at3 + k * qb, qb), arr)
         land4 = lambda arr, k: land(pl.ds(at4 + k * qb, qb), arr)
         land5 = lambda arr: land(pl.ds(at5, qb), arr)
@@ -686,22 +707,35 @@
                 return c
             lax.fori_loop(0, n // 16, go, 0, unroll=2)
 
+        def y_first(arr, z):
+            return arr == 1 and z >= slices // 2
+
+        def land2_x(arr, z, own_y):
+            return land(pl.ds(at2 + z * hb + (qb if own_y else 0), qb), arr)
+
+        def land2_y(arr, z):
+            return land(pl.ds(at2 + z * hb, hb), arr)
+
         def after1(arr):
-            def go(k, c):
+            for k in range(n_tensor):
+                z, own_y = k % slices, k >= slices
                 add(arr, rows_half(k, core), land1(arr, k), 0, k)
-
-                @pl.when(k < slices)
-                def _():
-                    send(grads[arr].at[rows_half(k, core)], land2(arr, k, hb), 1, arr, k, y_peer)
-                return c
-            lax.fori_loop(0, n_tensor, go, 0)
+                if not y_first(arr, z):
+                    send(grads[arr].at[rows_quarter(k, 1 - x)], land2_x(arr, z, own_y), 1, arr, k, x_peer)
+                elif not own_y:
+                    send(grads[arr].at[rows_half(k, core)], land2_y(arr, z), 1, arr, k, y_peer)
 
         def after2(arr):
-            def go(k, c):
-                add(arr, rows_half(slices + k, core), land2(arr, k, hb), 1, k)
-                send(grads[arr].at[rows_quarter(slices + k, 1 - x)], land3(arr, k), 2, arr, k, x_peer)
-                return c
-            lax.fori_loop(0, slices, go, 0)
+            for z in range(slices):
+                if y_first(arr, z):
+                    add(arr, rows_half(slices + z, core), land2_y(arr, z), 1, z)
+                    send(grads[arr].at[rows_quarter(slices + z, 1 - x)], land3(arr, z), 2, arr, z, x_peer)
+                else:
+                    add(arr, rows_quarter(z, x), land2_x(arr, z, False), 1, z)
+                    send(grads[arr].at[rows_quarter(z, x)], land3(arr, z), 2, arr, z, y_peer)
+            for z in range(slices):
+                if not y_first(arr, z):
+                    add(arr, rows_quarter(slices + z, x), land2_x(arr, z, True), 1, slices + z)
 
         def after3(arr):
             for offset in range(slices):
@@ -883,35 +917,30 @@
                 total = total + drows2[(offset - 1) * 8 : offset * 8, :]
             vec_o[...] = total
 
-        tables = [
-            pltpu.make_async_copy(src, dst, load.at[2 + i])
-            for i, (src, dst) in enumerate(((edge_ref, edge_v), (cos_ref, cos), (sin_ref, sin)))
-        ]
-        gather_one()
-        gather_start()
-        vectors_start()
+        gather_two(0)
+        slice_start(1)
+        gather_two(1)
+        gather_three(0)
+        gather_three(1)
         for move in tables:
-            move.start()
-        front_prefetch()
-        gather_two()
-        slice_start(0)
-        gather_three()
-        tables[1].wait()
-        tables[2].wait()
+            move.wait()
         vectors_arrived()
-        tables[0].wait()
         wait(a_all.at[pl.ds(0, width), two], slice_recv.at[0])
+        for j in range(2, seqs):
+            slice_start(j)
+        cot_start(0)
         front_pass([0], 1)
         front_prefetch()
-        slice_start(1)
-        for arr in range(2):
-            gather_four(arr)
-        for j in range(2, seqs):
-            slice_start(j)
+        gather_four(0)
+        for i in range(1, seqs):
+            wait(a_all.at[pl.ds(i * width, width), two], slice_recv.at[i])
+        front_pass(list(range(1, seqs)), 1)
+        back_prefetch()
+        gather_four(1)
         inverse = forward_mix(0)
-        cot_start(0)
         for arr in range(2):
             gather_last(arr)
+        cot_start(1)
         last = seqs - 1
         for j in range(seqs):
             if j:
@@ -919,19 +948,16 @@
             if j == last:
                 for i in range(seqs):
                     tokens_sent(i)
-                back_prefetch()
             forward_mlp(j)
-            if j == 0:
-                wait(a_all.at[pl.ds(width, width), two], slice_recv.at[1])
-                front_pass([1], 1)
-                front_prefetch()
-            if j + 1 < seqs:
+            if 0 < j and j + 1 < seqs:
                 cot_start(j + 1)
             if j == last:
                 words_back([0], f3)
                 back_prefetch()
             second_norm(j)
             backward_inner(j)
+            if j + 2 < seqs:
+                later_tokens(j + 2)
             if j == last:
                 gather_sent()
                 weight_grads(0, a_all, gl)
@@ -940,21 +966,17 @@
                 level1(0)
             backward_outer(j)
             first_back(j, inverse)
-            if j + 2 < seqs:
-                i = j + 2
-                wait(a_all.at[pl.ds(i * width, width), two], slice_recv.at[i])
-                front_pass([i], 1)
-        ready_wait(2)
+        ready_wait(1)
         after1(0)
         weight_grads(1, m_all, nl)
         level1(1)
         vector_grads()
+        ready_wait(2)
         after1(1)
         for j in range(1, last):
             words_back([j], f2)
             back_prefetch()
         words_back([last], f2)
-        ready_wait(1)
         after2(0)
         for i in range(3, 3 + slices - 1 + max(0, n_dp.bit_length() - 3)):
             ready_wait(i)
@@ -994,7 +1016,7 @@
             shape(w_in.shape, BF),
             shape((8, wide), F32),
         ],
-        in_specs=[ANY] * 9,
+        in_specs=[ANY] * 8 + [whole_vmem] * 7,
         out_specs=[ANY] * 7 + [whole_vmem],
         scratch_shapes=[
             pltpu.VMEM((units, width), BF),
@@ -1016,6 +1038,7 @@
             pltpu.VMEM((n_slots * depth, tokens), BF),
             pltpu.VMEM((tokens, 4 * half), BF),
             pltpu.VMEM((seqs * 2 * group, 128), BF),
+            pltpu.VMEM((8, wide), F32),
             pltpu.VMEM((units, 128), F32),
             pltpu.VMEM((5, width, 128), F32),
             pltpu.VMEM((units, 1), F32),
@@ -1058,7 +1081,8 @@
             collective_id=1, has_side_effects=True, vmem_limit_bytes=64 * 1024 * 1024
         ),
     )(
-        words, cotangent, w_in, w_out, jnp.asarray(hid_cos), jnp.asarray(hid_sin), table, edge_table, rows_in
+        words, cotangent, w_in, w_out, jnp.asarray(hid_cos), jnp.asarray(hid_sin), table, edge_table,
+        *[v[None] for v in (b_in, b_out, gain_one, shift_one, gain_two, shift_two, valid)],
     )
     grad_words = gw.astype(F32)
 

time: 378 us -> 341 us (0.902)
  Pallas kernels: 356 us -> 323 us
    pallas_call x1, Pallas kernels: 356 us -> 323 us  [on_device(): pl.pallas_call(layer_body, out_shape=[shape(words.shape, BF), shape((grou...]
    pad x7 -> x0, local copies, waits for them, and re-layouts: 3.98 us -> none  [on_device(): pad = lambda v: jnp.pad(v, (0, wide - v.shape[0]))]
where the time goes in v5:
time: 341 us; the launch traced here: 336 us
  Pallas kernels  323 us (95%)
  other arithmetic  6.69 us (2%)
  local copies, waits for them, and re-layouts  5.36 us (2%)
    pallas_call x1, Pallas kernels, on_device(): pl.pallas_call(layer_body, out_shape=[shape(words.shape, BF), shape((grou...  323 us

profile of v5, /device:TPU:0, one launch (start us, length us, event | category | flops | bytes accessed | tf_op | source)
XLA Modules:
  0.0 336.1 jit_solution(16456070292913567727)
XLA Ops:
  0.6 1.2 broadcast_in_dim.21.b_in_ref
  1.9 323.0 %shard_map.222 = (bf16[3,96,4096]{2,1,0:T(8,128)(2,1)}, bf16[8,288,512]{2,1,0:T(8,128)(2,1)}, bf16[8,48,128]{2,1,0:T(8,128)(2,1)}, bf16[3,96,4096]{2,1,0:T(8,128...) custom-call(bf16[3,96,4096]{2,1,0:T(8,128)(2,1)} %x_ref.1, ...), custom_call_target="tpu_custom_call" | custom-call | tf_op jit(solution)/shard_map/pallas_call | solution.py:1007
  324.9 1.4 slice_bitcast_fusion
  326.3 1.3 slice_reduce_fusion
  327.6 0.0 copy-start.2
  327.6 0.0 copy-start.1
  327.6 4.5 %convert_element_type.9 = f32[3,96,4096]{2,1,0:T(8,128)} convert(bf16[3,96,4096]{2,1,0:T(8,128)(2,1)} %get-tuple-element.16) | non-fusion elementwise | flops 1179648 | bytes 7077888 | tf_op jit(solution)/shard_map/convert_element_type | solution.py:1087
  332.1 0.0 copy-start
  332.1 0.0 copy-done.2
  332.1 1.1 convert_element_type.10
  333.2 0.0 copy-done.1
  333.2 1.1 convert_element_type.11
  334.3 0.0 copy-done
  334.3 1.4 copy.26
Async XLA Ops:
  327.6 4.5 %copy-start.2 = (bf16[384,768]{1,0:T(8,128)(2,1)S(1)}, bf16[384,768]{1,0:T(8,128)(2,1)}, u32[]{:S(2)}) copy-start(bf16[384,768]{1,0:T(8,128)(2,1)} %get-tuple-element.17) | copy-start | bytes 1769476
  327.6 5.6 %copy-start.1 = (bf16[384,768]{1,0:T(8,128)(2,1)S(1)}, bf16[384,768]{1,0:T(8,128)(2,1)}, u32[]{:S(2)}) copy-start(bf16[384,768]{1,0:T(8,128)(2,1)} %get-tuple-element.19) | copy-start | bytes 1769476
  332.1 2.2 copy-start

commit v6 on v5

--- a/solution.py
+++ b/solution.py
@@ -380,9 +380,9 @@
             pltpu.make_async_copy(
                 w_refs[arr], w_bufs[arr].at[pl.ds(pl.multiple_of(at.tensor * bt, 16), bt)], load.at[arr]).start()
 
-        def gather_two(arr):
+        def gather_two():
             for step in range(1, slices):
-                for way, there in ways:
+                for arr, (way, there) in [(arr, w) for arr in range(2) for w in ways]:
                     z = at.z - way * step
 
                     @pl.when((z >= 0) & (z < slices))
@@ -737,17 +737,33 @@
                 if not y_first(arr, z):
                     add(arr, rows_quarter(slices + z, x), land2_x(arr, z, True), 1, slices + z)
 
+        bits = [1 << b for b in range(slices.bit_length() - 1)]
+        first_slot = lambda bit: slices - slices // bit
+
         def after3(arr):
-            for offset in range(slices):
-                k = at.z ^ offset
-                add(arr, rows_quarter(slices + k, x), land3(arr, k), 2, k)
-                if offset:
-                    send(grads[arr].at[rows_quarter(slices + k, x)], land4(arr, offset - 1), 3, arr, offset - 1, z_peer(offset))
+            for z in range(slices):
+                add(arr, rows_quarter(slices + z, x), land3(arr, z), 2, z)
+            z_send(arr, 1)
+
+        def z_send(arr, bit):
+            for i in range(slices // (2 * bit)):
+                block_z = at.z ^ (bit + 2 * bit * i)
+                send(grads[arr].at[rows_quarter(slices + block_z, x)], land4(arr, first_slot(bit) + i), 3, arr,
+                     first_slot(bit) + i, z_peer(bit))
+
+        def z_add(arr, bit):
+            for i in range(slices // (2 * bit)):
+                add(arr, rows_quarter(slices + (at.z ^ (2 * bit * i)), x), land4(arr, first_slot(bit) + i), 3,
+                    first_slot(bit) + i)
+
+        def z_turn(arr):
+            for bit in bits[:-1]:
+                z_add(arr, bit)
+                z_send(arr, 2 * bit)
 
         def after4(arr):
             mine = rows_quarter(slices + at.z, x)
-            for offset in range(1, slices):
-                add(arr, mine, land4(arr, offset - 1), 3, offset - 1)
+            z_add(arr, bits[-1])
             for b in range(2, n_dp.bit_length() - 1):
                 k = b - 2
                 peer_ = flip(1 << b)
@@ -917,9 +933,8 @@
                 total = total + drows2[(offset - 1) * 8 : offset * 8, :]
             vec_o[...] = total
 
-        gather_two(0)
+        gather_two()
         slice_start(1)
-        gather_two(1)
         gather_three(0)
         gather_three(1)
         for move in tables:
@@ -958,31 +973,32 @@
             backward_inner(j)
             if j + 2 < seqs:
                 later_tokens(j + 2)
-            if j == last:
-                gather_sent()
-                weight_grads(0, a_all, gl)
-                ready_signal()
-                ready_wait(0)
-                level1(0)
             backward_outer(j)
             first_back(j, inverse)
+        gather_sent()
+        weight_grads(0, a_all, gl)
+        ready_signal()
+        ready_wait(0)
+        level1(0)
+        weight_grads(1, m_all, nl)
+        level1(1)
         ready_wait(1)
         after1(0)
-        weight_grads(1, m_all, nl)
-        level1(1)
         vector_grads()
         ready_wait(2)
         after1(1)
         for j in range(1, last):
             words_back([j], f2)
             back_prefetch()
+        after2(0)
         words_back([last], f2)
-        after2(0)
         for i in range(3, 3 + slices - 1 + max(0, n_dp.bit_length() - 3)):
             ready_wait(i)
         after3(0)
         after2(1)
+        z_turn(0)
         after3(1)
+        z_turn(1)
         vector_grads_two()
         after4(0)
         after4(1)

time: 341 us -> 330 us (0.968)
  Pallas kernels: 323 us -> 311 us
    pallas_call x1, Pallas kernels: 323 us -> 311 us  [on_device(): pl.pallas_call(layer_body, out_shape=[shape(words.shape, BF), shape((grou...]
where the time goes in v6:
time: 330 us; the launch traced here: 324 us
  Pallas kernels  311 us (94%)
  other arithmetic  6.69 us (2%)
  local copies, waits for them, and re-layouts  5.36 us (2%)
    pallas_call x1, Pallas kernels, on_device(): pl.pallas_call(layer_body, out_shape=[shape(words.shape, BF), shape((grou...  311 us

profile of v6, /device:TPU:0, one launch (start us, length us, event | category | flops | bytes accessed | tf_op | source)
XLA Modules:
  0.0 324.4 jit_solution(18224049797185875823)
XLA Ops:
  0.6 1.2 broadcast_in_dim.21.b_in_ref
  1.9 311.2 %shard_map.222 = (bf16[3,96,4096]{2,1,0:T(8,128)(2,1)}, bf16[8,288,512]{2,1,0:T(8,128)(2,1)}, bf16[8,48,128]{2,1,0:T(8,128)(2,1)}, bf16[3,96,4096]{2,1,0:T(8,128...) custom-call(bf16[3,96,4096]{2,1,0:T(8,128)(2,1)} %x_ref.1, ...), custom_call_target="tpu_custom_call" | custom-call | tf_op jit(solution)/shard_map/pallas_call | solution.py:1023
  313.1 1.4 slice_bitcast_fusion
  314.5 1.3 slice_reduce_fusion
  315.8 0.0 copy-start.2
  315.8 0.0 copy-start.1
  315.8 4.5 %convert_element_type.9 = f32[3,96,4096]{2,1,0:T(8,128)} convert(bf16[3,96,4096]{2,1,0:T(8,128)(2,1)} %get-tuple-element.16) | non-fusion elementwise | flops 1179648 | bytes 7077888 | tf_op jit(solution)/shard_map/convert_element_type | solution.py:1103
  320.3 0.0 copy-start
  320.3 0.0 copy-done.2
  320.3 1.1 convert_element_type.10
  321.4 0.0 copy-done.1
  321.4 1.1 convert_element_type.11
  322.5 0.0 copy-done
  322.5 1.4 copy.26
Async XLA Ops:
  315.8 4.5 %copy-start.2 = (bf16[384,768]{1,0:T(8,128)(2,1)S(1)}, bf16[384,768]{1,0:T(8,128)(2,1)}, u32[]{:S(2)}) copy-start(bf16[384,768]{1,0:T(8,128)(2,1)} %get-tuple-element.17) | copy-start | bytes 1769476
  315.8 5.6 %copy-start.1 = (bf16[384,768]{1,0:T(8,128)(2,1)S(1)}, bf16[384,768]{1,0:T(8,128)(2,1)}, u32[]{:S(2)}) copy-start(bf16[384,768]{1,0:T(8,128)(2,1)} %get-tuple-element.19) | copy-start | bytes 1769476
  320.3 2.2 copy-start

commit v7 on v6

--- a/solution.py
+++ b/solution.py
@@ -935,17 +935,17 @@
 
         gather_two()
         slice_start(1)
-        gather_three(0)
-        gather_three(1)
         for move in tables:
             move.wait()
-        vectors_arrived()
         wait(a_all.at[pl.ds(0, width), two], slice_recv.at[0])
         for j in range(2, seqs):
             slice_start(j)
         cot_start(0)
         front_pass([0], 1)
         front_prefetch()
+        gather_three(0)
+        gather_three(1)
+        vectors_arrived()
         gather_four(0)
         for i in range(1, seqs):
             wait(a_all.at[pl.ds(i * width, width), two], slice_recv.at[i])

time: 330 us -> 335 us (1.015)
  Pallas kernels: 311 us -> 317 us
    pallas_call x1, Pallas kernels: 311 us -> 317 us  [on_device(): pl.pallas_call(layer_body, out_shape=[shape(words.shape, BF), shape((grou...]
where the time goes in v7:
time: 335 us; the launch traced here: 330 us
  Pallas kernels  317 us (95%)
  other arithmetic  6.69 us (2%)
  local copies, waits for them, and re-layouts  5.36 us (2%)
    pallas_call x1, Pallas kernels, on_device(): pl.pallas_call(layer_body, out_shape=[shape(words.shape, BF), shape((grou...  317 us

profile of v7, /device:TPU:0, one launch (start us, length us, event | category | flops | bytes accessed | tf_op | source)
XLA Modules:
  0.0 330.4 jit_solution(4497349549730033288)
XLA Ops:
  0.6 1.2 broadcast_in_dim.21.b_in_ref
  1.9 317.3 %shard_map.222 = (bf16[3,96,4096]{2,1,0:T(8,128)(2,1)}, bf16[8,288,512]{2,1,0:T(8,128)(2,1)}, bf16[8,48,128]{2,1,0:T(8,128)(2,1)}, bf16[3,96,4096]{2,1,0:T(8,128...) custom-call(bf16[3,96,4096]{2,1,0:T(8,128)(2,1)} %x_ref.1, ...), custom_call_target="tpu_custom_call" | custom-call | tf_op jit(solution)/shard_map/pallas_call | solution.py:1023
  319.2 1.4 slice_bitcast_fusion
  320.6 1.3 slice_reduce_fusion
  321.9 0.0 copy-start.2
  321.9 0.0 copy-start.1
  321.9 4.5 %convert_element_type.9 = f32[3,96,4096]{2,1,0:T(8,128)} convert(bf16[3,96,4096]{2,1,0:T(8,128)(2,1)} %get-tuple-element.16) | non-fusion elementwise | flops 1179648 | bytes 7077888 | tf_op jit(solution)/shard_map/convert_element_type | solution.py:1103
  326.4 0.0 copy-start
  326.4 0.0 copy-done.2
  326.4 1.1 convert_element_type.10
  327.5 0.0 copy-done.1
  327.5 1.1 convert_element_type.11
  328.6 0.0 copy-done
  328.6 1.4 copy.26
Async XLA Ops:
  321.9 4.5 %copy-start.2 = (bf16[384,768]{1,0:T(8,128)(2,1)S(1)}, bf16[384,768]{1,0:T(8,128)(2,1)}, u32[]{:S(2)}) copy-start(bf16[384,768]{1,0:T(8,128)(2,1)} %get-tuple-element.17) | copy-start | bytes 1769476
  321.9 5.6 %copy-start.1 = (bf16[384,768]{1,0:T(8,128)(2,1)S(1)}, bf16[384,768]{1,0:T(8,128)(2,1)}, u32[]{:S(2)}) copy-start(bf16[384,768]{1,0:T(8,128)(2,1)} %get-tuple-element.19) | copy-start | bytes 1769476
  326.4 2.2 copy-start
